TPU v7x, 512 devices: a whole 4x4x16 slice. The times are simulated.
512 devices in a mesh: gx: 4 (over z_lo), gy: 16 (over x, z_hi), gz: 8 (over y, core).
Axes of the slice: x: 4, y: 4, z: 16 (z_hi: 4, z_lo: 4; z = z_hi * 4 + z_lo), core: 2. Of those that a mesh axis runs over, the one named last changes fastest.
Arguments:
- electric: float32 [3, 32, 256, 512], P(None, 'gz', 'gy', 'gx'), may hold values from -6 to 6
- magnetic: float32 [3, 32, 256, 512], P(None, 'gz', 'gy', 'gx'), may hold values from -6 to 6
- polar: float32 [3, 32, 256, 512], P(None, 'gz', 'gy', 'gx'), may hold values from -6 to 6
- current: float32 [3, 32, 256, 512], P(None, 'gz', 'gy', 'gx'), may hold values from -6 to 6
- material: int32 [32, 256, 512], P('gz', 'gy', 'gx'), may hold values from 0 to 2, as said below
- pml: int32 [32, 256, 512], P('gz', 'gy', 'gx'), may hold values from 0 to 3, as said below
Outputs:
- electric_out: float32 [3, 32, 256, 512], P(None, 'gz', 'gy', 'gx')
- magnetic_out: float32 [3, 32, 256, 512], P(None, 'gz', 'gy', 'gx')
- polar_out: float32 [3, 32, 256, 512], P(None, 'gz', 'gy', 'gx')
- current_out: float32 [3, 32, 256, 512], P(None, 'gz', 'gy', 'gx')
Inputs may be any that keep to these rules, and one draw needn't show every extreme that they name: `material`: 0 vacuum, 1 dielectric, 2 Lorentz metal; outside the slab, the middle half of the z cells, every cell is vacuum. `pml`: level rises toward the grid's outer faces and is 3 on its outermost cells along x, y and z.
All inputs are finite; a program needn't handle non-finite values.
Results may differ from a plain program's by a relative error of at most 0.00002.
Values sent between devices are 32-bit elements; how exact they have to be, the bound alone decides.
No kernel may reach another device: no remote copies, remote signals or barrier semaphores. Data moves between devices by JAX's collectives and lax.ppermute only.
A program may use at most 64 MiB of HBM per device.

v0:
```python
import jax
import jax.numpy as jnp
from jax import lax
from jax.sharding import PartitionSpec as P

STEPS = 2


time_step = 0.5
damping = 0.2
omega_sq = 1.0
strength = 3.0


def padded(array, sides, width):
    for axis, dim in sides:
        peers, length = (lax.axis_size(axis), array.shape[dim])
        up = [(i, (i + 1) % peers) for i in range(peers - 1)]
        down = [(j, i) for i, j in up]
        last = lax.slice_in_dim(array, length - width, length, axis=dim)
        first = lax.slice_in_dim(array, 0, width, axis=dim)
        before = lax.ppermute(last, axis, up)
        after = lax.ppermute(first, axis, down)
        array = jnp.concatenate([before, array, after], axis=dim)
    return array


def material_terms(code):
    metal = (code > 8.5).astype(jnp.float32)
    dielec = ((code > 4.5) & (code < 8.5)).astype(jnp.float32)
    inside = (code > 0.5).astype(jnp.float32)
    level = code - 1.0 - 4.0 * (2.0 * metal + dielec)
    sigma = jnp.where(
        level > 2.5, 1.0, jnp.where(level > 1.5, 0.4, jnp.where(level > 0.5, 0.1, 0.0))
    ).astype(jnp.float32)
    permit = 1.0 + 0.5 * metal + 1.25 * dielec
    return (sigma, permit, metal, inside)


def curl_forward(field):
    lead = field[:, :-1, :-1, :-1]
    d_z = field[:, 1:, :-1, :-1] - lead
    d_y = field[:, :-1, 1:, :-1] - lead
    d_x = field[:, :-1, :-1, 1:] - lead
    return jnp.stack([d_y[2] - d_z[1], d_z[0] - d_x[2], d_x[1] - d_y[0]])


def curl_backward(field):
    last = field[:, 1:, 1:, 1:]
    d_z = last - field[:, :-1, 1:, 1:]
    d_y = last - field[:, 1:, :-1, 1:]
    d_x = last - field[:, 1:, 1:, :-1]
    return jnp.stack([d_y[2] - d_z[1], d_z[0] - d_x[2], d_x[1] - d_y[0]])


def interior(field):
    return field[:, 1:-1, 1:-1, 1:-1]


def leapfrog(electric, magnetic, polar, current, code):
    sigma, permit, metal, inside = material_terms(code)
    loss_h = 0.5 * time_step * sigma[:, :-1, :-1, :-1]
    magnetic_new = (
        (1.0 - loss_h) * magnetic[:, :-1, :-1, :-1] - time_step * curl_forward(electric)
    ) / (1.0 + loss_h)
    magnetic_new = magnetic_new * inside[:, :-1, :-1, :-1]
    e_core = interior(electric)
    metal_core = interior(metal)
    current_new = (
        (1.0 - 0.5 * damping * time_step) * current
        + time_step * omega_sq * (strength * metal_core * e_core - polar)
    ) / (1.0 + 0.5 * damping * time_step)
    polar_new = polar + time_step * current_new
    loss_e = 0.5 * time_step * interior(sigma)
    permit_core = interior(permit)
    electric_new = (
        (permit_core - loss_e) * e_core
        + time_step * (curl_backward(magnetic_new) - metal_core * current_new)
    ) / (permit_core + loss_e)
    electric_new = electric_new * interior(inside)
    return (electric_new, magnetic_new, polar_new, current_new)


def extend(stacked, width):
    return padded(stacked, (("gx", 3), ("gy", 2), ("gz", 1)), width)


def on_device(electric, magnetic, polar, current, material, pml):
    code = (1 + 4 * material + pml).astype(jnp.float32)[None]
    field_e, field_h, field_p, field_j = (electric, magnetic, polar, current)
    for step in range(STEPS):
        widened = extend(jnp.concatenate([field_e, field_h, code], axis=0), 1)
        field_e, magnetic_new, field_p, field_j = leapfrog(
            widened[0:3], widened[3:6], field_p, field_j, widened[6:7]
        )
        field_h = magnetic_new[:, 1:, 1:, 1:]
    return (field_e, field_h, field_p, field_j)


def solution(mesh):
    return jax.shard_map(
        on_device,
        mesh=mesh,
        in_specs=(
            P(None, "gz", "gy", "gx"),
            P(None, "gz", "gy", "gx"),
            P(None, "gz", "gy", "gx"),
            P(None, "gz", "gy", "gx"),
            P("gz", "gy", "gx"),
            P("gz", "gy", "gx"),
        ),
        out_specs=(
            P(None, "gz", "gy", "gx"),
            P(None, "gz", "gy", "gx"),
            P(None, "gz", "gy", "gx"),
            P(None, "gz", "gy", "gx"),
        ),
        check_vma=False,
    )
```

profile of v0, /device:TPU:1, one launch (start us, length us, event | category | flops | bytes accessed | tf_op | source)
XLA Modules:
  0.0 92.8 jit_solution(822013533678011648)
XLA Ops:
  0.6 0.0 copy-start
  0.6 0.8 convert_bitcast_fusion
  1.5 0.1 copy-done
  1.6 0.9 pad_maximum_fusion.11
  2.5 0.0 copy-start.1
  2.5 0.1 fusion.55
  2.6 4.4 %collective-permute-start = (f32[7,4,16,1]{3,2,1,0:T(8,128)S(1)}, f32[7,4,16,1]{3,2,1,0:T(8,128)S(1)}, u32[]{:S(2)}, u32[]{:S(2)}) collective-permute-start(f32[7,4,16,1]{3,2,1,0:T(8,128)S(1)} %get-tuple-element.40), channel_id=1, source_target_pairs={{0,128},{128,256},{256,384},{1,129},{129,257},{257,385},{2,130},{1... | collective-permute-start | bytes 5384 | tf_op jit(solution)/shard_map/ppermute | solution.py:22
  7.0 1.3 %collective-permute-start.1 = (f32[7,4,16,1]{3,2,1,0:T(8,128)S(1)}, f32[7,4,16,1]{3,2,1,0:T(8,128)S(1)}, u32[]{:S(2)}, u32[]{:S(2)}) collective-permute-start(f32[7,4,16,1]{3,2,1,0:T(8,128)S(1)} %get-tuple-element.41), channel_id=1, source_target_pairs={{128,0},{256,128},{384,256},{129,1},{257,129},{385,257},{130,2},{2... | collective-permute-start | bytes 5384 | tf_op jit(solution)/shard_map/ppermute | solution.py:23
  8.3 1.6 %collective-permute-done = f32[7,4,16,1]{3,2,1,0:T(8,128)S(1)} collective-permute-done((f32[7,4,16,1]{3,2,1,0:T(8,128)S(1)}, f32[7,4,16,1]{3,2,1,0:T(8,128)S(1)}, u32[]{:S(2)}, u32[]{:S(2)}) %collective-permute-start) | collective-permute-done | bytes 1824 | tf_op jit(solution)/shard_map/ppermute | solution.py:22
  9.9 4.0 %collective-permute-done.1 = f32[7,4,16,1]{3,2,1,0:T(8,128)S(1)} collective-permute-done((f32[7,4,16,1]{3,2,1,0:T(8,128)S(1)}, f32[7,4,16,1]{3,2,1,0:T(8,128)S(1)}, u32[]{:S(2)}, u32[]{:S(2)}) %collective-permute-start.1) | collective-permute-done | bytes 1824 | tf_op jit(solution)/shard_map/ppermute | solution.py:23
  13.9 0.2 fusion.19
  14.2 10.3 %collective-permute-start.2 = (f32[7,4,1,130]{3,2,1,0:T(1,128)S(1)}, f32[7,4,1,130]{3,2,1,0:T(1,128)S(1)}, u32[]{:S(2)}, u32[]{:S(2)}) collective-permute-start(f32[7,4,1,130]{3,2,1,0:T(1,128)S(1)} %get-tuple-element.26), channel_id=1, source_target_pairs={{0,8},{8,16},{16,24},{24,32},{32,40},{40,48},{48,56},{56,64},{64,7... | collective-permute-start | bytes 43688 | tf_op jit(solution)/shard_map/ppermute | solution.py:22
  24.5 1.3 %collective-permute-start.3 = (f32[7,4,1,130]{3,2,1,0:T(1,128)S(1)}, f32[7,4,1,130]{3,2,1,0:T(1,128)S(1)}, u32[]{:S(2)}, u32[]{:S(2)}) collective-permute-start(f32[7,4,1,130]{3,2,1,0:T(1,128)S(1)} %get-tuple-element.27), channel_id=1, source_target_pairs={{8,0},{16,8},{24,16},{32,24},{40,32},{48,40},{56,48},{64,56},{72,6... | collective-permute-start | bytes 43688 | tf_op jit(solution)/shard_map/ppermute | solution.py:23
  25.8 0.0 collective-permute-done.2
  25.9 7.5 %collective-permute-done.3 = f32[7,4,1,130]{3,2,1,0:T(1,128)S(1)} collective-permute-done((f32[7,4,1,130]{3,2,1,0:T(1,128)S(1)}, f32[7,4,1,130]{3,2,1,0:T(1,128)S(1)}, u32[]{:S(2)}, u32[]{:S(2)}) %collective-permute-start.3) | collective-permute-done | bytes 14592 | tf_op jit(solution)/shard_map/ppermute | solution.py:23
  33.3 0.3 fusion.13
  33.7 6.1 %collective-permute-start.4 = (f32[7,1,18,130]{3,2,1,0:T(8,128)S(1)}, f32[7,1,18,130]{3,2,1,0:T(8,128)S(1)}, u32[]{:S(2)}, u32[]{:S(2)}) collective-permute-start(f32[7,1,18,130]{3,2,1,0:T(8,128)S(1)} %get-tuple-element.21), channel_id=1, source_target_pairs={{0,1},{1,2},{2,3},{3,4},{4,5},{5,6},{6,7},{8,9},{9,10},{10,11},{11... | collective-permute-start | bytes 196568 | tf_op jit(solution)/shard_map/ppermute | solution.py:22
  39.9 1.9 %collective-permute-start.5 = (f32[7,1,18,130]{3,2,1,0:T(8,128)S(1)}, f32[7,1,18,130]{3,2,1,0:T(8,128)S(1)}, u32[]{:S(2)}, u32[]{:S(2)}) collective-permute-start(f32[7,1,18,130]{3,2,1,0:T(8,128)S(1)} %get-tuple-element.20), channel_id=1, source_target_pairs={{1,0},{2,1},{3,2},{4,3},{5,4},{6,5},{7,6},{9,8},{10,9},{11,10},{12... | collective-permute-start | bytes 196568 | tf_op jit(solution)/shard_map/ppermute | solution.py:23
  41.8 0.3 pad_maximum_fusion.1
  42.1 0.1 collective-permute-done.4
  42.2 4.4 %collective-permute-done.5 = f32[7,1,18,130]{3,2,1,0:T(8,128)S(1)} collective-permute-done((f32[7,1,18,130]{3,2,1,0:T(8,128)S(1)}, f32[7,1,18,130]{3,2,1,0:T(8,128)S(1)}, u32[]{:S(2)}, u32[]{:S(2)}) %collective-permute-start.5) | collective-permute-done | bytes 65552 | tf_op jit(solution)/shard_map/ppermute | solution.py:23
  46.6 0.1 broadcast_compare_fusion.1
  46.7 0.1 select_select_fusion.1
  46.9 0.3 fusion.4
  47.2 0.3 fusion.27
  47.5 0.1 slice_subtract_fusion.9
  47.6 0.1 fusion.41
  47.7 0.1 slice_subtract_fusion.14
  47.8 0.1 select_bitcast_fusion.3
  47.9 0.0 copy-start.2
  48.0 0.0 copy-start.3
  48.0 0.8 copy-done.2
  48.8 0.0 copy-done.3
  48.9 0.1 fusion.45
  49.0 0.1 fusion.54
  49.1 3.6 %collective-permute-start.6 = (f32[7,4,16,1]{3,2,1,0:T(8,128)S(1)}, f32[7,4,16,1]{3,2,1,0:T(8,128)S(1)}, u32[]{:S(2)}, u32[]{:S(2)}) collective-permute-start(f32[7,4,16,1]{3,2,1,0:T(8,128)S(1)} %get-tuple-element.38), channel_id=1, source_target_pairs={{0,128},{128,256},{256,384},{1,129},{129,257},{257,385},{2,130},{1... | collective-permute-start | bytes 5384 | tf_op jit(solution)/shard_map/ppermute | solution.py:22
  52.7 1.3 %collective-permute-start.7 = (f32[7,4,16,1]{3,2,1,0:T(8,128)S(1)}, f32[7,4,16,1]{3,2,1,0:T(8,128)S(1)}, u32[]{:S(2)}, u32[]{:S(2)}) collective-permute-start(f32[7,4,16,1]{3,2,1,0:T(8,128)S(1)} %get-tuple-element.39), channel_id=1, source_target_pairs={{128,0},{256,128},{384,256},{129,1},{257,129},{385,257},{130,2},{2... | collective-permute-start | bytes 5384 | tf_op jit(solution)/shard_map/ppermute | solution.py:23
  54.0 1.6 %collective-permute-done.6 = f32[7,4,16,1]{3,2,1,0:T(8,128)S(1)} collective-permute-done((f32[7,4,16,1]{3,2,1,0:T(8,128)S(1)}, f32[7,4,16,1]{3,2,1,0:T(8,128)S(1)}, u32[]{:S(2)}, u32[]{:S(2)}) %collective-permute-start.6) | collective-permute-done | bytes 1824 | tf_op jit(solution)/shard_map/ppermute | solution.py:22
  55.7 3.8 %collective-permute-done.7 = f32[7,4,16,1]{3,2,1,0:T(8,128)S(1)} collective-permute-done((f32[7,4,16,1]{3,2,1,0:T(8,128)S(1)}, f32[7,4,16,1]{3,2,1,0:T(8,128)S(1)}, u32[]{:S(2)}, u32[]{:S(2)}) %collective-permute-start.7) | collective-permute-done | bytes 1824 | tf_op jit(solution)/shard_map/ppermute | solution.py:23
  59.5 0.2 fusion.21
  59.8 7.0 %collective-permute-start.8 = (f32[7,4,1,130]{3,2,1,0:T(1,128)S(1)}, f32[7,4,1,130]{3,2,1,0:T(1,128)S(1)}, u32[]{:S(2)}, u32[]{:S(2)}) collective-permute-start(f32[7,4,1,130]{3,2,1,0:T(1,128)S(1)} %get-tuple-element.24), channel_id=1, source_target_pairs={{0,8},{8,16},{16,24},{24,32},{32,40},{40,48},{48,56},{56,64},{64,7... | collective-permute-start | bytes 43688 | tf_op jit(solution)/shard_map/ppermute | solution.py:22
  66.8 1.3 %collective-permute-start.9 = (f32[7,4,1,130]{3,2,1,0:T(1,128)S(1)}, f32[7,4,1,130]{3,2,1,0:T(1,128)S(1)}, u32[]{:S(2)}, u32[]{:S(2)}) collective-permute-start(f32[7,4,1,130]{3,2,1,0:T(1,128)S(1)} %get-tuple-element.25), channel_id=1, source_target_pairs={{8,0},{16,8},{24,16},{32,24},{40,32},{48,40},{56,48},{64,56},{72,6... | collective-permute-start | bytes 43688 | tf_op jit(solution)/shard_map/ppermute | solution.py:23
  68.1 0.0 collective-permute-done.8
  68.2 7.5 %collective-permute-done.9 = f32[7,4,1,130]{3,2,1,0:T(1,128)S(1)} collective-permute-done((f32[7,4,1,130]{3,2,1,0:T(1,128)S(1)}, f32[7,4,1,130]{3,2,1,0:T(1,128)S(1)}, u32[]{:S(2)}, u32[]{:S(2)}) %collective-permute-start.9) | collective-permute-done | bytes 14592 | tf_op jit(solution)/shard_map/ppermute | solution.py:23
  75.7 0.3 fusion.17
  76.0 6.5 %collective-permute-start.10 = (f32[7,1,18,130]{3,2,1,0:T(8,128)S(1)}, f32[7,1,18,130]{3,2,1,0:T(8,128)S(1)}, u32[]{:S(2)}, u32[]{:S(2)}) collective-permute-start(f32[7,1,18,130]{3,2,1,0:T(8,128)S(1)} %get-tuple-element.19), channel_id=1, source_target_pairs={{0,1},{1,2},{2,3},{3,4},{4,5},{5,6},{6,7},{8,9},{9,10},{10,11},{11... | collective-permute-start | bytes 196568 | tf_op jit(solution)/shard_map/ppermute | solution.py:22
  82.6 1.9 %collective-permute-start.11 = (f32[7,1,18,130]{3,2,1,0:T(8,128)S(1)}, f32[7,1,18,130]{3,2,1,0:T(8,128)S(1)}, u32[]{:S(2)}, u32[]{:S(2)}) collective-permute-start(f32[7,1,18,130]{3,2,1,0:T(8,128)S(1)} %get-tuple-element.18), channel_id=1, source_target_pairs={{1,0},{2,1},{3,2},{4,3},{5,4},{6,5},{7,6},{9,8},{10,9},{11,10},{12... | collective-permute-start | bytes 196568 | tf_op jit(solution)/shard_map/ppermute | solution.py:23
  84.5 0.3 pad_maximum_fusion
  84.8 0.1 collective-permute-done.10
  84.9 4.4 %collective-permute-done.11 = f32[7,1,18,130]{3,2,1,0:T(8,128)S(1)} collective-permute-done((f32[7,1,18,130]{3,2,1,0:T(8,128)S(1)}, f32[7,1,18,130]{3,2,1,0:T(8,128)S(1)}, u32[]{:S(2)}, u32[]{:S(2)}) %collective-permute-start.11) | collective-permute-done | bytes 65552 | tf_op jit(solution)/shard_map/ppermute | solution.py:23
  89.3 0.1 compare_and_fusion
  89.4 0.1 select_select_fusion
  89.5 0.1 slice_bitcast_fusion.2
  89.6 0.3 fusion.9
  90.0 0.3 fusion.33
  90.3 0.1 slice_subtract_fusion.6
  90.4 0.1 fusion.38
  90.5 0.1 slice_subtract_fusion.11
  90.6 0.0 copy-start.4
  90.6 0.1 slice_subtract_fusion.10
  90.7 0.5 copy-done.4
  91.2 0.1 subtract_bitcast_fusion.2
  91.4 0.7 broadcast_multiply_fusion
  92.1 0.8 multiply_add_fusion
  (13 shorter events, 0.3 us)
Async XLA Ops:
  0.6 0.9 copy-start
  2.5 11.5 %copy-start.1 = (f32[3,4,16,128]{3,2,1,0:T(8,128)S(1)}, f32[3,4,16,128]{3,2,1,0:T(8,128)}, u32[]{:S(2)}) copy-start(f32[3,4,16,128]{3,2,1,0:T(8,128)} %param.7) | copy-start | bytes 294916
  2.6 7.3 %collective-permute-start = (f32[7,4,16,1]{3,2,1,0:T(8,128)S(1)}, f32[7,4,16,1]{3,2,1,0:T(8,128)S(1)}, u32[]{:S(2)}, u32[]{:S(2)}) collective-permute-start(f32[7,4,16,1]{3,2,1,0:T(8,128)S(1)} %get-tuple-element.40), channel_id=1, source_target_pairs={{0,128},{128,256},{256,384},{1,129},{129,257},{257,385},{2,130},{1... | collective-permute-start | bytes 5384 | tf_op jit(solution)/shard_map/ppermute | solution.py:22
  7.0 6.9 %collective-permute-start.1 = (f32[7,4,16,1]{3,2,1,0:T(8,128)S(1)}, f32[7,4,16,1]{3,2,1,0:T(8,128)S(1)}, u32[]{:S(2)}, u32[]{:S(2)}) collective-permute-start(f32[7,4,16,1]{3,2,1,0:T(8,128)S(1)} %get-tuple-element.41), channel_id=1, source_target_pairs={{128,0},{256,128},{384,256},{129,1},{257,129},{385,257},{130,2},{2... | collective-permute-start | bytes 5384 | tf_op jit(solution)/shard_map/ppermute | solution.py:23
  14.2 11.6 %collective-permute-start.2 = (f32[7,4,1,130]{3,2,1,0:T(1,128)S(1)}, f32[7,4,1,130]{3,2,1,0:T(1,128)S(1)}, u32[]{:S(2)}, u32[]{:S(2)}) collective-permute-start(f32[7,4,1,130]{3,2,1,0:T(1,128)S(1)} %get-tuple-element.26), channel_id=1, source_target_pairs={{0,8},{8,16},{16,24},{24,32},{32,40},{40,48},{48,56},{56,64},{64,7... | collective-permute-start | bytes 43688 | tf_op jit(solution)/shard_map/ppermute | solution.py:22
  24.5 8.8 %collective-permute-start.3 = (f32[7,4,1,130]{3,2,1,0:T(1,128)S(1)}, f32[7,4,1,130]{3,2,1,0:T(1,128)S(1)}, u32[]{:S(2)}, u32[]{:S(2)}) collective-permute-start(f32[7,4,1,130]{3,2,1,0:T(1,128)S(1)} %get-tuple-element.27), channel_id=1, source_target_pairs={{8,0},{16,8},{24,16},{32,24},{40,32},{48,40},{56,48},{64,56},{72,6... | collective-permute-start | bytes 43688 | tf_op jit(solution)/shard_map/ppermute | solution.py:23
  33.7 8.5 %collective-permute-start.4 = (f32[7,1,18,130]{3,2,1,0:T(8,128)S(1)}, f32[7,1,18,130]{3,2,1,0:T(8,128)S(1)}, u32[]{:S(2)}, u32[]{:S(2)}) collective-permute-start(f32[7,1,18,130]{3,2,1,0:T(8,128)S(1)} %get-tuple-element.21), channel_id=1, source_target_pairs={{0,1},{1,2},{2,3},{3,4},{4,5},{5,6},{6,7},{8,9},{9,10},{10,11},{11... | collective-permute-start | bytes 196568 | tf_op jit(solution)/shard_map/ppermute | solution.py:22
  39.9 6.7 %collective-permute-start.5 = (f32[7,1,18,130]{3,2,1,0:T(8,128)S(1)}, f32[7,1,18,130]{3,2,1,0:T(8,128)S(1)}, u32[]{:S(2)}, u32[]{:S(2)}) collective-permute-start(f32[7,1,18,130]{3,2,1,0:T(8,128)S(1)} %get-tuple-element.20), channel_id=1, source_target_pairs={{1,0},{2,1},{3,2},{4,3},{5,4},{6,5},{7,6},{9,8},{10,9},{11,10},{12... | collective-permute-start | bytes 196568 | tf_op jit(solution)/shard_map/ppermute | solution.py:23
  47.9 0.9 copy-start.2
  48.0 0.9 %copy-start.3 = (f32[3,4,16,128]{3,2,1,0:T(8,128)S(1)}, f32[3,4,16,128]{3,2,1,0:T(8,128)}, u32[]{:S(2)}) copy-start(f32[3,4,16,128]{3,2,1,0:T(8,128)} %param.9) | copy-start | bytes 294916
  49.1 6.6 %collective-permute-start.6 = (f32[7,4,16,1]{3,2,1,0:T(8,128)S(1)}, f32[7,4,16,1]{3,2,1,0:T(8,128)S(1)}, u32[]{:S(2)}, u32[]{:S(2)}) collective-permute-start(f32[7,4,16,1]{3,2,1,0:T(8,128)S(1)} %get-tuple-element.38), channel_id=1, source_target_pairs={{0,128},{128,256},{256,384},{1,129},{129,257},{257,385},{2,130},{1... | collective-permute-start | bytes 5384 | tf_op jit(solution)/shard_map/ppermute | solution.py:22
  52.7 6.8 %collective-permute-start.7 = (f32[7,4,16,1]{3,2,1,0:T(8,128)S(1)}, f32[7,4,16,1]{3,2,1,0:T(8,128)S(1)}, u32[]{:S(2)}, u32[]{:S(2)}) collective-permute-start(f32[7,4,16,1]{3,2,1,0:T(8,128)S(1)} %get-tuple-element.39), channel_id=1, source_target_pairs={{128,0},{256,128},{384,256},{129,1},{257,129},{385,257},{130,2},{2... | collective-permute-start | bytes 5384 | tf_op jit(solution)/shard_map/ppermute | solution.py:23
  59.8 8.3 %collective-permute-start.8 = (f32[7,4,1,130]{3,2,1,0:T(1,128)S(1)}, f32[7,4,1,130]{3,2,1,0:T(1,128)S(1)}, u32[]{:S(2)}, u32[]{:S(2)}) collective-permute-start(f32[7,4,1,130]{3,2,1,0:T(1,128)S(1)} %get-tuple-element.24), channel_id=1, source_target_pairs={{0,8},{8,16},{16,24},{24,32},{32,40},{40,48},{48,56},{56,64},{64,7... | collective-permute-start | bytes 43688 | tf_op jit(solution)/shard_map/ppermute | solution.py:22
  66.8 8.8 %collective-permute-start.9 = (f32[7,4,1,130]{3,2,1,0:T(1,128)S(1)}, f32[7,4,1,130]{3,2,1,0:T(1,128)S(1)}, u32[]{:S(2)}, u32[]{:S(2)}) collective-permute-start(f32[7,4,1,130]{3,2,1,0:T(1,128)S(1)} %get-tuple-element.25), channel_id=1, source_target_pairs={{8,0},{16,8},{24,16},{32,24},{40,32},{48,40},{56,48},{64,56},{72,6... | collective-permute-start | bytes 43688 | tf_op jit(solution)/shard_map/ppermute | solution.py:23
  76.0 8.9 %collective-permute-start.10 = (f32[7,1,18,130]{3,2,1,0:T(8,128)S(1)}, f32[7,1,18,130]{3,2,1,0:T(8,128)S(1)}, u32[]{:S(2)}, u32[]{:S(2)}) collective-permute-start(f32[7,1,18,130]{3,2,1,0:T(8,128)S(1)} %get-tuple-element.19), channel_id=1, source_target_pairs={{0,1},{1,2},{2,3},{3,4},{4,5},{5,6},{6,7},{8,9},{9,10},{10,11},{11... | collective-permute-start | bytes 196568 | tf_op jit(solution)/shard_map/ppermute | solution.py:22
  82.6 6.7 %collective-permute-start.11 = (f32[7,1,18,130]{3,2,1,0:T(8,128)S(1)}, f32[7,1,18,130]{3,2,1,0:T(8,128)S(1)}, u32[]{:S(2)}, u32[]{:S(2)}) collective-permute-start(f32[7,1,18,130]{3,2,1,0:T(8,128)S(1)} %get-tuple-element.18), channel_id=1, source_target_pairs={{1,0},{2,1},{3,2},{4,3},{5,4},{6,5},{7,6},{9,8},{10,9},{11,10},{12... | collective-permute-start | bytes 196568 | tf_op jit(solution)/shard_map/ppermute | solution.py:23
  90.6 0.6 copy-start.4
where the time goes:
time: 93.3 us; the launch traced here: 92.8 us
  starting transfers between devices  47 us (50%)
  waiting for transfers between devices  35.2 us (38%)
  other arithmetic  7.63 us (8%)
  local copies, waits for them, and re-layouts  2.01 us (2%)
  between operations  1.01 us (1%)
    ppermute x6, starting transfers between devices, padded(): before = lax.ppermute(last, axis, up)  38 us
    ppermute x6, waiting for transfers between devices, padded(): after = lax.ppermute(first, axis, down)  31.6 us
    ppermute x6, starting transfers between devices, padded(): after = lax.ppermute(first, axis, down)  9.01 us
    ppermute x6, waiting for transfers between devices, padded(): before = lax.ppermute(last, axis, up)  3.55 us
    concatenate x6, other arithmetic, padded(): array = jnp.concatenate([before, array, after], axis=dim)  1.87 us
  transfers between devices with their start and end apart: 12, of which 10 were waited for; matrix products, arithmetic and copies ran while one was open for 1% of the time, Pallas kernels for 0%

commit v1 on v0

v1 whole, which is shorter than its diff:
```python
import jax
import jax.numpy as jnp
from jax import lax
from jax.sharding import PartitionSpec as P

time_step = 0.5
damping = 0.2
omega_sq = 1.0
strength = 3.0

DIMS = (("gy", 2), ("gx", 3), ("gz", 1))


def widened(low, high, axis, dim):
    peers = lax.axis_size(axis)
    up = [(i, i + 1) for i in range(peers - 1)]
    down = [(i + 1, i) for i in range(peers - 1)]
    after = lax.ppermute(high, axis, down)
    before = lax.ppermute(low, axis, up)
    return before, after


def ends(array, dim, low, high):
    n = array.shape[dim]
    return (
        lax.slice_in_dim(array, n - low, n, axis=dim),
        lax.slice_in_dim(array, 0, high, axis=dim),
    )


def exchange(groups):
    arrays = [g[0] for g in groups]
    widths = [(g[1], g[2]) for g in groups]
    for axis, dim in DIMS:
        cuts = [ends(a, dim, lo, hi) for a, (lo, hi) in zip(arrays, widths)]
        lows = [c[0] for c in cuts]
        highs = [c[1] for c in cuts]
        flat_low = jnp.concatenate([c.reshape(-1) for c in lows])
        flat_high = jnp.concatenate([c.reshape(-1) for c in highs])
        sizes = flat_low.size, flat_high.size

        def lined(flat):
            return jnp.pad(flat, (0, -flat.size % 1024)).reshape(-1, 128)

        before, after = widened(lined(flat_low), lined(flat_high), axis, dim)
        before, after = before.reshape(-1), after.reshape(-1)
        out, at_b, at_a = [], 0, 0
        for a, lo, hi in zip(arrays, lows, highs):
            b = before[at_b : at_b + lo.size].reshape(lo.shape)
            c = after[at_a : at_a + hi.size].reshape(hi.shape)
            at_b, at_a = at_b + lo.size, at_a + hi.size
            out.append(jnp.concatenate([b, a, c], axis=dim))
        arrays = out
    return arrays


def cut(array, low, high):
    _, z, y, x = array.shape
    return array[:, low : z - high, low : y - high, low : x - high]


def material_terms(code):
    metal = (code > 8.5).astype(jnp.float32)
    dielec = ((code > 4.5) & (code < 8.5)).astype(jnp.float32)
    inside = (code > 0.5).astype(jnp.float32)
    level = code - 1.0 - 4.0 * (2.0 * metal + dielec)
    sigma = jnp.where(
        level > 2.5, 1.0, jnp.where(level > 1.5, 0.4, jnp.where(level > 0.5, 0.1, 0.0))
    ).astype(jnp.float32)
    permit = 1.0 + 0.5 * metal + 1.25 * dielec
    return sigma, permit, metal, inside


def curl(d_x, d_y, d_z):
    return jnp.stack([d_y[2] - d_z[1], d_z[0] - d_x[2], d_x[1] - d_y[0]])


def forward(field):
    lead = field[:, :-1, :-1, :-1]
    return curl(
        field[:, :-1, :-1, 1:] - lead,
        field[:, :-1, 1:, :-1] - lead,
        field[:, 1:, :-1, :-1] - lead,
    )


def backward(field):
    last = field[:, 1:, 1:, 1:]
    return curl(
        last - field[:, 1:, 1:, :-1],
        last - field[:, 1:, :-1, 1:],
        last - field[:, :-1, 1:, 1:],
    )


DECAY = 1.0 + 0.5 * damping * time_step


def magnetic_step(magnetic, electric, code):
    sigma, _, _, inside = material_terms(code)
    loss = 0.5 * time_step * sigma
    return inside * ((1.0 - loss) * magnetic - time_step * forward(electric)) / (1.0 + loss)


def electric_step(electric, magnetic, current, code):
    sigma, permit, metal, inside = material_terms(code)
    loss = 0.5 * time_step * sigma
    return (
        inside
        * ((permit - loss) * electric + time_step * (backward(magnetic) - metal * current))
        / (permit + loss)
    )


def on_device(electric, magnetic, polar, current, material, pml):
    code = (1 + 4 * material + pml).astype(jnp.float32)[None]
    keep = ((1.0 - 0.5 * damping * time_step) * current - time_step * omega_sq * polar) / DECAY
    gain = time_step * omega_sq * strength / DECAY

    e0, h0, c0, q0 = exchange([(electric, 2, 2), (magnetic, 2, 1), (code, 2, 1), (keep, 1, 1)])

    h1 = magnetic_step(h0, e0, c0)
    c1 = cut(c0, 1, 0)
    metal = (c1 > 8.5).astype(jnp.float32)
    e0_mid = cut(e0, 1, 1)
    j1 = q0 + gain * metal * e0_mid
    e1 = electric_step(e0_mid, h1, j1, c1)
    current1 = cut(j1, 1, 1)
    polar1 = polar + time_step * current1

    h2 = magnetic_step(cut(h1, 1, 1), e1, cut(c1, 0, 1))
    c2 = cut(c1, 1, 1)
    metal = (c2 > 8.5).astype(jnp.float32)
    e1_mid = cut(e1, 1, 1)
    current2 = (
        (1.0 - 0.5 * damping * time_step) * current1
        + time_step * omega_sq * (strength * metal * e1_mid - polar1)
    ) / DECAY
    polar2 = polar1 + time_step * current2
    e2 = electric_step(e1_mid, h2, current2, c2)
    return e2, cut(h2, 1, 0), polar2, current2


def solution(mesh):
    fields = P(None, "gz", "gy", "gx")
    cells = P("gz", "gy", "gx")
    return jax.shard_map(
        on_device,
        mesh=mesh,
        in_specs=(fields, fields, fields, fields, cells, cells),
        out_specs=(fields, fields, fields, fields),
        check_vma=False,
    )
```

time: 93.3 us -> 67.4 us (0.72)
  the two profiles are of different devices: /device:TPU:1 before, /device:TPU:10 now
where the time goes in v1:
time: 67.4 us; the launch traced here: 66.7 us
  starting transfers between devices  23.7 us (35%)
  waiting for transfers between devices  15.5 us (23%)
  local copies, waits for them, and re-layouts  15.2 us (23%)
  other arithmetic  10.9 us (16%)
  between operations  1.43 us (2%)
    ppermute x3, starting transfers between devices, widened(): after = lax.ppermute(high, axis, down)  15.9 us
    ppermute x3, waiting for transfers between devices, widened(): before = lax.ppermute(low, axis, up)  11.3 us
    ppermute x3, starting transfers between devices, widened(): before = lax.ppermute(low, axis, up)  7.83 us
    unnamed x48, local copies, waits for them, and re-layouts  5.5 us
    ppermute x3, waiting for transfers between devices, widened(): after = lax.ppermute(high, axis, down)  4.21 us
    reshape x9, local copies, waits for them, and re-layouts, exchange(): b = before[at_b:at_b + lo.size].reshape(lo.shape)  1.99 us
    reshape x10, local copies, waits for them, and re-layouts, exchange(): c = after[at_a:at_a + hi.size].reshape(hi.shape)  1.93 us
  transfers between devices with their start and end apart: 6, of which 3 were waited for; matrix products, arithmetic and copies ran while one was open for 6% of the time, Pallas kernels for 0%

profile of v1, /device:TPU:10, one launch (start us, length us, event | category | flops | bytes accessed | tf_op | source)
XLA Modules:
  0.0 66.7 jit_solution(2157256087435293338)
XLA Ops:
  0.6 1.0 %subtract_multiply_fusion = f32[3,4,16,128]{3,2,1,0:T(8,128)S(1)} fusion(f32[3,4,16,128]{3,2,1,0:T(8,128)} %param.8, f32[3,4,16,128]{3,2,1,0:T(8,128)} %param.9), kind=kLoop, calls=%fused_computation.86 | loop fusion | flops 98304 | bytes 294912 | tf_op jit(solution)/shard_map/div | solution.py:117
  1.7 0.7 %copy-done.22 = s32[4,16,128]{2,1,0:T(8,128)S(1)} copy-done((s32[4,16,128]{2,1,0:T(8,128)S(1)}, s32[4,16,128]{2,1,0:T(8,128)}, u32[]{:S(2)}) %copy-start.22) | copy-done | bytes 32792
  2.4 0.6 fusion.17
  3.0 0.3 copy-done
  3.4 12.7 %collective-permute-start.1 = (f32[56,128]{1,0:T(8,128)S(1)}, f32[56,128]{1,0:T(8,128)S(1)}, u32[]{:S(2)}, u32[]{:S(2)}) collective-permute-start(f32[56,128]{1,0:T(8,128)S(1)} %fusion.19), channel_id=1, source_target_pairs={{8,0},{16,8},{24,16},{32,24},{40,32},{48,40},{56,48},{64,56},{72,6... | collective-permute-start | bytes 86024 | tf_op jit(solution)/shard_map/ppermute | solution.py:18
  16.1 1.9 %collective-permute-start = (f32[72,128]{1,0:T(8,128)S(1)}, f32[72,128]{1,0:T(8,128)S(1)}, u32[]{:S(2)}, u32[]{:S(2)}) collective-permute-start(f32[72,128]{1,0:T(8,128)S(1)} %fusion.14), channel_id=1, source_target_pairs={{0,8},{8,16},{16,24},{24,32},{32,40},{40,48},{48,56},{56,64},{64,7... | collective-permute-start | bytes 110600 | tf_op jit(solution)/shard_map/ppermute | solution.py:19
  18.1 9.4 %collective-permute-done = f32[72,128]{1,0:T(8,128)S(1)} collective-permute-done((f32[72,128]{1,0:T(8,128)S(1)}, f32[72,128]{1,0:T(8,128)S(1)}, u32[]{:S(2)}, u32[]{:S(2)}) %collective-permute-start) | collective-permute-done | bytes 36896 | tf_op jit(solution)/shard_map/ppermute | solution.py:19
  28.0 0.2 slice_reduce_fusion.2
  28.7 0.1 reshape.511
  28.8 0.1 reshape.498
  29.0 0.1 reshape.501
  29.1 0.1 reshape.504
  29.4 3.5 %collective-permute-start.2 = (f32[16,128]{1,0:T(8,128)S(1)}, f32[16,128]{1,0:T(8,128)S(1)}, u32[]{:S(2)}, u32[]{:S(2)}) collective-permute-start(f32[16,128]{1,0:T(8,128)S(1)} %pad_bitcast_fusion.2), channel_id=1, source_target_pairs={{0,128},{128,256},{256,384},{1,129},{129,257},{257,385},{2,130},{1... | collective-permute-start | bytes 24584 | tf_op jit(solution)/shard_map/ppermute | solution.py:19
  33.0 1.3 %collective-permute-start.3 = (f32[8,128]{1,0:T(8,128)S(1)}, f32[8,128]{1,0:T(8,128)S(1)}, u32[]{:S(2)}, u32[]{:S(2)}) collective-permute-start(f32[8,128]{1,0:T(8,128)S(1)} %fusion.20), channel_id=1, source_target_pairs={{128,0},{256,128},{384,256},{129,1},{257,129},{385,257},{130,2},{2... | collective-permute-start | bytes 12296 | tf_op jit(solution)/shard_map/ppermute | solution.py:18
  34.3 4.2 %collective-permute-done.3 = f32[8,128]{1,0:T(8,128)S(1)} collective-permute-done((f32[8,128]{1,0:T(8,128)S(1)}, f32[8,128]{1,0:T(8,128)S(1)}, u32[]{:S(2)}, u32[]{:S(2)}) %collective-permute-start.3) | collective-permute-done | bytes 4128 | tf_op jit(solution)/shard_map/ppermute | solution.py:18
  38.7 0.1 reshape.517
  38.9 0.2 reshape.547
  39.1 0.1 reshape.548
  39.2 0.2 reshape.550
  39.7 0.1 reshape.519
  39.9 0.2 pad_maximum_fusion.2
  40.5 0.6 copy-done.9
  41.1 0.1 reshape.510
  41.2 0.2 pad_maximum_fusion.1
  41.5 0.1 reshape.531
  41.7 0.2 reshape.532
  42.0 0.2 reshape.549
  42.2 0.1 pad_maximum_fusion.24
  42.3 0.2 reshape.534
  42.6 1.9 %collective-permute-start.5 = (f32[264,128]{1,0:T(8,128)S(1)}, f32[264,128]{1,0:T(8,128)S(1)}, u32[]{:S(2)}, u32[]{:S(2)}) collective-permute-start(f32[264,128]{1,0:T(8,128)S(1)} %pad_bitcast_fusion.1), channel_id=1, source_target_pairs={{1,0},{2,1},{3,2},{4,3},{5,4},{6,5},{7,6},{9,8},{10,9},{11,10},{12... | collective-permute-start | bytes 405512 | tf_op jit(solution)/shard_map/ppermute | solution.py:18
  44.7 0.3 reshape.521
  45.1 0.5 slice-done
  45.5 0.1 reshape.524
  45.7 0.2 reshape.527
  46.0 2.4 %collective-permute-start.4 = (f32[336,128]{1,0:T(8,128)S(1)}, f32[336,128]{1,0:T(8,128)S(1)}, u32[]{:S(2)}, u32[]{:S(2)}) collective-permute-start(f32[336,128]{1,0:T(8,128)S(1)} %pad_bitcast_fusion), channel_id=1, source_target_pairs={{0,1},{1,2},{2,3},{3,4},{4,5},{5,6},{6,7},{8,9},{9,10},{10,11},{11... | collective-permute-start | bytes 516104 | tf_op jit(solution)/shard_map/ppermute | solution.py:19
  48.4 0.7 %fusion.16 = (f32[4,16,128]{2,1,0:T(8,128)}, f32[4,16,128]{2,1,0:T(8,128)}, f32[4,16,128]{2,1,0:T(8,128)}, f32[4,16,128]{2,1,0:T(8,128)}) fusion(s32[4,16,128]{2,1,0:T(8,128)S(1)} %get-tuple-element.11), kind=kLoop, calls=%fused_computation.111 | loop fusion | flops 212992 | bytes 163840 | tf_op jit(solution)/shard_map/sub | solution.py:110
  49.7 0.2 reshape.541
  50.0 0.8 %reshape.543 = f32[3,1,18,130]{3,2,1,0:T(8,128)} reshape(f32[7020]{0:T(1024)S(1)} %slice.448) | data formatting | bytes 56160 | tf_op jit(solution)/shard_map/reshape | solution.py:50
  50.8 1.9 %collective-permute-done.4 = f32[336,128]{1,0:T(8,128)S(1)} collective-permute-done((f32[336,128]{1,0:T(8,128)S(1)}, f32[336,128]{1,0:T(8,128)S(1)}, u32[]{:S(2)}, u32[]{:S(2)}) %collective-permute-start.4) | collective-permute-done | bytes 172064 | tf_op jit(solution)/shard_map/ppermute | solution.py:19
  52.9 0.1 concatenate.118
  53.2 0.1 reshape.530
  53.4 0.8 %select_bitcast_fusion = (f32[6,18,130]{2,1,0:T(8,128)S(1)}, f32[6,18,130]{2,1,0:T(8,128)}) fusion(f32[1,1,19,131]{3,2,1,0:T(8,128)S(1)} %reshape.537, f32[1,4,19,1]{3,2,1,0:T(8,128)S(1)} %reshape.548, f32[1,4,1,128]{3,2,1,0:T(1,128)S(1)} %bitcast.80, f32[1,4,16,128]{3,2,1,0:T(8,128)S(1)} %convert_bitcast_fusion.3, f32[1,4,2,128]{3,2,1,0:T(2,128)S(1)} %bitcast.58, ...), kind=kLoop, calls=%fused_computation.54 | loop fusion | flops 407160 | bytes 182012 | tf_op jit(solution)/shard_map/mul | solution.py:126
  54.2 0.9 %convert_bitcast_fusion.1 = (f32[6,18,130]{2,1,0:T(8,128)}, f32[6,18,130]{2,1,0:T(8,128)}) fusion(f32[1,1,19,131]{3,2,1,0:T(8,128)S(1)} %reshape.537, f32[1,4,19,1]{3,2,1,0:T(8,128)S(1)} %reshape.548, f32[1,4,1,128]{3,2,1,0:T(1,128)S(1)} %bitcast.81, f32[1,4,16,128]{3,2,1,0:T(8,128)S(1)} %convert_bitcast_fusion.3, f32[1,4,2,128]{3,2,1,0:T(2,128)S(1)} %bitcast.59, ...), kind=kLoop, calls=%fused_computation.52 | loop fusion | flops 140400 | bytes 182012 | tf_op jit(solution)/shard_map/mul | solution.py:109
  55.1 0.9 %subtract_bitcast_fusion = f32[6,18,130]{2,1,0:T(8,128)} fusion(f32[1,1,19,131]{3,2,1,0:T(8,128)S(1)} %reshape.537, f32[1,4,19,1]{3,2,1,0:T(8,128)S(1)} %reshape.548, f32[1,4,1,128]{3,2,1,0:T(1,128)S(1)} %bitcast.82, f32[1,4,16,128]{3,2,1,0:T(8,128)S(1)} %convert_bitcast_fusion.3, f32[1,4,2,128]{3,2,1,0:T(2,128)S(1)} %bitcast.60, ...), kind=kLoop, calls=%fused_computation.55 | loop fusion | flops 393120 | bytes 125852 | tf_op jit(solution)/shard_map/mul | solution.py:110
  55.9 0.7 %slice.447 = f32[7020]{0:T(1024)} slice(f32[43008]{0:T(1024)S(1)} %bitcast.76), slice={[35752:42772]} | slice | bytes 56160 | tf_op jit(solution)/shard_map/slice | solution.py:49
  56.6 0.8 %convert_bitcast_fusion.2 = f32[5,17,129]{2,1,0:T(8,128)} fusion(f32[1,4,19,1]{3,2,1,0:T(8,128)S(1)} %reshape.548, f32[1,4,1,128]{3,2,1,0:T(1,128)S(1)} %bitcast.83, f32[1,4,16,128]{3,2,1,0:T(8,128)S(1)} %convert_bitcast_fusion.3, f32[1,4,2,128]{3,2,1,0:T(2,128)S(1)} %bitcast.61, f32[1,4,19,2]{3,2,1,0:T(8,128)S(1)} %reshape.522, ...), kind=kLoop, calls=%fused_computation.69 | loop fusion | flops 76755 | bytes 103596 | tf_op jit(solution)/shard_map/mul | solution.py:102
  57.4 0.3 reshape.540
  57.9 0.2 pad_maximum_fusion
  58.1 0.2 slice_subtract_fusion.1
  58.4 0.3 fusion.2
  58.7 0.4 slice_subtract_fusion.4
  59.1 0.3 copy-done.17
  59.4 0.8 %reshape.542 = f32[3,1,18,130]{3,2,1,0:T(8,128)} reshape(f32[7020]{0:T(1024)S(1)} %copy-done.17) | data formatting | bytes 56160 | tf_op jit(solution)/shard_map/reshape | solution.py:49
  60.4 0.8 %copy-done.3 = f32[6,18,130]{2,1,0:T(8,128)S(1)} copy-done((f32[6,18,130]{2,1,0:T(8,128)S(1)}, f32[6,18,130]{2,1,0:T(8,128)}, u32[]{:S(2)}) %copy-start.3) | copy-done | bytes 56184
  61.5 0.4 fusion.6
  61.9 0.2 slice_subtract_fusion.7
  62.0 0.2 slice_subtract_fusion.17
  62.3 0.9 %copy-done.7 = f32[5,17,129]{2,1,0:T(8,128)S(1)} copy-done((f32[5,17,129]{2,1,0:T(8,128)S(1)}, f32[5,17,129]{2,1,0:T(8,128)}, u32[]{:S(2)}) %copy-start.7) | copy-done | bytes 43884
  63.1 0.2 fusion.9
  63.6 0.5 copy-done.8
  64.1 0.3 copy-done.2
  64.4 0.8 %broadcast_multiply_fusion = (f32[3,4,16,128]{3,2,1,0:T(8,128)}, f32[3,4,16,128]{3,2,1,0:T(8,128)S(1)}) fusion(f32[3,4,16,128]{3,2,1,0:T(8,128)S(1)} %copy-done.2, f32[3,6,18,130]{3,2,1,0:T(8,128)S(1)} %get-tuple-element.16, f32[4,16,128]{2,1,0:T(8,128)S(1)} %copy-done.15, f32[3,6,18,130]{3,2,1,0:T(8,128)S(1)} %get-tuple-element.17), kind=kLoop, calls=%fused_computation.98 | loop fusion | flops 196608 | bytes 524288 | tf_op jit(solution)/shard_map/div | solution.py:135
  65.2 0.7 %copy-done.12 = f32[4,16,128]{2,1,0:T(8,128)S(1)} copy-done((f32[4,16,128]{2,1,0:T(8,128)S(1)}, f32[4,16,128]{2,1,0:T(8,128)}, u32[]{:S(2)}) %copy-start.12) | copy-done | bytes 32792
  66.0 0.8 %multiply_add_fusion = (f32[3,4,16,128]{3,2,1,0:T(8,128)}, f32[3,4,16,128]{3,2,1,0:T(8,128)}) fusion(f32[3,4,16,128]{3,2,1,0:T(8,128)S(1)} %get-tuple-element.9, f32[3,4,16,128]{3,2,1,0:T(8,128)S(1)} %copy-done.2, f32[3,6,18,130]{3,2,1,0:T(8,128)S(1)} %get-tuple-element.17, f32[4,16,128]{2,1,0:T(8,128)S(1)} %copy-done.13, f32[4,16,128]{2,1,0:T(8,128)S(1)} %copy-done.14, ...), kind=kLoop, calls=%fused_computation.83 | loop fusion | flops 319488 | bytes 819200 | tf_op jit(solution)/shard_map/add | solution.py:139
  (120 shorter events, 4.5 us)
Async XLA Ops:
  0.6 1.0 %copy-start.23 = (s32[4,16,128]{2,1,0:T(8,128)S(1)}, s32[4,16,128]{2,1,0:T(8,128)}, u32[]{:S(2)}) copy-start(s32[4,16,128]{2,1,0:T(8,128)} %param.10) | copy-start | bytes 98308
  1.6 0.8 %copy-start.22 = (s32[4,16,128]{2,1,0:T(8,128)S(1)}, s32[4,16,128]{2,1,0:T(8,128)}, u32[]{:S(2)}) copy-start(s32[4,16,128]{2,1,0:T(8,128)} %param.11) | copy-start | bytes 98308
  2.4 0.9 %copy-start = (f32[3,4,16,128]{3,2,1,0:T(8,128)S(1)}, f32[3,4,16,128]{3,2,1,0:T(8,128)}, u32[]{:S(2)}) copy-start(f32[3,4,16,128]{3,2,1,0:T(8,128)} %param.7) | copy-start | bytes 294916
  2.4 1.0 %copy-start.1 = (f32[3,4,16,128]{3,2,1,0:T(8,128)S(1)}, f32[3,4,16,128]{3,2,1,0:T(8,128)}, u32[]{:S(2)}) copy-start(f32[3,4,16,128]{3,2,1,0:T(8,128)} %param.6) | copy-start | bytes 294916
  3.4 14.7 %collective-permute-start.1 = (f32[56,128]{1,0:T(8,128)S(1)}, f32[56,128]{1,0:T(8,128)S(1)}, u32[]{:S(2)}, u32[]{:S(2)}) collective-permute-start(f32[56,128]{1,0:T(8,128)S(1)} %fusion.19), channel_id=1, source_target_pairs={{8,0},{16,8},{24,16},{32,24},{40,32},{48,40},{56,48},{64,56},{72,6... | collective-permute-start | bytes 86024 | tf_op jit(solution)/shard_map/ppermute | solution.py:18
  16.1 11.4 %collective-permute-start = (f32[72,128]{1,0:T(8,128)S(1)}, f32[72,128]{1,0:T(8,128)S(1)}, u32[]{:S(2)}, u32[]{:S(2)}) collective-permute-start(f32[72,128]{1,0:T(8,128)S(1)} %fusion.14), channel_id=1, source_target_pairs={{0,8},{8,16},{16,24},{24,32},{32,40},{40,48},{48,56},{56,64},{64,7... | collective-permute-start | bytes 110600 | tf_op jit(solution)/shard_map/ppermute | solution.py:19
  18.1 24.1 %copy-start.18 = (f32[3,4,1,128]{3,1,0,2:T(4,128)}, f32[3,4,1,128]{3,1,0,2:T(4,128)S(1)}, u32[]{:S(2)}) copy-start(f32[3,4,1,128]{3,1,0,2:T(4,128)S(1)} %reshape.506) | copy-start | bytes 18436
  28.0 14.2 %copy-start.20 = (f32[3,4,1,128]{3,1,0,2:T(4,128)}, f32[3,4,1,128]{3,1,0,2:T(4,128)S(1)}, u32[]{:S(2)}) copy-start(f32[3,4,1,128]{3,1,0,2:T(4,128)S(1)} %reshape.505) | copy-start | bytes 18436
  29.4 10.0 %collective-permute-start.2 = (f32[16,128]{1,0:T(8,128)S(1)}, f32[16,128]{1,0:T(8,128)S(1)}, u32[]{:S(2)}, u32[]{:S(2)}) collective-permute-start(f32[16,128]{1,0:T(8,128)S(1)} %pad_bitcast_fusion.2), channel_id=1, source_target_pairs={{0,128},{128,256},{256,384},{1,129},{129,257},{257,385},{2,130},{1... | collective-permute-start | bytes 24584 | tf_op jit(solution)/shard_map/ppermute | solution.py:19
  33.0 5.5 %collective-permute-start.3 = (f32[8,128]{1,0:T(8,128)S(1)}, f32[8,128]{1,0:T(8,128)S(1)}, u32[]{:S(2)}, u32[]{:S(2)}) collective-permute-start(f32[8,128]{1,0:T(8,128)S(1)} %fusion.20), channel_id=1, source_target_pairs={{128,0},{256,128},{384,256},{129,1},{257,129},{385,257},{130,2},{2... | collective-permute-start | bytes 12296 | tf_op jit(solution)/shard_map/ppermute | solution.py:18
  40.5 0.6 copy-start.9
  42.6 6.6 %collective-permute-start.5 = (f32[264,128]{1,0:T(8,128)S(1)}, f32[264,128]{1,0:T(8,128)S(1)}, u32[]{:S(2)}, u32[]{:S(2)}) collective-permute-start(f32[264,128]{1,0:T(8,128)S(1)} %pad_bitcast_fusion.1), channel_id=1, source_target_pairs={{1,0},{2,1},{3,2},{4,3},{5,4},{6,5},{7,6},{9,8},{10,9},{11,10},{12... | collective-permute-start | bytes 405512 | tf_op jit(solution)/shard_map/ppermute | solution.py:18
  44.7 0.8 %slice-start = ((f32[1,4,19,131]{3,2,1,0:T(8,128)}), f32[1,2,19,131]{3,2,1,0:T(8,128)S(1)}, s32[]{:S(2)}) async-start(f32[1,4,19,131]{3,2,1,0:T(8,128)} %copy-done.9), calls=%async_computation | async-start | bytes 98304 | tf_op jit(solution)/shard_map/slice | solution.py:26
  46.0 6.7 %collective-permute-start.4 = (f32[336,128]{1,0:T(8,128)S(1)}, f32[336,128]{1,0:T(8,128)S(1)}, u32[]{:S(2)}, u32[]{:S(2)}) collective-permute-start(f32[336,128]{1,0:T(8,128)S(1)} %pad_bitcast_fusion), channel_id=1, source_target_pairs={{0,1},{1,2},{2,3},{3,4},{4,5},{5,6},{6,7},{8,9},{9,10},{10,11},{11... | collective-permute-start | bytes 516104 | tf_op jit(solution)/shard_map/ppermute | solution.py:19
  58.7 0.8 %copy-start.17 = (f32[7020]{0:T(1024)S(1)}, f32[7020]{0:T(1024)}, u32[]{:S(2)}) copy-start(f32[7020]{0:T(1024)} %slice.447) | copy-start | bytes 84244
  60.3 0.9 %copy-start.3 = (f32[6,18,130]{2,1,0:T(8,128)S(1)}, f32[6,18,130]{2,1,0:T(8,128)}, u32[]{:S(2)}) copy-start(f32[6,18,130]{2,1,0:T(8,128)} %get-tuple-element.43) | copy-start | bytes 168484
  60.3 1.0 %copy-start.4 = (f32[6,18,130]{2,1,0:T(8,128)S(1)}, f32[6,18,130]{2,1,0:T(8,128)}, u32[]{:S(2)}) copy-start(f32[6,18,130]{2,1,0:T(8,128)} %get-tuple-element.44) | copy-start | bytes 168484
  60.3 1.0 %copy-start.5 = (f32[6,18,130]{2,1,0:T(8,128)S(1)}, f32[6,18,130]{2,1,0:T(8,128)}, u32[]{:S(2)}) copy-start(f32[6,18,130]{2,1,0:T(8,128)} %get-tuple-element.45) | copy-start | bytes 168484
  60.3 1.1 %copy-start.6 = (f32[6,18,130]{2,1,0:T(8,128)S(1)}, f32[6,18,130]{2,1,0:T(8,128)}, u32[]{:S(2)}) copy-start(f32[6,18,130]{2,1,0:T(8,128)} %subtract_bitcast_fusion) | copy-start | bytes 168484
  60.3 1.2 %copy-start.10 = (f32[3,1,18,130]{3,2,1,0:T(8,128)S(1)}, f32[3,1,18,130]{3,2,1,0:T(8,128)}, u32[]{:S(2)}) copy-start(f32[3,1,18,130]{3,2,1,0:T(8,128)} %reshape.543) | copy-start | bytes 84244
  60.3 1.2 %copy-start.11 = (f32[3,1,18,130]{3,2,1,0:T(8,128)S(1)}, f32[3,1,18,130]{3,2,1,0:T(8,128)}, u32[]{:S(2)}) copy-start(f32[3,1,18,130]{3,2,1,0:T(8,128)} %reshape.542) | copy-start | bytes 84244
  60.4 1.1 %copy-start.21 = (f32[3,4,1,128]{3,1,0,2:T(4,128)S(1)}, f32[3,4,1,128]{3,1,0,2:T(4,128)}, u32[]{:S(2)}) copy-start(f32[3,4,1,128]{3,1,0,2:T(4,128)} %copy-done.20) | copy-start | bytes 18436
  60.4 1.1 %copy-start.19 = (f32[3,4,1,128]{3,1,0,2:T(4,128)S(1)}, f32[3,4,1,128]{3,1,0,2:T(4,128)}, u32[]{:S(2)}) copy-start(f32[3,4,1,128]{3,1,0,2:T(4,128)} %copy-done.18) | copy-start | bytes 18436
  62.2 0.9 %copy-start.7 = (f32[5,17,129]{2,1,0:T(8,128)S(1)}, f32[5,17,129]{2,1,0:T(8,128)}, u32[]{:S(2)}) copy-start(f32[5,17,129]{2,1,0:T(8,128)} %convert_bitcast_fusion.2) | copy-start | bytes 131584
  63.4 0.6 copy-start.8
  63.5 0.9 %copy-start.2 = (f32[3,4,16,128]{3,2,1,0:T(8,128)S(1)}, f32[3,4,16,128]{3,2,1,0:T(8,128)}, u32[]{:S(2)}) copy-start(f32[3,4,16,128]{3,2,1,0:T(8,128)} %param.8) | copy-start | bytes 294916
  63.5 0.9 %copy-start.15 = (f32[4,16,128]{2,1,0:T(8,128)S(1)}, f32[4,16,128]{2,1,0:T(8,128)}, u32[]{:S(2)}) copy-start(f32[4,16,128]{2,1,0:T(8,128)} %get-tuple-element.61) | copy-start | bytes 98308
  65.2 0.8 %copy-start.12 = (f32[4,16,128]{2,1,0:T(8,128)S(1)}, f32[4,16,128]{2,1,0:T(8,128)}, u32[]{:S(2)}) copy-start(f32[4,16,128]{2,1,0:T(8,128)} %get-tuple-element.59) | copy-start | bytes 98308
  65.2 0.8 %copy-start.13 = (f32[4,16,128]{2,1,0:T(8,128)S(1)}, f32[4,16,128]{2,1,0:T(8,128)}, u32[]{:S(2)}) copy-start(f32[4,16,128]{2,1,0:T(8,128)} %get-tuple-element.60) | copy-start | bytes 98308
  65.2 0.8 %copy-start.14 = (f32[4,16,128]{2,1,0:T(8,128)S(1)}, f32[4,16,128]{2,1,0:T(8,128)}, u32[]{:S(2)}) copy-start(f32[4,16,128]{2,1,0:T(8,128)} %get-tuple-element.62) | copy-start | bytes 98308
  65.2 0.8 %copy-start.16 = (f32[4,16,128]{2,1,0:T(8,128)S(1)}, f32[4,16,128]{2,1,0:T(8,128)}, u32[]{:S(2)}) copy-start(f32[4,16,128]{2,1,0:T(8,128)} %get-tuple-element.10) | copy-start | bytes 98308

commit v2 on v0

v2 whole, which is shorter than its diff:
```python
import functools

import jax
import jax.numpy as jnp
from jax import lax
from jax.experimental import pallas as pl
from jax.experimental.pallas import tpu as pltpu
from jax.sharding import PartitionSpec as P

time_step = 0.5
damping = 0.2
omega_sq = 1.0
strength = 3.0

DECAY = 1.0 + 0.5 * damping * time_step
HOLD = (1.0 - 0.5 * damping * time_step) / DECAY
PULL = time_step * omega_sq / DECAY
GAIN = PULL * strength

EX, EY, EZ, HX, HY, HZ, QX, QY, QZ, CODE = range(10)
EVERY = tuple(range(10))

Y_UP = [(c, 14) for c in (EX, EY, EZ, HX, HZ, CODE)] + [(c, 15) for c in EVERY]
Y_DOWN = [(c, 0) for c in (EX, EY, EZ, HX, HY, HZ, QX, QZ, CODE)] + [(EX, 1), (EZ, 1)]
Z_UP = [(c, 2) for c in (EX, EY, EZ, HX, HY, CODE)] + [(c, 3) for c in EVERY]
Z_DOWN = [(c, 0) for c in (EX, EY, EZ, HX, HY, HZ, QX, QY, CODE)] + [(EX, 1), (EY, 1)]

ROWS = 24
PLANES = range(-2, 6)
SPAN = 32


def up_of(n):
    return [(i, i + 1) for i in range(n - 1)]


def down_of(n):
    return [(i + 1, i) for i in range(n - 1)]


def code_of(material, pml):
    return (1 + 4 * material + pml).astype(jnp.float32)


def y_faces(e, h, p, j, material, pml, up, down):
    def face(c, row):
        if c < HX:
            return e[c, :, row, :]
        if c < QX:
            return h[c - HX, :, row, :]
        if c < CODE:
            return HOLD * j[c - QX, :, row, :] - PULL * p[c - QX, :, row, :]
        return code_of(material[:, row, :], pml[:, row, :])

    down[...] = jnp.zeros_like(down)
    for ref, faces in ((up, Y_UP), (down, Y_DOWN)):
        for i, (c, row) in enumerate(faces):
            ref[4 * i : 4 * i + 4, :] = face(c, row)


def z_faces(e, h, p, j, material, pml, before, after, wide, up, down):
    for z in range(4):
        for c in EVERY:
            if c < HX:
                own = e[c, z]
            elif c < QX:
                own = h[c - HX, z]
            elif c < CODE:
                own = HOLD * j[c - QX, z] - PULL * p[c - QX, z]
            else:
                own = code_of(material[z], pml[z])
            wide[z, c, 0:16, :] = own
            wide[z, c, 16:24, :] = jnp.zeros((8, 128), jnp.float32)
        for i, (c, row) in enumerate(Y_UP):
            wide[z, c, row + 8 : row + 9, :] = before[4 * i + z : 4 * i + z + 1, :]
        for i, (c, row) in enumerate(Y_DOWN):
            wide[z, c, row + 16 : row + 17, :] = after[4 * i + z : 4 * i + z + 1, :]
    for i, (c, z) in enumerate(Z_UP):
        up[i] = wide[z, c]
    for i, (c, z) in enumerate(Z_DOWN):
        down[i] = wide[z, c]


def planes_of(flags, wide, before, after):
    first = flags[0] == 0
    last = flags[1] == 0

    def plane(c, z):
        if 0 <= z < 4:
            return wide[z, c]
        if z < 0:
            if (c, z + 4) not in Z_UP:
                return None
            got = before[Z_UP.index((c, z + 4))]
            return jnp.where(first, 0.0, got)
        if (c, z - 4) not in Z_DOWN:
            return None
        got = after[Z_DOWN.index((c, z - 4))]
        return jnp.where(last, 0.0, got)

    return plane


def lanes():
    return lax.broadcasted_iota(jnp.int32, (ROWS, 128), 1)


def roll(array, shift, axis):
    shift = shift % array.shape[axis]
    return pltpu.roll(array, shift, axis) if shift else array


def x_edges(flags, wide, before, after, edges):
    plane = planes_of(flags, wide, before, after)
    lane = lanes()
    for g in range(3):
        total = jnp.zeros((ROWS, 128), jnp.float32)
        for c in range(4 * g, min(4 * g + 4, 10)):
            for z in PLANES:
                value = plane(c, z)
                if value is None:
                    continue
                at = SPAN * (c - 4 * g) + 4 * (z + 2)
                moved = roll(value, at - 126, 1)
                total = jnp.where((lane >= at) & (lane < at + 4), moved, total)
        edges[g] = total


def factors(code):
    metal = code > 8.5
    dielec = (code > 4.5) & (code < 8.5)
    inside = code > 0.5
    level = code - jnp.where(metal, 9.0, jnp.where(dielec, 5.0, 1.0))
    loss = jnp.where(level > 2.5, 0.25, jnp.where(level > 1.5, 0.1, jnp.where(level > 0.5, 0.025, 0.0)))
    permit = jnp.where(metal, 1.5, jnp.where(dielec, 2.25, 1.0))
    over_h = jnp.where(inside, 1.0 / (1.0 + loss), 0.0)
    over_e = jnp.where(inside, 1.0 / (permit + loss), 0.0)
    return (
        (1.0 - loss) * over_h,
        time_step * over_h,
        (permit - loss) * over_e,
        time_step * over_e,
        jnp.where(metal, 1.0, 0.0),
    )


def magnetic_new(h, e, ey, ez, ex, keep, push):
    curl = (
        (ey[2] - e[2]) - (ez[1] - e[1]),
        (ez[0] - e[0]) - (ex[2] - e[2]),
        (ex[1] - e[1]) - (ey[0] - e[0]),
    )
    return [None if h[k] is None else keep * h[k] - push * curl[k] for k in range(3)]


def electric_new(e, h, hy, hz, hx, drag, keep, push):
    curl = (
        (h[2] - hy[2]) - (h[1] - hz[1]),
        (h[0] - hz[0]) - (h[2] - hx[2]),
        (h[1] - hx[1]) - (h[0] - hy[0]),
    )
    return [keep * e[k] + push * (curl[k] - drag[k]) for k in range(3)]


def both_steps(flags, wide, before, after, own, left, right, polar, e_out, h_out, p_out, j_out, h1, e1, h2):
    plane = planes_of(flags, wide, before, after)
    lane = lanes()
    side = (lane % 4) < 2

    edge = []
    for g in range(3):
        low = jnp.where(side, left[g], own[g])
        high = jnp.where(side, own[g], right[g])
        for k in range(4):
            edge.append(jnp.where(lane < SPAN, roll(low, -SPAN * k, 1), roll(high, SPAN - SPAN * k, 1)))
    x_next = lambda a: roll(a, -1, 1)
    x_back = lambda a: roll(a, 1, 1)
    y_next = lambda a: roll(a, -1, 0)
    y_back = lambda a: roll(a, 1, 0)
    z_next = lambda a: roll(a, -4, 1)
    z_back = lambda a: roll(a, 4, 1)

    def nexts(f):
        return (
            {0: y_next(f[0]), 2: y_next(f[2])},
            {0: z_next(f[0]), 1: z_next(f[1])},
            {1: x_next(f[1]), 2: x_next(f[2])},
        )

    def backs(f):
        return (
            {0: y_back(f[0]), 2: y_back(f[2])},
            {0: z_back(f[0]), 1: z_back(f[1])},
            {1: x_back(f[1]), 2: x_back(f[2])},
        )

    keep_h, push_h, keep_e, push_e, metal = factors(edge[CODE])
    ce0 = edge[EX : EZ + 1]
    ch1 = magnetic_new(edge[HX : HZ + 1], ce0, *nexts(ce0), keep_h, push_h)
    drag = [metal * (edge[QX + k] + GAIN * ce0[k]) for k in range(3)]
    ce1 = electric_new(ce0, ch1, *backs(ch1), drag, keep_e, push_e)
    ch2 = magnetic_new(ch1, ce1, *nexts(ce1), keep_h, push_h)

    def after_x(array, z, column):
        return jnp.where(lane == 127, roll(column, 127 - (SPAN + 4 * (z + 2) + 2), 1), roll(array, -1, 1))

    def before_x(array, z, column):
        return jnp.where(lane == 0, roll(column, -(4 * (z + 2) + 1), 1), roll(array, 1, 1))

    for z in range(-2, 5):
        e = [plane(EX + k, z) for k in range(3)]
        up = [plane(EX + k, z + 1) for k in range(2)]
        h = [plane(HX + k, z) for k in range(3)]
        keep_h, push_h, _, _, _ = factors(plane(CODE, z))
        new = magnetic_new(
            h,
            e,
            {0: y_next(e[0]), 2: y_next(e[2])},
            {0: up[0], 1: up[1]},
            {1: after_x(e[1], z, ce0[1]), 2: after_x(e[2], z, ce0[2])},
            keep_h,
            push_h,
        )
        for k in range(3):
            if new[k] is not None:
                h1[z + 2, k] = new[k]
    for z in range(-1, 5):
        e = [plane(EX + k, z) for k in range(3)]
        h = [h1[z + 2, k] for k in range(3)]
        down = [h1[z + 1, k] for k in range(2)]
        _, _, keep_e, push_e, metal = factors(plane(CODE, z))
        held = [plane(QX + k, z) for k in range(3)]
        flow = [None if held[k] is None else held[k] + GAIN * metal * e[k] for k in range(3)]
        if 0 <= z < 4:
            for k in range(3):
                j_out[k, z] = flow[k][0:16]
        new = electric_new(
            e,
            h,
            {0: y_back(h[0]), 2: y_back(h[2])},
            {0: down[0], 1: down[1]},
            {1: before_x(h[1], z, ch1[1]), 2: before_x(h[2], z, ch1[2])},
            [0.0 if flow[k] is None else metal * flow[k] for k in range(3)],
            keep_e,
            push_e,
        )
        for k in range(3):
            e1[z + 1, k] = new[k]
    for z in range(-1, 4):
        e = [e1[z + 1, k] for k in range(3)]
        up = [e1[z + 2, k] for k in range(2)]
        h = [h1[z + 2, k] for k in range(3)]
        keep_h, push_h, _, _, _ = factors(plane(CODE, z))
        new = magnetic_new(
            h,
            e,
            {0: y_next(e[0]), 2: y_next(e[2])},
            {0: up[0], 1: up[1]},
            {1: after_x(e[1], z, ce1[1]), 2: after_x(e[2], z, ce1[2])},
            keep_h,
            push_h,
        )
        for k in range(3):
            h2[z + 1, k] = new[k]
            if z >= 0:
                h_out[k, z] = new[k][0:16]
    for z in range(4):
        h = [h2[z + 1, k] for k in range(3)]
        down = [h2[z, k] for k in range(2)]
        _, _, keep_e, push_e, metal = [f[0:16] for f in factors(plane(CODE, z))]
        e = [e1[z + 1, k][0:16] for k in range(3)]
        drag = []
        for k in range(3):
            flow = j_out[k, z]
            bound = polar[k, z] + time_step * flow
            flow = HOLD * flow - PULL * bound + GAIN * metal * e[k]
            j_out[k, z] = flow
            p_out[k, z] = bound + time_step * flow
            drag.append(metal * flow)
        new = electric_new(
            e,
            [a[0:16] for a in h],
            {0: y_back(h[0])[0:16], 2: y_back(h[2])[0:16]},
            {0: down[0][0:16], 1: down[1][0:16]},
            {1: before_x(h[1], z, ch2[1])[0:16], 2: before_x(h[2], z, ch2[2])[0:16]},
            drag,
            keep_e,
            push_e,
        )
        for k in range(3):
            e_out[k, z] = new[k]


VMEM = pl.BlockSpec(memory_space=pltpu.VMEM)
SMEM = pl.BlockSpec(memory_space=pltpu.SMEM)


def call(kernel, outs, args, scratch=(), flops=0, name=None):
    size = sum(a.size for a in args) + sum(o.size for o in outs)
    return pl.pallas_call(
        kernel,
        out_shape=outs,
        in_specs=[SMEM if a.ndim == 1 else VMEM for a in args],
        out_specs=[VMEM] * len(outs),
        scratch_shapes=list(scratch),
        cost_estimate=pl.CostEstimate(flops=flops, bytes_accessed=4 * size, transcendentals=0),
        compiler_params=pltpu.CompilerParams(vmem_limit_bytes=16 * 2**20),
        name=name,
    )(*args)


def f32(*shape):
    return jax.ShapeDtypeStruct(shape, jnp.float32)


def on_device(electric, magnetic, polar, current, material, pml):
    cells = (electric, magnetic, polar, current, material, pml)
    gx, gy, gz = (lax.axis_size(a) for a in ("gx", "gy", "gz"))
    place = lax.axis_index("gz")
    flags = jnp.stack([place, gz - 1 - place]).astype(jnp.int32)

    up, down = call(y_faces, [f32(64, 128), f32(48, 128)], cells, name="y_faces")
    before = lax.ppermute(up, "gy", up_of(gy))
    after = lax.ppermute(down, "gy", down_of(gy))

    wide, up, down = call(
        z_faces,
        [f32(4, 10, ROWS, 128), f32(16, ROWS, 128), f32(11, ROWS, 128)],
        (*cells, before, after),
        name="z_faces",
    )
    before = lax.ppermute(up, "gz", [(i, (i + 1) % gz) for i in range(gz)])
    after = lax.ppermute(down, "gz", [((i + 1) % gz, i) for i in range(gz)])

    (own,) = call(x_edges, [f32(3, ROWS, 128)], (flags, wide, before, after), name="x_edges")
    left = lax.ppermute(own, "gx", up_of(gx))
    right = lax.ppermute(own, "gx", down_of(gx))

    return tuple(
        call(
            both_steps,
            [f32(3, 4, 16, 128)] * 4,
            (flags, wide, before, after, own, left, right, polar),
            scratch=[
                pltpu.VMEM((7, 3, ROWS, 128), jnp.float32),
                pltpu.VMEM((6, 3, ROWS, 128), jnp.float32),
                pltpu.VMEM((5, 3, ROWS, 128), jnp.float32),
            ],
            flops=4_000_000,
            name="both_steps",
        )
    )


def solution(mesh):
    fields = P(None, "gz", "gy", "gx")
    cells = P("gz", "gy", "gx")
    return jax.shard_map(
        on_device,
        mesh=mesh,
        in_specs=(fields, fields, fields, fields, cells, cells),
        out_specs=(fields, fields, fields, fields),
        check_vma=False,
    )
```

time: 93.3 us -> 43.7 us (0.47)
  the two profiles are of different devices: /device:TPU:1 before, /device:TPU:38 now
where the time goes in v2:
time: 43.7 us; the launch traced here: 43.2 us
  starting transfers between devices  22.8 us (52%)
  waiting for transfers between devices  11.8 us (27%)
  local copies, waits for them, and re-layouts  5.08 us (12%)
  Pallas kernels  2.75 us (6%)
  between operations  0.71 us (2%)
    ppermute x1, starting transfers between devices, on_device(): before = lax.ppermute(up, 'gy', up_of(gy))  9.1 us
    unnamed x14, local copies, waits for them, and re-layouts  5.08 us
    ppermute x1, waiting for transfers between devices, on_device(): after = lax.ppermute(down, 'gy', down_of(gy))  5.06 us
    ppermute x1, starting transfers between devices, on_device(): after = lax.ppermute(down, 'gy', down_of(gy))  4.92 us
    ppermute x1, starting transfers between devices, on_device(): right = lax.ppermute(own, 'gx', down_of(gx))  3.44 us
    ppermute x1, waiting for transfers between devices, on_device(): left = lax.ppermute(own, 'gx', up_of(gx))  3.43 us
    ppermute x1, starting transfers between devices, on_device(): after = lax.ppermute(down, 'gz', [((i + 1) % gz, i) for i in range(gz)])  2.94 us
    pallas_call x4, Pallas kernels, call(): pl.pallas_call(kernel, out_shape=outs, in_specs=[SMEM if a.ndim == 1 else...  2.75 us
  transfers between devices with their start and end apart: 6, of which 4 were waited for; matrix products, arithmetic and copies ran while one was open for 0% of the time, Pallas kernels for 0%

profile of v2, /device:TPU:38, one launch (start us, length us, event | category | flops | bytes accessed | tf_op | source)
XLA Modules:
  0.0 43.2 jit_solution(11108629076848383281)
XLA Ops:
  0.6 0.0 copy-start
  0.6 0.9 %copy-done = f32[3,4,16,128]{3,2,1,0:T(8,128)S(1)} copy-done((f32[3,4,16,128]{3,2,1,0:T(8,128)S(1)}, f32[3,4,16,128]{3,2,1,0:T(8,128)}, u32[]{:S(2)}) %copy-start) | copy-done | bytes 98328
  1.5 0.0 copy-start.2
  1.5 0.9 %copy-done.2 = f32[3,4,16,128]{3,2,1,0:T(8,128)S(1)} copy-done((f32[3,4,16,128]{3,2,1,0:T(8,128)S(1)}, f32[3,4,16,128]{3,2,1,0:T(8,128)}, u32[]{:S(2)}) %copy-start.2) | copy-done | bytes 98328
  2.4 0.0 copy-start.3
  2.4 0.9 %copy-done.3 = f32[3,4,16,128]{3,2,1,0:T(8,128)S(1)} copy-done((f32[3,4,16,128]{3,2,1,0:T(8,128)S(1)}, f32[3,4,16,128]{3,2,1,0:T(8,128)}, u32[]{:S(2)}) %copy-start.3) | copy-done | bytes 98328
  3.3 0.0 copy-start.4
  3.3 0.9 %copy-done.4 = f32[3,4,16,128]{3,2,1,0:T(8,128)S(1)} copy-done((f32[3,4,16,128]{3,2,1,0:T(8,128)S(1)}, f32[3,4,16,128]{3,2,1,0:T(8,128)}, u32[]{:S(2)}) %copy-start.4) | copy-done | bytes 98328
  4.2 0.0 copy-start.5
  4.2 0.8 %copy-done.5 = s32[4,16,128]{2,1,0:T(8,128)S(1)} copy-done((s32[4,16,128]{2,1,0:T(8,128)S(1)}, s32[4,16,128]{2,1,0:T(8,128)}, u32[]{:S(2)}) %copy-start.5) | copy-done | bytes 32792
  5.0 0.0 copy-start.6
  5.0 0.8 %copy-done.6 = s32[4,16,128]{2,1,0:T(8,128)S(1)} copy-done((s32[4,16,128]{2,1,0:T(8,128)S(1)}, s32[4,16,128]{2,1,0:T(8,128)}, u32[]{:S(2)}) %copy-start.6) | copy-done | bytes 32792
  5.7 0.1 y_faces.1
  5.8 9.1 %collective-permute-start = (f32[64,128]{1,0:T(8,128)S(1)}, f32[64,128]{1,0:T(8,128)S(1)}, u32[]{:S(2)}, u32[]{:S(2)}) collective-permute-start(f32[64,128]{1,0:T(8,128)S(1)} %get-tuple-element.9), channel_id=1, source_target_pairs={{0,8},{8,16},{16,24},{24,32},{32,40},{40,48},{48,56},{56,64},{64,7... | collective-permute-start | bytes 98312 | tf_op jit(solution)/shard_map/ppermute | solution.py:323
  14.9 4.9 %collective-permute-start.1 = (f32[48,128]{1,0:T(8,128)S(1)}, f32[48,128]{1,0:T(8,128)S(1)}, u32[]{:S(2)}, u32[]{:S(2)}) collective-permute-start(f32[48,128]{1,0:T(8,128)S(1)} %get-tuple-element.10), channel_id=1, source_target_pairs={{8,0},{16,8},{24,16},{32,24},{40,32},{48,40},{56,48},{64,56},{72,6... | collective-permute-start | bytes 73736 | tf_op jit(solution)/shard_map/ppermute | solution.py:324
  19.8 5.1 %collective-permute-done.1.after = f32[48,128]{1,0:T(8,128)S(1)} collective-permute-done((f32[48,128]{1,0:T(8,128)S(1)}, f32[48,128]{1,0:T(8,128)S(1)}, u32[]{:S(2)}, u32[]{:S(2)}) %collective-permute-start.1) | collective-permute-done | bytes 24608 | tf_op jit(solution)/shard_map/ppermute | solution.py:324
  24.9 0.0 collective-permute-done.before
  24.9 0.1 z_faces.1
  25.0 0.0 collective-permute-start.2
  25.0 2.9 %collective-permute-start.3 = (f32[11,24,128]{2,1,0:T(8,128)S(1)}, f32[11,24,128]{2,1,0:T(8,128)S(1)}, u32[]{:S(2)}, u32[]{:S(2)}) collective-permute-start(f32[11,24,128]{2,1,0:T(8,128)S(1)} %get-tuple-element.13), channel_id=1, source_target_pairs={{1,0},{2,1},{3,2},{4,3},{5,4},{6,5},{7,6},{0,7},{9,8},{10,9},{11,1... | collective-permute-start | bytes 405512 | tf_op jit(solution)/shard_map/ppermute | solution.py:333
  28.0 0.1 pad_add_fusion.flags
  28.0 2.5 %collective-permute-done.3.after = f32[11,24,128]{2,1,0:T(8,128)S(1)} collective-permute-done((f32[11,24,128]{2,1,0:T(8,128)S(1)}, f32[11,24,128]{2,1,0:T(8,128)S(1)}, u32[]{:S(2)}, u32[]{:S(2)}) %collective-permute-start.3) | collective-permute-done | bytes 135200 | tf_op jit(solution)/shard_map/ppermute | solution.py:333
  30.5 0.8 %collective-permute-done.2.before = f32[16,24,128]{2,1,0:T(8,128)S(1)} collective-permute-done((f32[16,24,128]{2,1,0:T(8,128)S(1)}, f32[16,24,128]{2,1,0:T(8,128)S(1)}, u32[]{:S(2)}, u32[]{:S(2)}) %collective-permute-start.2) | collective-permute-done | bytes 196640 | tf_op jit(solution)/shard_map/ppermute | solution.py:332
  31.3 0.0 copy-start.1
  31.3 0.8 %x_edges.1.own = f32[3,24,128]{2,1,0:T(8,128)S(1)} custom-call(s32[2]{0:T(128)S(1)} %pad_add_fusion.flags, f32[4,10,24,128]{3,2,1,0:T(8,128)S(1)} %get-tuple-element.11.wide, f32[16,24,128]{2,1,0:T(8,128)S(1)} %collective-permute-done.2.before, f32[11,24,128]{2,1,0:T(8,128)S(1)} %collective-permute-done.3.after), custom_call_target="tpu_custom_call" | custom-call | bytes 860168 | tf_op jit(solution)/shard_map/x_edges/pallas_call | solution.py:300
  32.1 3.4 %collective-permute-start.5 = (f32[3,24,128]{2,1,0:T(8,128)S(1)}, f32[3,24,128]{2,1,0:T(8,128)S(1)}, u32[]{:S(2)}, u32[]{:S(2)}) collective-permute-start(f32[3,24,128]{2,1,0:T(8,128)S(1)} %x_edges.1.own), channel_id=1, source_target_pairs={{128,0},{256,128},{384,256},{129,1},{257,129},{385,257},{130,2},{2... | collective-permute-start | bytes 110600 | tf_op jit(solution)/shard_map/ppermute | solution.py:337
  35.6 2.4 %collective-permute-start.4 = (f32[3,24,128]{2,1,0:T(8,128)S(1)}, f32[3,24,128]{2,1,0:T(8,128)S(1)}, u32[]{:S(2)}, u32[]{:S(2)}) collective-permute-start(f32[3,24,128]{2,1,0:T(8,128)S(1)} %x_edges.1.own), channel_id=1, source_target_pairs={{0,128},{128,256},{256,384},{1,129},{129,257},{257,385},{2,130},{1... | collective-permute-start | bytes 110600 | tf_op jit(solution)/shard_map/ppermute | solution.py:336
  38.0 0.0 collective-permute-done.5.right
  38.0 3.4 %collective-permute-done.4.left = f32[3,24,128]{2,1,0:T(8,128)S(1)} collective-permute-done((f32[3,24,128]{2,1,0:T(8,128)S(1)}, f32[3,24,128]{2,1,0:T(8,128)S(1)}, u32[]{:S(2)}, u32[]{:S(2)}) %collective-permute-start.4) | collective-permute-done | bytes 36896 | tf_op jit(solution)/shard_map/ppermute | solution.py:336
  41.4 0.0 copy-done.1
  41.4 1.8 %both_steps.1 = (f32[3,4,16,128]{3,2,1,0:T(8,128)}, f32[3,4,16,128]{3,2,1,0:T(8,128)}, f32[3,4,16,128]{3,2,1,0:T(8,128)}, f32[3,4,16,128]{3,2,1,0:T(8,128)}) custom-call(s32[2]{0:T(128)S(1)} %pad_add_fusion.flags, f32[4,10,24,128]{3,2,1,0:T(8,128)S(1)} %get-tuple-element.11.wide, f32[16,24,128]{2,1,0:T(8,128)S(1)} %collective-permute-done.2.before, ...), custom_call_target="tpu_custom_call" | custom-call | flops 4000000 | bytes 1425416 | tf_op jit(solution)/shard_map/both_steps/pallas_call | solution.py:300
Async XLA Ops:
  0.6 0.9 %copy-start = (f32[3,4,16,128]{3,2,1,0:T(8,128)S(1)}, f32[3,4,16,128]{3,2,1,0:T(8,128)}, u32[]{:S(2)}) copy-start(f32[3,4,16,128]{3,2,1,0:T(8,128)} %polar.1) | copy-start | bytes 294916
  1.5 0.9 %copy-start.2 = (f32[3,4,16,128]{3,2,1,0:T(8,128)S(1)}, f32[3,4,16,128]{3,2,1,0:T(8,128)}, u32[]{:S(2)}) copy-start(f32[3,4,16,128]{3,2,1,0:T(8,128)} %e.3) | copy-start | bytes 294916
  2.4 0.9 %copy-start.3 = (f32[3,4,16,128]{3,2,1,0:T(8,128)S(1)}, f32[3,4,16,128]{3,2,1,0:T(8,128)}, u32[]{:S(2)}) copy-start(f32[3,4,16,128]{3,2,1,0:T(8,128)} %h.3) | copy-start | bytes 294916
  3.3 0.9 %copy-start.4 = (f32[3,4,16,128]{3,2,1,0:T(8,128)S(1)}, f32[3,4,16,128]{3,2,1,0:T(8,128)}, u32[]{:S(2)}) copy-start(f32[3,4,16,128]{3,2,1,0:T(8,128)} %j.3) | copy-start | bytes 294916
  4.2 0.8 %copy-start.5 = (s32[4,16,128]{2,1,0:T(8,128)S(1)}, s32[4,16,128]{2,1,0:T(8,128)}, u32[]{:S(2)}) copy-start(s32[4,16,128]{2,1,0:T(8,128)} %material.3) | copy-start | bytes 98308
  5.0 0.8 %copy-start.6 = (s32[4,16,128]{2,1,0:T(8,128)S(1)}, s32[4,16,128]{2,1,0:T(8,128)}, u32[]{:S(2)}) copy-start(s32[4,16,128]{2,1,0:T(8,128)} %pml.3) | copy-start | bytes 98308
  5.8 19.1 %collective-permute-start = (f32[64,128]{1,0:T(8,128)S(1)}, f32[64,128]{1,0:T(8,128)S(1)}, u32[]{:S(2)}, u32[]{:S(2)}) collective-permute-start(f32[64,128]{1,0:T(8,128)S(1)} %get-tuple-element.9), channel_id=1, source_target_pairs={{0,8},{8,16},{16,24},{24,32},{32,40},{40,48},{48,56},{56,64},{64,7... | collective-permute-start | bytes 98312 | tf_op jit(solution)/shard_map/ppermute | solution.py:323
  14.9 10.0 %collective-permute-start.1 = (f32[48,128]{1,0:T(8,128)S(1)}, f32[48,128]{1,0:T(8,128)S(1)}, u32[]{:S(2)}, u32[]{:S(2)}) collective-permute-start(f32[48,128]{1,0:T(8,128)S(1)} %get-tuple-element.10), channel_id=1, source_target_pairs={{8,0},{16,8},{24,16},{32,24},{40,32},{48,40},{56,48},{64,56},{72,6... | collective-permute-start | bytes 73736 | tf_op jit(solution)/shard_map/ppermute | solution.py:324
  25.0 6.3 %collective-permute-start.2 = (f32[16,24,128]{2,1,0:T(8,128)S(1)}, f32[16,24,128]{2,1,0:T(8,128)S(1)}, u32[]{:S(2)}, u32[]{:S(2)}) collective-permute-start(f32[16,24,128]{2,1,0:T(8,128)S(1)} %get-tuple-element.12), channel_id=1, source_target_pairs={{0,1},{1,2},{2,3},{3,4},{4,5},{5,6},{6,7},{7,0},{8,9},{9,10},{10,1... | collective-permute-start | bytes 589832 | tf_op jit(solution)/shard_map/ppermute | solution.py:332
  25.0 5.5 %collective-permute-start.3 = (f32[11,24,128]{2,1,0:T(8,128)S(1)}, f32[11,24,128]{2,1,0:T(8,128)S(1)}, u32[]{:S(2)}, u32[]{:S(2)}) collective-permute-start(f32[11,24,128]{2,1,0:T(8,128)S(1)} %get-tuple-element.13), channel_id=1, source_target_pairs={{1,0},{2,1},{3,2},{4,3},{5,4},{6,5},{7,6},{0,7},{9,8},{10,9},{11,1... | collective-permute-start | bytes 405512 | tf_op jit(solution)/shard_map/ppermute | solution.py:333
  31.3 10.1 %copy-start.1 = (f32[3,4,16,128]{3,2,1,0:T(8,128)S(1)}, f32[3,4,16,128]{3,2,1,0:T(8,128)}, u32[]{:S(2)}) copy-start(f32[3,4,16,128]{3,2,1,0:T(8,128)} %polar.1) | copy-start | bytes 294916
  32.1 5.9 %collective-permute-start.5 = (f32[3,24,128]{2,1,0:T(8,128)S(1)}, f32[3,24,128]{2,1,0:T(8,128)S(1)}, u32[]{:S(2)}, u32[]{:S(2)}) collective-permute-start(f32[3,24,128]{2,1,0:T(8,128)S(1)} %x_edges.1.own), channel_id=1, source_target_pairs={{128,0},{256,128},{384,256},{129,1},{257,129},{385,257},{130,2},{2... | collective-permute-start | bytes 110600 | tf_op jit(solution)/shard_map/ppermute | solution.py:337
  35.6 5.9 %collective-permute-start.4 = (f32[3,24,128]{2,1,0:T(8,128)S(1)}, f32[3,24,128]{2,1,0:T(8,128)S(1)}, u32[]{:S(2)}, u32[]{:S(2)}) collective-permute-start(f32[3,24,128]{2,1,0:T(8,128)S(1)} %x_edges.1.own), channel_id=1, source_target_pairs={{0,128},{128,256},{256,384},{1,129},{129,257},{257,385},{2,130},{1... | collective-permute-start | bytes 110600 | tf_op jit(solution)/shard_map/ppermute | solution.py:336

commit v3 on v2

--- a/solution.py
+++ b/solution.py
@@ -1,5 +1,3 @@
-import functools
-
 import jax
 import jax.numpy as jnp
 from jax import lax
@@ -28,6 +26,7 @@
 ROWS = 24
 PLANES = range(-2, 6)
 SPAN = 32
+HINT = 1 << 26
 
 
 def up_of(n):
@@ -42,23 +41,40 @@
     return (1 + 4 * material + pml).astype(jnp.float32)
 
 
-def y_faces(e, h, p, j, material, pml, up, down):
-    def face(c, row):
-        if c < HX:
-            return e[c, :, row, :]
-        if c < QX:
-            return h[c - HX, :, row, :]
-        if c < CODE:
-            return HOLD * j[c - QX, :, row, :] - PULL * p[c - QX, :, row, :]
-        return code_of(material[:, row, :], pml[:, row, :])
-
+def y_face(cells, c, row):
+    e, h, p, j, material, pml = cells
+    if c < HX:
+        return e[c, :, row, :]
+    if c < QX:
+        return h[c - HX, :, row, :]
+    if c < CODE:
+        return HOLD * j[c - QX, :, row, :] - PULL * p[c - QX, :, row, :]
+    return code_of(material[:, row, :], pml[:, row, :])
+
+
+def load_and_low_faces(*refs):
+    far, near, down, done = refs[:6], refs[6:12], refs[12], refs[13]
+    copies = [pltpu.make_async_copy(a, b, done.at[i]) for i, (a, b) in enumerate(zip(far, near))]
+    for copy in copies:
+        copy.start()
+    for copy in copies:
+        copy.wait()
     down[...] = jnp.zeros_like(down)
-    for ref, faces in ((up, Y_UP), (down, Y_DOWN)):
-        for i, (c, row) in enumerate(faces):
-            ref[4 * i : 4 * i + 4, :] = face(c, row)
-
-
-def z_faces(e, h, p, j, material, pml, before, after, wide, up, down):
+    for i, (c, row) in enumerate(Y_DOWN):
+        down[4 * i : 4 * i + 4, :] = y_face(near, c, row)
+
+
+def high_faces(*refs):
+    near, _, up = refs[:6], refs[6], refs[7]
+    for i, (c, row) in enumerate(Y_UP):
+        up[4 * i : 4 * i + 4, :] = y_face(near, c, row)
+
+
+def again(down, _, copy):
+    copy[...] = down[0:48, :]
+
+
+def z_faces(e, h, p, j, material, pml, before, after, later, wide, up, down):
     for z in range(4):
         for c in EVERY:
             if c < HX:
@@ -74,7 +90,8 @@
         for i, (c, row) in enumerate(Y_UP):
             wide[z, c, row + 8 : row + 9, :] = before[4 * i + z : 4 * i + z + 1, :]
         for i, (c, row) in enumerate(Y_DOWN):
-            wide[z, c, row + 16 : row + 17, :] = after[4 * i + z : 4 * i + z + 1, :]
+            at = slice(4 * i + z, 4 * i + z + 1)
+            wide[z, c, row + 16 : row + 17, :] = after[at, :] + later[at, :]
     for i, (c, z) in enumerate(Z_UP):
         up[i] = wide[z, c]
     for i, (c, z) in enumerate(Z_DOWN):
@@ -293,14 +310,15 @@
 
 VMEM = pl.BlockSpec(memory_space=pltpu.VMEM)
 SMEM = pl.BlockSpec(memory_space=pltpu.SMEM)
-
-
-def call(kernel, outs, args, scratch=(), flops=0, name=None):
-    size = sum(a.size for a in args) + sum(o.size for o in outs)
+HBM = pl.BlockSpec(memory_space=pltpu.HBM)
+
+
+def call(kernel, outs, args, scratch=(), flops=0, size=0, far=False, name=None):
+    size = size or sum(a.size for a in args) + sum(o.size for o in outs)
     return pl.pallas_call(
         kernel,
         out_shape=outs,
-        in_specs=[SMEM if a.ndim == 1 else VMEM for a in args],
+        in_specs=[HBM if far else SMEM if a.ndim == 1 else VMEM for a in args],
         out_specs=[VMEM] * len(outs),
         scratch_shapes=list(scratch),
         cost_estimate=pl.CostEstimate(flops=flops, bytes_accessed=4 * size, transcendentals=0),
@@ -319,14 +337,28 @@
     place = lax.axis_index("gz")
     flags = jnp.stack([place, gz - 1 - place]).astype(jnp.int32)
 
-    up, down = call(y_faces, [f32(64, 128), f32(48, 128)], cells, name="y_faces")
+    shapes = [jax.ShapeDtypeStruct(a.shape, a.dtype) for a in cells]
+    cells = [pltpu.with_memory_space_constraint(a, pltpu.HBM) for a in cells]
+    *cells, down = call(
+        load_and_low_faces,
+        [*shapes, f32(72, 128)],
+        cells,
+        scratch=[pltpu.SemaphoreType.DMA((6,))],
+        far=True,
+        name="load_and_low_faces",
+    )
+    near = [(i, j) for i, j in down_of(gy) if i % 4 in (1, 2)]
+    rest = [(i, j) for i, j in down_of(gy) if i % 4 in (0, 3)]
+    after = lax.ppermute(down, "gy", near)
+    (up,) = call(high_faces, [f32(64, 128)], (*cells, down), size=HINT, name="high_faces")
     before = lax.ppermute(up, "gy", up_of(gy))
-    after = lax.ppermute(down, "gy", down_of(gy))
+    (down,) = call(again, [f32(48, 128)], (down, up), size=HINT, name="again")
+    later = lax.ppermute(down, "gy", rest)
 
     wide, up, down = call(
         z_faces,
         [f32(4, 10, ROWS, 128), f32(16, ROWS, 128), f32(11, ROWS, 128)],
-        (*cells, before, after),
+        (*cells, before, after, later),
         name="z_faces",
     )
     before = lax.ppermute(up, "gz", [(i, (i + 1) % gz) for i in range(gz)])

time: 43.7 us -> 37 us (0.85)
  the two profiles are of different devices: /device:TPU:38 before, /device:TPU:6 now
where the time goes in v3:
time: 37 us; the launch traced here: 36.8 us
  starting transfers between devices  22.8 us (62%)
  waiting for transfers between devices  9.33 us (25%)
  Pallas kernels  3.87 us (10%)
  between operations  0.72 us (2%)
    ppermute x1, starting transfers between devices, on_device(): before = lax.ppermute(up, 'gy', up_of(gy))  9.73 us
    ppermute x1, starting transfers between devices, on_device(): later = lax.ppermute(down, 'gy', rest)  4.56 us
    ppermute x1, waiting for transfers between devices, on_device(): right = lax.ppermute(own, 'gx', down_of(gx))  4.24 us
    pallas_call x6, Pallas kernels, call(): pl.pallas_call(kernel, out_shape=outs, in_specs=[HBM if far else SMEM if...  3.87 us
    ppermute x1, starting transfers between devices, on_device(): after = lax.ppermute(down, 'gz', [((i + 1) % gz, i) for i in range(gz)])  2.94 us
    ppermute x1, starting transfers between devices, on_device(): left = lax.ppermute(own, 'gx', up_of(gx))  2.92 us
    ppermute x1, waiting for transfers between devices, on_device(): after = lax.ppermute(down, 'gz', [((i + 1) % gz, i) for i in range(gz)])  2.48 us
    ppermute x1, waiting for transfers between devices, on_device(): later = lax.ppermute(down, 'gy', rest)  1.5 us
  transfers between devices with their start and end apart: 7, of which 5 were waited for; matrix products, arithmetic and copies ran while one was open for 0% of the time, Pallas kernels for 0%

profile of v3, /device:TPU:6, one launch (start us, length us, event | category | flops | bytes accessed | tf_op | source)
XLA Modules:
  0.0 36.8 jit_solution(6125135772606478880)
XLA Ops:
  0.6 1.1 %load_and_low_faces.1 = (f32[3,4,16,128]{3,2,1,0:T(8,128)S(1)}, f32[3,4,16,128]{3,2,1,0:T(8,128)S(1)}, f32[3,4,16,128]{3,2,1,0:T(8,128)S(1)}, f32[3,4,16,128]{3,...) custom-call(f32[3,4,16,128]{3,2,1,0:T(8,128)} %refs_0_.1, ...), custom_call_target="tpu_custom_call" | custom-call | bytes 954368 | tf_op jit(solution)/shard_map/load_and_low_faces/pallas_call | solution.py:318
  1.8 1.3 %collective-permute-start.1 = (f32[72,128]{1,0:T(8,128)S(1)}, f32[72,128]{1,0:T(8,128)S(1)}, u32[]{:S(2)}, u32[]{:S(2)}) collective-permute-start(f32[72,128]{1,0:T(8,128)S(1)} %get-tuple-element.20.refs_6_.down), channel_id=1, source_target_pairs={{8,0},{16,8},{40,32},{48,40},{72,64},{80,72},{104,96},{112,104},{9... | collective-permute-start | bytes 110600 | tf_op jit(solution)/shard_map/ppermute | solution.py:352
  3.1 9.7 %collective-permute-start = (f32[64,128]{1,0:T(8,128)S(1)}, f32[64,128]{1,0:T(8,128)S(1)}, u32[]{:S(2)}, u32[]{:S(2)}) collective-permute-start(f32[64,128]{1,0:T(8,128)S(1)} %high_faces.1._), channel_id=1, source_target_pairs={{0,8},{8,16},{16,24},{24,32},{32,40},{40,48},{48,56},{56,64},{64,7... | collective-permute-start | bytes 98312 | tf_op jit(solution)/shard_map/ppermute | solution.py:354
  12.8 4.6 %collective-permute-start.2 = (f32[48,128]{1,0:T(8,128)S(1)}, f32[48,128]{1,0:T(8,128)S(1)}, u32[]{:S(2)}, u32[]{:S(2)}) collective-permute-start(f32[48,128]{1,0:T(8,128)S(1)} %again.1), channel_id=1, source_target_pairs={{24,16},{32,24},{56,48},{64,56},{88,80},{96,88},{120,112},{25,17},... | collective-permute-start | bytes 73736 | tf_op jit(solution)/shard_map/ppermute | solution.py:356
  17.4 1.5 %collective-permute-done.2.later = f32[48,128]{1,0:T(8,128)S(1)} collective-permute-done((f32[48,128]{1,0:T(8,128)S(1)}, f32[48,128]{1,0:T(8,128)S(1)}, u32[]{:S(2)}, u32[]{:S(2)}) %collective-permute-start.2) | collective-permute-done | bytes 24608 | tf_op jit(solution)/shard_map/ppermute | solution.py:356
  18.9 0.0 collective-permute-done.before
  18.9 0.0 collective-permute-done.1.after
  18.9 0.1 z_faces.1
  19.0 0.0 collective-permute-start.3
  19.1 2.9 %collective-permute-start.4 = (f32[11,24,128]{2,1,0:T(8,128)S(1)}, f32[11,24,128]{2,1,0:T(8,128)S(1)}, u32[]{:S(2)}, u32[]{:S(2)}) collective-permute-start(f32[11,24,128]{2,1,0:T(8,128)S(1)} %get-tuple-element.23), channel_id=1, source_target_pairs={{1,0},{2,1},{3,2},{4,3},{5,4},{6,5},{7,6},{0,7},{9,8},{10,9},{11,1... | collective-permute-start | bytes 405512 | tf_op jit(solution)/shard_map/ppermute | solution.py:365
  22.0 0.1 pad_add_fusion.flags
  22.1 2.5 %collective-permute-done.4.after = f32[11,24,128]{2,1,0:T(8,128)S(1)} collective-permute-done((f32[11,24,128]{2,1,0:T(8,128)S(1)}, f32[11,24,128]{2,1,0:T(8,128)S(1)}, u32[]{:S(2)}, u32[]{:S(2)}) %collective-permute-start.4) | collective-permute-done | bytes 135200 | tf_op jit(solution)/shard_map/ppermute | solution.py:365
  24.6 0.8 %collective-permute-done.3.before = f32[16,24,128]{2,1,0:T(8,128)S(1)} collective-permute-done((f32[16,24,128]{2,1,0:T(8,128)S(1)}, f32[16,24,128]{2,1,0:T(8,128)S(1)}, u32[]{:S(2)}, u32[]{:S(2)}) %collective-permute-start.3) | collective-permute-done | bytes 196640 | tf_op jit(solution)/shard_map/ppermute | solution.py:364
  25.4 0.0 copy-start
  25.4 0.8 %x_edges.1.own = f32[3,24,128]{2,1,0:T(8,128)S(1)} custom-call(s32[2]{0:T(128)S(1)} %pad_add_fusion.flags, f32[4,10,24,128]{3,2,1,0:T(8,128)S(1)} %get-tuple-element.21.wide, f32[16,24,128]{2,1,0:T(8,128)S(1)} %collective-permute-done.3.before, f32[11,24,128]{2,1,0:T(8,128)S(1)} %collective-permute-done.4.after), custom_call_target="tpu_custom_call" | custom-call | bytes 860168 | tf_op jit(solution)/shard_map/x_edges/pallas_call | solution.py:318
  26.2 2.9 %collective-permute-start.5 = (f32[3,24,128]{2,1,0:T(8,128)S(1)}, f32[3,24,128]{2,1,0:T(8,128)S(1)}, u32[]{:S(2)}, u32[]{:S(2)}) collective-permute-start(f32[3,24,128]{2,1,0:T(8,128)S(1)} %x_edges.1.own), channel_id=1, source_target_pairs={{0,128},{128,256},{256,384},{1,129},{129,257},{257,385},{2,130},{1... | collective-permute-start | bytes 110600 | tf_op jit(solution)/shard_map/ppermute | solution.py:368
  29.1 1.3 %collective-permute-start.6 = (f32[3,24,128]{2,1,0:T(8,128)S(1)}, f32[3,24,128]{2,1,0:T(8,128)S(1)}, u32[]{:S(2)}, u32[]{:S(2)}) collective-permute-start(f32[3,24,128]{2,1,0:T(8,128)S(1)} %x_edges.1.own), channel_id=1, source_target_pairs={{128,0},{256,128},{384,256},{129,1},{257,129},{385,257},{130,2},{2... | collective-permute-start | bytes 110600 | tf_op jit(solution)/shard_map/ppermute | solution.py:369
  30.4 0.3 collective-permute-done.5.left
  30.7 4.2 %collective-permute-done.6.right = f32[3,24,128]{2,1,0:T(8,128)S(1)} collective-permute-done((f32[3,24,128]{2,1,0:T(8,128)S(1)}, f32[3,24,128]{2,1,0:T(8,128)S(1)}, u32[]{:S(2)}, u32[]{:S(2)}) %collective-permute-start.6) | collective-permute-done | bytes 36896 | tf_op jit(solution)/shard_map/ppermute | solution.py:369
  35.0 0.0 copy-done
  35.0 1.8 %both_steps.1 = (f32[3,4,16,128]{3,2,1,0:T(8,128)}, f32[3,4,16,128]{3,2,1,0:T(8,128)}, f32[3,4,16,128]{3,2,1,0:T(8,128)}, f32[3,4,16,128]{3,2,1,0:T(8,128)}) custom-call(s32[2]{0:T(128)S(1)} %pad_add_fusion.flags, f32[4,10,24,128]{3,2,1,0:T(8,128)S(1)} %get-tuple-element.21.wide, f32[16,24,128]{2,1,0:T(8,128)S(1)} %collective-permute-done.3.before, ...), custom_call_target="tpu_custom_call" | custom-call | flops 4000000 | bytes 1425416 | tf_op jit(solution)/shard_map/both_steps/pallas_call | solution.py:318
  (2 shorter events, 0.0 us)
Async XLA Ops:
  1.8 17.2 %collective-permute-start.1 = (f32[72,128]{1,0:T(8,128)S(1)}, f32[72,128]{1,0:T(8,128)S(1)}, u32[]{:S(2)}, u32[]{:S(2)}) collective-permute-start(f32[72,128]{1,0:T(8,128)S(1)} %get-tuple-element.20.refs_6_.down), channel_id=1, source_target_pairs={{8,0},{16,8},{40,32},{48,40},{72,64},{80,72},{104,96},{112,104},{9... | collective-permute-start | bytes 110600 | tf_op jit(solution)/shard_map/ppermute | solution.py:352
  3.1 15.8 %collective-permute-start = (f32[64,128]{1,0:T(8,128)S(1)}, f32[64,128]{1,0:T(8,128)S(1)}, u32[]{:S(2)}, u32[]{:S(2)}) collective-permute-start(f32[64,128]{1,0:T(8,128)S(1)} %high_faces.1._), channel_id=1, source_target_pairs={{0,8},{8,16},{16,24},{24,32},{32,40},{40,48},{48,56},{56,64},{64,7... | collective-permute-start | bytes 98312 | tf_op jit(solution)/shard_map/ppermute | solution.py:354
  12.8 6.1 %collective-permute-start.2 = (f32[48,128]{1,0:T(8,128)S(1)}, f32[48,128]{1,0:T(8,128)S(1)}, u32[]{:S(2)}, u32[]{:S(2)}) collective-permute-start(f32[48,128]{1,0:T(8,128)S(1)} %again.1), channel_id=1, source_target_pairs={{24,16},{32,24},{56,48},{64,56},{88,80},{96,88},{120,112},{25,17},... | collective-permute-start | bytes 73736 | tf_op jit(solution)/shard_map/ppermute | solution.py:356
  19.0 6.3 %collective-permute-start.3 = (f32[16,24,128]{2,1,0:T(8,128)S(1)}, f32[16,24,128]{2,1,0:T(8,128)S(1)}, u32[]{:S(2)}, u32[]{:S(2)}) collective-permute-start(f32[16,24,128]{2,1,0:T(8,128)S(1)} %get-tuple-element.22), channel_id=1, source_target_pairs={{0,1},{1,2},{2,3},{3,4},{4,5},{5,6},{6,7},{7,0},{8,9},{9,10},{10,1... | collective-permute-start | bytes 589832 | tf_op jit(solution)/shard_map/ppermute | solution.py:364
  19.1 5.5 %collective-permute-start.4 = (f32[11,24,128]{2,1,0:T(8,128)S(1)}, f32[11,24,128]{2,1,0:T(8,128)S(1)}, u32[]{:S(2)}, u32[]{:S(2)}) collective-permute-start(f32[11,24,128]{2,1,0:T(8,128)S(1)} %get-tuple-element.23), channel_id=1, source_target_pairs={{1,0},{2,1},{3,2},{4,3},{5,4},{6,5},{7,6},{0,7},{9,8},{10,9},{11,1... | collective-permute-start | bytes 405512 | tf_op jit(solution)/shard_map/ppermute | solution.py:365
  25.4 9.6 %copy-start = (f32[3,4,16,128]{3,2,1,0:T(8,128)S(1)}, f32[3,4,16,128]{3,2,1,0:T(8,128)}, u32[]{:S(2)}) copy-start(f32[3,4,16,128]{3,2,1,0:T(8,128)} %polar.1) | copy-start | bytes 294916
  26.2 4.5 %collective-permute-start.5 = (f32[3,24,128]{2,1,0:T(8,128)S(1)}, f32[3,24,128]{2,1,0:T(8,128)S(1)}, u32[]{:S(2)}, u32[]{:S(2)}) collective-permute-start(f32[3,24,128]{2,1,0:T(8,128)S(1)} %x_edges.1.own), channel_id=1, source_target_pairs={{0,128},{128,256},{256,384},{1,129},{129,257},{257,385},{2,130},{1... | collective-permute-start | bytes 110600 | tf_op jit(solution)/shard_map/ppermute | solution.py:368
  29.1 5.9 %collective-permute-start.6 = (f32[3,24,128]{2,1,0:T(8,128)S(1)}, f32[3,24,128]{2,1,0:T(8,128)S(1)}, u32[]{:S(2)}, u32[]{:S(2)}) collective-permute-start(f32[3,24,128]{2,1,0:T(8,128)S(1)} %x_edges.1.own), channel_id=1, source_target_pairs={{128,0},{256,128},{384,256},{129,1},{257,129},{385,257},{130,2},{2... | collective-permute-start | bytes 110600 | tf_op jit(solution)/shard_map/ppermute | solution.py:369

commit v4 on v3

v4 whole, which is shorter than its diff:
```python
import jax
import jax.numpy as jnp
from jax import lax
from jax.experimental import pallas as pl
from jax.experimental.pallas import tpu as pltpu
from jax.sharding import PartitionSpec as P

time_step = 0.5
damping = 0.2
omega_sq = 1.0
strength = 3.0

DECAY = 1.0 + 0.5 * damping * time_step
HOLD = (1.0 - 0.5 * damping * time_step) / DECAY
PULL = time_step * omega_sq / DECAY
GAIN = PULL * strength

EX, EY, EZ, HX, HY, HZ, QX, QY, QZ, CODE = range(10)
EVERY = tuple(range(10))

Y_UP = [(c, 14) for c in (EX, EY, EZ, HX, HZ, CODE)] + [(c, 15) for c in EVERY]
Y_DOWN = [(c, 0) for c in (EX, EY, EZ, HX, HY, HZ, QX, QZ, CODE)] + [(EX, 1), (EZ, 1)]
Z_UP = [(c, 2) for c in (EX, EY, EZ, HX, HY, CODE)] + [(c, 3) for c in EVERY]
Z_DOWN = [(c, 0) for c in (EX, EY, EZ, HX, HY, HZ, QX, QY, CODE)] + [(EX, 1), (EY, 1)]

ROWS = 24
PLANES = range(-2, 6)
SPAN = 32
HINT = 1 << 26


def up_of(n):
    return [(i, i + 1) for i in range(n - 1)]


def down_of(n):
    return [(i + 1, i) for i in range(n - 1)]


def code_of(material, pml):
    return (1 + 4 * material + pml).astype(jnp.float32)


def y_face(cells, c, row):
    e, h, p, j, material, pml = cells
    if c < HX:
        return e[c, :, row, :]
    if c < QX:
        return h[c - HX, :, row, :]
    if c < CODE:
        return HOLD * j[c - QX, :, row, :] - PULL * p[c - QX, :, row, :]
    return code_of(material[:, row, :], pml[:, row, :])


def load_and_low_faces(*refs):
    far, near, down, done = refs[:6], refs[6:12], refs[12], refs[13]
    copies = [pltpu.make_async_copy(a, b, done.at[i]) for i, (a, b) in enumerate(zip(far, near))]
    for copy in copies:
        copy.start()
    for copy in copies:
        copy.wait()
    down[...] = jnp.zeros_like(down)
    for i, (c, row) in enumerate(Y_DOWN):
        down[4 * i : 4 * i + 4, :] = y_face(near, c, row)


def high_faces(*refs):
    near, _, up = refs[:6], refs[6], refs[7]
    for i, (c, row) in enumerate(Y_UP):
        up[4 * i : 4 * i + 4, :] = y_face(near, c, row)


def again(down, _, copy):
    copy[...] = down[0:48, :]


def widen_rows(e, h, p, j, material, pml, before, after, later, wide, edges):
    lane = lanes()
    for z in range(4):
        for c in EVERY:
            if c < HX:
                own = e[c, z]
            elif c < QX:
                own = h[c - HX, z]
            elif c < CODE:
                own = HOLD * j[c - QX, z] - PULL * p[c - QX, z]
            else:
                own = code_of(material[z], pml[z])
            wide[z, c, 0:16, :] = own
            wide[z, c, 16:24, :] = jnp.zeros((8, 128), jnp.float32)
        for i, (c, row) in enumerate(Y_UP):
            wide[z, c, row + 8 : row + 9, :] = before[4 * i + z : 4 * i + z + 1, :]
        for i, (c, row) in enumerate(Y_DOWN):
            at = slice(4 * i + z, 4 * i + z + 1)
            wide[z, c, row + 16 : row + 17, :] = after[at, :] + later[at, :]
    for g in range(3):
        total = jnp.zeros((ROWS, 128), jnp.float32)
        for c in range(4 * g, min(4 * g + 4, 10)):
            for z in range(4):
                at = SPAN * (c - 4 * g) + 4 * (z + 2)
                moved = roll(wide[z, c], at - 126, 1)
                total = jnp.where((lane >= at) & (lane < at + 4), moved, total)
        edges[g] = total


def z_faces(wide, _, up, down):
    for i, (c, z) in enumerate(Z_UP):
        up[i] = wide[z, c]
    for i, (c, z) in enumerate(Z_DOWN):
        down[i] = wide[z, c]


def sides(own, left, right, g):
    near = (lanes() % 4) < 2
    return jnp.where(near, left[g], own[g]), jnp.where(near, own[g], right[g])


def columns_on(own, left, right, out):
    part = (lanes() % SPAN) // 8
    for g in range(3):
        low, high = sides(own, left, right, g)
        up = jnp.where(part == 0, roll(low, -16, 1), roll(high, -8, 1))
        down = jnp.where(part == 2, roll(high, 8, 1), roll(low, 16, 1))
        out[g] = jnp.where(part < 2, up, down)


def grid_ends():
    place = lax.axis_index("gz")
    return place == 0, place == lax.axis_size("gz") - 1


def planes_of(wide, before, after):
    first, last = grid_ends()

    def plane(c, z):
        if 0 <= z < 4:
            return wide[z, c]
        if z < 0:
            if (c, z + 4) not in Z_UP:
                return None
            got = before[Z_UP.index((c, z + 4))]
            return jnp.where(first, 0.0, got)
        if (c, z - 4) not in Z_DOWN:
            return None
        got = after[Z_DOWN.index((c, z - 4))]
        return jnp.where(last, 0.0, got)

    return plane


def lanes():
    return lax.broadcasted_iota(jnp.int32, (ROWS, 128), 1)


def roll(array, shift, axis):
    shift = shift % array.shape[axis]
    return pltpu.roll(array, shift, axis) if shift else array


def factors(code):
    metal = code > 8.5
    dielec = (code > 4.5) & (code < 8.5)
    inside = code > 0.5
    level = code - jnp.where(metal, 9.0, jnp.where(dielec, 5.0, 1.0))
    loss = jnp.where(level > 2.5, 0.25, jnp.where(level > 1.5, 0.1, jnp.where(level > 0.5, 0.025, 0.0)))
    permit = jnp.where(metal, 1.5, jnp.where(dielec, 2.25, 1.0))
    over_h = jnp.where(inside, 1.0 / (1.0 + loss), 0.0)
    over_e = jnp.where(inside, 1.0 / (permit + loss), 0.0)
    return (
        (1.0 - loss) * over_h,
        time_step * over_h,
        (permit - loss) * over_e,
        time_step * over_e,
        jnp.where(metal, 1.0, 0.0),
    )


def magnetic_new(h, e, ey, ez, ex, keep, push):
    curl = (
        (ey[2] - e[2]) - (ez[1] - e[1]),
        (ez[0] - e[0]) - (ex[2] - e[2]),
        (ex[1] - e[1]) - (ey[0] - e[0]),
    )
    return [None if h[k] is None else keep * h[k] - push * curl[k] for k in range(3)]


def electric_new(e, h, hy, hz, hx, drag, keep, push):
    curl = (
        (h[2] - hy[2]) - (h[1] - hz[1]),
        (h[0] - hz[0]) - (h[2] - hx[2]),
        (h[1] - hx[1]) - (h[0] - hy[0]),
    )
    return [keep * e[k] + push * (curl[k] - drag[k]) for k in range(3)]


x_next = lambda a: roll(a, -1, 1)
x_back = lambda a: roll(a, 1, 1)
y_next = lambda a: roll(a, -1, 0)
y_back = lambda a: roll(a, 1, 0)


def first_step(wide, before, after, polar, h1, e1, p1, j1, fh, fe):
    plane = planes_of(wide, before, after)
    for z in range(-2, 5):
        e = [plane(EX + k, z) for k in range(3)]
        up = [plane(EX + k, z + 1) for k in range(2)]
        h = [plane(HX + k, z) for k in range(3)]
        keep_h, push_h, keep_e, push_e, metal = factors(plane(CODE, z))
        new = magnetic_new(
            h,
            e,
            {0: y_next(e[0]), 2: y_next(e[2])},
            {0: up[0], 1: up[1]},
            {1: x_next(e[1]), 2: x_next(e[2])},
            keep_h,
            push_h,
        )
        for k in range(3):
            if new[k] is not None:
                h1[z + 2, k] = new[k]
        if -1 <= z < 4:
            fh[z + 1, 0] = keep_h
            fh[z + 1, 1] = push_h
        if 0 <= z < 4:
            for k, f in enumerate((keep_e, push_e, metal)):
                fe[z, k] = f[0:16]
        if z == -2:
            continue
        h = new
        down = [h1[z + 1, k] for k in range(2)]
        held = [plane(QX + k, z) for k in range(3)]
        flow = [None if held[k] is None else held[k] + GAIN * metal * e[k] for k in range(3)]
        if 0 <= z < 4:
            for k in range(3):
                j1[k, z] = flow[k][0:16]
                p1[k, z] = polar[k, z] + time_step * flow[k][0:16]
        new = electric_new(
            e,
            h,
            {0: y_back(h[0]), 2: y_back(h[2])},
            {0: down[0], 1: down[1]},
            {1: x_back(h[1]), 2: x_back(h[2])},
            [0.0 if flow[k] is None else metal * flow[k] for k in range(3)],
            keep_e,
            push_e,
        )
        for k in range(3):
            e1[z + 1, k] = new[k]


def columns(own, left, right, before, after):
    first, last = grid_ends()
    lane = lanes()
    part = (lane % SPAN) // 8
    values = []
    for g in range(3):
        low, high = sides(own, left, right, g)
        up = jnp.where(first, 0.0, before[g])
        down = jnp.where(last, 0.0, after[g])
        low = jnp.where(part == 0, up, jnp.where(part == 3, down, low))
        high = jnp.where(part == 0, roll(up, -8, 1), jnp.where(part == 3, roll(down, 8, 1), high))
        for k in range(4):
            values.append(jnp.where(lane < SPAN, roll(low, -SPAN * k, 1), roll(high, SPAN - SPAN * k, 1)))
    z_next = lambda a: roll(a, -4, 1)
    z_back = lambda a: roll(a, 4, 1)

    def shifted(f, y, z, x):
        return {0: y(f[0]), 2: y(f[2])}, {0: z(f[0]), 1: z(f[1])}, {1: x(f[1]), 2: x(f[2])}

    keep_h, push_h, keep_e, push_e, metal = factors(values[CODE])
    e0 = values[EX : EZ + 1]
    h1 = magnetic_new(values[HX : HZ + 1], e0, *shifted(e0, y_next, z_next, x_next), keep_h, push_h)
    drag = [metal * (values[QX + k] + GAIN * e0[k]) for k in range(3)]
    e1 = electric_new(e0, h1, *shifted(h1, y_back, z_back, x_back), drag, keep_e, push_e)
    h2 = magnetic_new(h1, e1, *shifted(e1, y_next, z_next, x_next), keep_h, push_h)
    return h1, e1, h2


def second_step(own, left, right, before, after, h1, e1, p1, j1, fh, fe, *rest):
    outs, near, h2, done = rest[:4], rest[4:8], rest[8], rest[9]
    e_near, h_near, p_near, j_near = near
    lane = lanes()
    ch1, ce1, ch2 = columns(own, left, right, before, after)

    def at_ends(column):
        return jnp.where(lane % 4 == 1, roll(column, -SPAN, 1), column)

    def put_right(array, z, column):
        return jnp.where((lane == 0) | (lane == 127), roll(column, 127 - (4 * (z + 2) + 1), 1), array)

    ends_h = [at_ends(a) for a in ch1]
    ends_e = [at_ends(a) for a in ce1]

    def after_x(array, z):
        return lambda k: jnp.where(lane == 127, roll(ce1[k], 127 - (SPAN + 4 * (z + 2) + 2), 1), x_next(array[k]))

    def before_x(array, z):
        return lambda k: jnp.where(lane == 0, roll(ch2[k], -(4 * (z + 2) + 1), 1), x_back(array[k]))

    def fixed_e(z):
        return [put_right(e1[z + 1, k], z, ends_e[k]) for k in range(3)]

    copies = [pltpu.make_async_copy(a, b, done.at[i]) for i, (a, b) in enumerate(zip(near, outs))]
    for z in range(4):
        metal = fe[z, 2]
        for k in range(3):
            e = put_right(e1[z + 1, k], z, ends_e[k])[0:16]
            flow = HOLD * j1[k, z] - PULL * p1[k, z] + GAIN * metal * e
            j_near[k, z] = flow
            p_near[k, z] = p1[k, z] + time_step * flow
    copies[2].start()
    copies[3].start()
    e = fixed_e(-1)
    for z in range(-1, 4):
        up = fixed_e(z + 1)
        h = [h1[z + 2, 0]] + [put_right(h1[z + 2, k], z, ends_h[k]) for k in (1, 2)]
        x = after_x(e, z)
        new = magnetic_new(
            h,
            e,
            {0: y_next(e[0]), 2: y_next(e[2])},
            {0: up[0], 1: up[1]},
            {1: x(1), 2: x(2)},
            fh[z + 1, 0],
            fh[z + 1, 1],
        )
        for k in range(3):
            h2[z + 1, k] = new[k]
            if z >= 0:
                h_near[k, z] = new[k][0:16]
        e = up
    copies[1].start()
    for z in range(4):
        h = [h2[z + 1, k] for k in range(3)]
        down = [h2[z, k] for k in range(2)]
        x = before_x(h, z)
        new = electric_new(
            [a[0:16] for a in fixed_e(z)],
            [a[0:16] for a in h],
            {0: y_back(h[0])[0:16], 2: y_back(h[2])[0:16]},
            {0: down[0][0:16], 1: down[1][0:16]},
            {1: x(1)[0:16], 2: x(2)[0:16]},
            [fe[z, 2] * j_near[k, z] for k in range(3)],
            fe[z, 0],
            fe[z, 1],
        )
        for k in range(3):
            e_near[k, z] = new[k]
    copies[0].start()
    for copy in copies:
        copy.wait()


VMEM = pl.BlockSpec(memory_space=pltpu.VMEM)
HBM = pl.BlockSpec(memory_space=pltpu.HBM)


def call(kernel, outs, args, scratch=(), flops=0, size=0, far=False, far_out=False, name=None):
    size = size or sum(a.size for a in args) + sum(o.size for o in outs)
    return pl.pallas_call(
        kernel,
        out_shape=outs,
        in_specs=[HBM if far else VMEM] * len(args),
        out_specs=[HBM if far_out else VMEM] * len(outs),
        scratch_shapes=list(scratch),
        cost_estimate=pl.CostEstimate(flops=flops, bytes_accessed=4 * size, transcendentals=0),
        compiler_params=pltpu.CompilerParams(vmem_limit_bytes=16 * 2**20),
        name=name,
    )(*args)


def f32(*shape):
    return jax.ShapeDtypeStruct(shape, jnp.float32)


def on_device(electric, magnetic, polar, current, material, pml):
    cells = (electric, magnetic, polar, current, material, pml)
    gx, gy, gz = (lax.axis_size(a) for a in ("gx", "gy", "gz"))
    shapes = [jax.ShapeDtypeStruct(a.shape, a.dtype) for a in cells]
    cells = [pltpu.with_memory_space_constraint(a, pltpu.HBM) for a in cells]
    *cells, down = call(
        load_and_low_faces,
        [*shapes, f32(72, 128)],
        cells,
        scratch=[pltpu.SemaphoreType.DMA((6,))],
        far=True,
        name="load_and_low_faces",
    )
    near = [(i, j) for i, j in down_of(gy) if i % 4 in (1, 2)]
    rest = [(i, j) for i, j in down_of(gy) if i % 4 in (0, 3)]
    after = lax.ppermute(down, "gy", near)
    (up,) = call(high_faces, [f32(64, 128)], (*cells, down), size=HINT, name="high_faces")
    before = lax.ppermute(up, "gy", up_of(gy))
    (down,) = call(again, [f32(48, 128)], (down, up), size=HINT, name="again")
    later = lax.ppermute(down, "gy", rest)

    wide, own = call(
        widen_rows,
        [f32(4, 10, ROWS, 128), f32(3, ROWS, 128)],
        (*cells, before, after, later),
        name="widen_rows",
    )
    right = lax.ppermute(own, "gx", down_of(gx))
    left = lax.ppermute(own, "gx", up_of(gx))

    ring_up = [(i, (i + 1) % gz) for i in range(gz)]
    ring_down = [((i + 1) % gz, i) for i in range(gz)]
    up, down = call(z_faces, [f32(16, ROWS, 128), f32(11, ROWS, 128)], (wide, right), name="z_faces")
    before = lax.ppermute(up, "gz", ring_up)
    after = lax.ppermute(down, "gz", ring_down)
    (beside,) = call(columns_on, [f32(3, ROWS, 128)], (own, left, right), size=1 << 30, flops=1 << 36, name="columns_on")
    columns_before = lax.ppermute(beside, "gz", ring_up)
    columns_after = lax.ppermute(beside, "gz", ring_down)

    polar = cells[2]
    brick = f32(3, 4, 16, 128)
    first = call(
        first_step,
        [f32(7, 3, ROWS, 128), f32(6, 3, ROWS, 128), brick, brick, f32(5, 2, ROWS, 128), f32(4, 3, 16, 128)],
        (wide, before, after, polar),
        flops=2_000_000,
        name="first_step",
    )
    return tuple(
        call(
            second_step,
            [brick] * 4,
            (own, left, right, columns_before, columns_after, *first),
            scratch=[pltpu.VMEM((3, 4, 16, 128), jnp.float32)] * 4
            + [pltpu.VMEM((5, 3, ROWS, 128), jnp.float32), pltpu.SemaphoreType.DMA((4,))],
            far_out=True,
            flops=2_000_000,
            name="second_step",
        )
    )


def solution(mesh):
    fields = P(None, "gz", "gy", "gx")
    cells = P("gz", "gy", "gx")
    return jax.shard_map(
        on_device,
        mesh=mesh,
        in_specs=(fields, fields, fields, fields, cells, cells),
        out_specs=(fields, fields, fields, fields),
        check_vma=False,
    )
```

time: 37 us -> 34.8 us (0.941)
  the two profiles are of different devices: /device:TPU:6 before, /device:TPU:31 now
where the time goes in v4:
time: 34.8 us; the launch traced here: 34.6 us
  starting transfers between devices  25.5 us (73%)
  waiting for transfers between devices  5.25 us (15%)
  Pallas kernels  3.1 us (9%)
  between operations  0.74 us (2%)
    ppermute x1, starting transfers between devices, on_device(): before = lax.ppermute(up, 'gy', up_of(gy))  9.45 us
    ppermute x1, starting transfers between devices, on_device(): later = lax.ppermute(down, 'gy', rest)  4.56 us
    ppermute x1, starting transfers between devices, on_device(): left = lax.ppermute(own, 'gx', up_of(gx))  3.99 us
    pallas_call x8, Pallas kernels, call(): pl.pallas_call(kernel, out_shape=outs, in_specs=[HBM if far else VMEM] *...  3.1 us
    ppermute x1, starting transfers between devices, on_device(): columns_before = lax.ppermute(beside, 'gz', ring_up)  2.77 us
    ppermute x1, waiting for transfers between devices, on_device(): after = lax.ppermute(down, 'gz', ring_down)  2.56 us
    ppermute x1, starting transfers between devices, on_device(): before = lax.ppermute(up, 'gz', ring_up)  1.93 us
    ppermute x1, waiting for transfers between devices, on_device(): columns_after = lax.ppermute(beside, 'gz', ring_down)  1.74 us
  transfers between devices with their start and end apart: 9, of which 3 were waited for; matrix products, arithmetic and copies ran while one was open for 0% of the time, Pallas kernels for 1%

profile of v4, /device:TPU:31, one launch (start us, length us, event | category | flops | bytes accessed | tf_op | source)
XLA Modules:
  0.0 34.6 jit_solution(14347060235561418918)
XLA Ops:
  0.6 1.1 %load_and_low_faces.1 = (f32[3,4,16,128]{3,2,1,0:T(8,128)S(1)}, f32[3,4,16,128]{3,2,1,0:T(8,128)S(1)}, f32[3,4,16,128]{3,2,1,0:T(8,128)S(1)}, f32[3,4,16,128]{3,...) custom-call(f32[3,4,16,128]{3,2,1,0:T(8,128)} %refs_0_.1, ...), custom_call_target="tpu_custom_call" | custom-call | bytes 954368 | tf_op jit(solution)/shard_map/load_and_low_faces/pallas_call | solution.py:360
  1.8 1.3 %collective-permute-start.1 = (f32[72,128]{1,0:T(8,128)S(1)}, f32[72,128]{1,0:T(8,128)S(1)}, u32[]{:S(2)}, u32[]{:S(2)}) collective-permute-start(f32[72,128]{1,0:T(8,128)S(1)} %get-tuple-element.27.refs_6_.down), channel_id=1, source_target_pairs={{8,0},{16,8},{40,32},{48,40},{72,64},{80,72},{104,96},{112,104},{9... | collective-permute-start | bytes 110600 | tf_op jit(solution)/shard_map/ppermute | solution.py:391
  3.1 9.4 %collective-permute-start = (f32[64,128]{1,0:T(8,128)S(1)}, f32[64,128]{1,0:T(8,128)S(1)}, u32[]{:S(2)}, u32[]{:S(2)}) collective-permute-start(f32[64,128]{1,0:T(8,128)S(1)} %high_faces.1._), channel_id=1, source_target_pairs={{0,8},{8,16},{16,24},{24,32},{32,40},{40,48},{48,56},{56,64},{64,7... | collective-permute-start | bytes 98312 | tf_op jit(solution)/shard_map/ppermute | solution.py:393
  12.6 4.6 %collective-permute-start.2 = (f32[48,128]{1,0:T(8,128)S(1)}, f32[48,128]{1,0:T(8,128)S(1)}, u32[]{:S(2)}, u32[]{:S(2)}) collective-permute-start(f32[48,128]{1,0:T(8,128)S(1)} %again.1), channel_id=1, source_target_pairs={{24,16},{32,24},{56,48},{64,56},{88,80},{96,88},{120,112},{25,17},... | collective-permute-start | bytes 73736 | tf_op jit(solution)/shard_map/ppermute | solution.py:395
  17.1 0.9 %collective-permute-done.2.later = f32[48,128]{1,0:T(8,128)S(1)} collective-permute-done((f32[48,128]{1,0:T(8,128)S(1)}, f32[48,128]{1,0:T(8,128)S(1)}, u32[]{:S(2)}, u32[]{:S(2)}) %collective-permute-start.2) | collective-permute-done | bytes 24608 | tf_op jit(solution)/shard_map/ppermute | solution.py:395
  18.1 0.0 collective-permute-done.before
  18.1 0.0 collective-permute-done.1.after
  18.1 0.2 widen_rows.1
  18.3 1.3 %collective-permute-start.4 = (f32[3,24,128]{2,1,0:T(8,128)S(1)}, f32[3,24,128]{2,1,0:T(8,128)S(1)}, u32[]{:S(2)}, u32[]{:S(2)}) collective-permute-start(f32[3,24,128]{2,1,0:T(8,128)S(1)} %get-tuple-element.28.own), channel_id=1, source_target_pairs={{128,0},{256,128},{384,256},{129,1},{257,129},{385,257},{130,2},{2... | collective-permute-start | bytes 110600 | tf_op jit(solution)/shard_map/ppermute | solution.py:403
  19.6 4.0 %collective-permute-start.3 = (f32[3,24,128]{2,1,0:T(8,128)S(1)}, f32[3,24,128]{2,1,0:T(8,128)S(1)}, u32[]{:S(2)}, u32[]{:S(2)}) collective-permute-start(f32[3,24,128]{2,1,0:T(8,128)S(1)} %get-tuple-element.28.own), channel_id=1, source_target_pairs={{0,128},{128,256},{256,384},{1,129},{129,257},{257,385},{2,130},{1... | collective-permute-start | bytes 110600 | tf_op jit(solution)/shard_map/ppermute | solution.py:404
  23.6 0.0 collective-permute-done.4.right._
  23.6 1.9 %collective-permute-start.7 = (f32[16,24,128]{2,1,0:T(8,128)S(1)}, f32[16,24,128]{2,1,0:T(8,128)S(1)}, u32[]{:S(2)}, u32[]{:S(2)}) collective-permute-start(f32[16,24,128]{2,1,0:T(8,128)S(1)} %get-tuple-element.30), channel_id=1, source_target_pairs={{0,1},{1,2},{2,3},{3,4},{4,5},{5,6},{6,7},{7,0},{8,9},{9,10},{10,1... | collective-permute-start | bytes 589832 | tf_op jit(solution)/shard_map/ppermute | solution.py:409
  25.6 0.2 collective-permute-start.8
  25.8 0.0 collective-permute-done.3.left
  25.8 0.1 columns_on.1
  25.9 2.8 %collective-permute-start.5 = (f32[3,24,128]{2,1,0:T(8,128)S(1)}, f32[3,24,128]{2,1,0:T(8,128)S(1)}, u32[]{:S(2)}, u32[]{:S(2)}) collective-permute-start(f32[3,24,128]{2,1,0:T(8,128)S(1)} %columns_on.1), channel_id=1, source_target_pairs={{0,1},{1,2},{2,3},{3,4},{4,5},{5,6},{6,7},{7,0},{8,9},{9,10},{10,1... | collective-permute-start | bytes 110600 | tf_op jit(solution)/shard_map/ppermute | solution.py:412
  28.7 0.0 collective-permute-start.6
  28.7 2.6 %collective-permute-done.8.after = f32[11,24,128]{2,1,0:T(8,128)S(1)} collective-permute-done((f32[11,24,128]{2,1,0:T(8,128)S(1)}, f32[11,24,128]{2,1,0:T(8,128)S(1)}, u32[]{:S(2)}, u32[]{:S(2)}) %collective-permute-start.8) | collective-permute-done | bytes 135200 | tf_op jit(solution)/shard_map/ppermute | solution.py:410
  31.2 0.0 collective-permute-done.7.before
  31.2 0.3 first_step.1
  31.5 0.0 collective-permute-done.5.before
  31.5 1.7 %collective-permute-done.6.after = f32[3,24,128]{2,1,0:T(8,128)S(1)} collective-permute-done((f32[3,24,128]{2,1,0:T(8,128)S(1)}, f32[3,24,128]{2,1,0:T(8,128)S(1)}, u32[]{:S(2)}, u32[]{:S(2)}) %collective-permute-start.6) | collective-permute-done | bytes 36896 | tf_op jit(solution)/shard_map/ppermute | solution.py:413
  33.3 1.3 %second_step.1 = (f32[3,4,16,128]{3,2,1,0:T(8,128)}, f32[3,4,16,128]{3,2,1,0:T(8,128)}, f32[3,4,16,128]{3,2,1,0:T(8,128)}, f32[3,4,16,128]{3,2,1,0:T(8,128)}) custom-call(f32[3,24,128]{2,1,0:T(8,128)S(1)} %get-tuple-element.28.own, f32[3,24,128]{2,1,0:T(8,128)S(1)} %collective-permute-done.3.left, f32[3,24,128]{2,1,0:T(8,128)S(1)} %collective-permute-done.4.right._, ...), custom_call_target="tpu_custom_call" | custom-call | flops 2000000 | bytes 1474560 | tf_op jit(solution)/shard_map/second_step/pallas_call | solution.py:360
  (3 shorter events, 0.1 us)
Async XLA Ops:
  1.8 16.3 %collective-permute-start.1 = (f32[72,128]{1,0:T(8,128)S(1)}, f32[72,128]{1,0:T(8,128)S(1)}, u32[]{:S(2)}, u32[]{:S(2)}) collective-permute-start(f32[72,128]{1,0:T(8,128)S(1)} %get-tuple-element.27.refs_6_.down), channel_id=1, source_target_pairs={{8,0},{16,8},{40,32},{48,40},{72,64},{80,72},{104,96},{112,104},{9... | collective-permute-start | bytes 110600 | tf_op jit(solution)/shard_map/ppermute | solution.py:391
  3.1 15.0 %collective-permute-start = (f32[64,128]{1,0:T(8,128)S(1)}, f32[64,128]{1,0:T(8,128)S(1)}, u32[]{:S(2)}, u32[]{:S(2)}) collective-permute-start(f32[64,128]{1,0:T(8,128)S(1)} %high_faces.1._), channel_id=1, source_target_pairs={{0,8},{8,16},{16,24},{24,32},{32,40},{40,48},{48,56},{56,64},{64,7... | collective-permute-start | bytes 98312 | tf_op jit(solution)/shard_map/ppermute | solution.py:393
  12.6 5.5 %collective-permute-start.2 = (f32[48,128]{1,0:T(8,128)S(1)}, f32[48,128]{1,0:T(8,128)S(1)}, u32[]{:S(2)}, u32[]{:S(2)}) collective-permute-start(f32[48,128]{1,0:T(8,128)S(1)} %again.1), channel_id=1, source_target_pairs={{24,16},{32,24},{56,48},{64,56},{88,80},{96,88},{120,112},{25,17},... | collective-permute-start | bytes 73736 | tf_op jit(solution)/shard_map/ppermute | solution.py:395
  18.3 5.3 %collective-permute-start.4 = (f32[3,24,128]{2,1,0:T(8,128)S(1)}, f32[3,24,128]{2,1,0:T(8,128)S(1)}, u32[]{:S(2)}, u32[]{:S(2)}) collective-permute-start(f32[3,24,128]{2,1,0:T(8,128)S(1)} %get-tuple-element.28.own), channel_id=1, source_target_pairs={{128,0},{256,128},{384,256},{129,1},{257,129},{385,257},{130,2},{2... | collective-permute-start | bytes 110600 | tf_op jit(solution)/shard_map/ppermute | solution.py:403
  19.6 6.2 %collective-permute-start.3 = (f32[3,24,128]{2,1,0:T(8,128)S(1)}, f32[3,24,128]{2,1,0:T(8,128)S(1)}, u32[]{:S(2)}, u32[]{:S(2)}) collective-permute-start(f32[3,24,128]{2,1,0:T(8,128)S(1)} %get-tuple-element.28.own), channel_id=1, source_target_pairs={{0,128},{128,256},{256,384},{1,129},{129,257},{257,385},{2,130},{1... | collective-permute-start | bytes 110600 | tf_op jit(solution)/shard_map/ppermute | solution.py:404
  23.6 7.6 %collective-permute-start.7 = (f32[16,24,128]{2,1,0:T(8,128)S(1)}, f32[16,24,128]{2,1,0:T(8,128)S(1)}, u32[]{:S(2)}, u32[]{:S(2)}) collective-permute-start(f32[16,24,128]{2,1,0:T(8,128)S(1)} %get-tuple-element.30), channel_id=1, source_target_pairs={{0,1},{1,2},{2,3},{3,4},{4,5},{5,6},{6,7},{7,0},{8,9},{9,10},{10,1... | collective-permute-start | bytes 589832 | tf_op jit(solution)/shard_map/ppermute | solution.py:409
  25.6 5.6 %collective-permute-start.8 = (f32[11,24,128]{2,1,0:T(8,128)S(1)}, f32[11,24,128]{2,1,0:T(8,128)S(1)}, u32[]{:S(2)}, u32[]{:S(2)}) collective-permute-start(f32[11,24,128]{2,1,0:T(8,128)S(1)} %get-tuple-element.31), channel_id=1, source_target_pairs={{1,0},{2,1},{3,2},{4,3},{5,4},{6,5},{7,6},{0,7},{9,8},{10,9},{11,1... | collective-permute-start | bytes 405512 | tf_op jit(solution)/shard_map/ppermute | solution.py:410
  25.9 5.6 %collective-permute-start.5 = (f32[3,24,128]{2,1,0:T(8,128)S(1)}, f32[3,24,128]{2,1,0:T(8,128)S(1)}, u32[]{:S(2)}, u32[]{:S(2)}) collective-permute-start(f32[3,24,128]{2,1,0:T(8,128)S(1)} %columns_on.1), channel_id=1, source_target_pairs={{0,1},{1,2},{2,3},{3,4},{4,5},{5,6},{6,7},{7,0},{8,9},{9,10},{10,1... | collective-permute-start | bytes 110600 | tf_op jit(solution)/shard_map/ppermute | solution.py:412
  28.7 4.6 %collective-permute-start.6 = (f32[3,24,128]{2,1,0:T(8,128)S(1)}, f32[3,24,128]{2,1,0:T(8,128)S(1)}, u32[]{:S(2)}, u32[]{:S(2)}) collective-permute-start(f32[3,24,128]{2,1,0:T(8,128)S(1)} %columns_on.1), channel_id=1, source_target_pairs={{1,0},{2,1},{3,2},{4,3},{5,4},{6,5},{7,6},{0,7},{9,8},{10,9},{11,1... | collective-permute-start | bytes 110600 | tf_op jit(solution)/shard_map/ppermute | solution.py:413

commit v5 on v4

--- a/solution.py
+++ b/solution.py
@@ -20,11 +20,9 @@
 
 Y_UP = [(c, 14) for c in (EX, EY, EZ, HX, HZ, CODE)] + [(c, 15) for c in EVERY]
 Y_DOWN = [(c, 0) for c in (EX, EY, EZ, HX, HY, HZ, QX, QZ, CODE)] + [(EX, 1), (EZ, 1)]
-Z_UP = [(c, 2) for c in (EX, EY, EZ, HX, HY, CODE)] + [(c, 3) for c in EVERY]
-Z_DOWN = [(c, 0) for c in (EX, EY, EZ, HX, HY, HZ, QX, QY, CODE)] + [(EX, 1), (EY, 1)]
+Z_UP, Z_DOWN = 9, 8
 
 ROWS = 24
-PLANES = range(-2, 6)
 SPAN = 32
 HINT = 1 << 26
 
@@ -103,22 +101,56 @@
         edges[g] = total
 
 
-def z_faces(wide, _, up, down):
-    for i, (c, z) in enumerate(Z_UP):
-        up[i] = wide[z, c]
-    for i, (c, z) in enumerate(Z_DOWN):
-        down[i] = wide[z, c]
-
-
-def sides(own, left, right, g):
+def z_faces(wide, polar, _, up, down, h1, r1, p1, j1, fh, fe, push):
+    for z in range(4):
+        e = [wide[z, EX + k] for k in range(3)]
+        h = [wide[z, HX + k] for k in range(3)]
+        keep_h, push_h, keep_e, push_e, metal = factors(wide[z, CODE])
+        later = [wide[z + 1, EX + k] for k in range(2)] if z < 3 else [0.0, 0.0]
+        new = magnetic_new(
+            h,
+            e,
+            {0: y_next(e[0]), 2: y_next(e[2])},
+            {0: later[0], 1: later[1]},
+            {1: x_next(e[1]), 2: x_next(e[2])},
+            keep_h,
+            push_h,
+        )
+        flow = [wide[z, QX + k] + GAIN * metal * e[k] for k in range(3)]
+        rest = [keep_e * e[k] - push_e * (metal * flow[k]) for k in range(3)]
+        for k in range(3):
+            h1[z, k] = new[k]
+            r1[z, k] = rest[k]
+            j1[k, z] = flow[k][0:16]
+            p1[k, z] = polar[k, z] + time_step * flow[k][0:16]
+        fh[z, 0] = keep_h
+        fh[z, 1] = push_h
+        push[z] = push_e
+        for k, f in enumerate((keep_e, push_e, metal)):
+            fe[z, k] = f[0:16]
+        if z == 0:
+            for i, value in enumerate(new + rest[:2] + [wide[z, CODE]] + e[:2]):
+                down[i] = value
+        if z == 2:
+            up[7] = new[0]
+            up[8] = new[1]
+        if z == 3:
+            for i, value in enumerate(new + rest + [wide[z, CODE]]):
+                up[i] = value
+
+
+def sides(own, outer, inner, g):
     near = (lanes() % 4) < 2
-    return jnp.where(near, left[g], own[g]), jnp.where(near, own[g], right[g])
-
-
-def columns_on(own, left, right, out):
+    odd = lax.axis_index("gx") % 2 == 1
+    left = jnp.where(odd, outer[g], inner[g])
+    right = jnp.where(odd, inner[g], outer[g])
+    return jnp.where(near, left, own[g]), jnp.where(near, own[g], right)
+
+
+def columns_on(own, outer, inner, out):
     part = (lanes() % SPAN) // 8
     for g in range(3):
-        low, high = sides(own, left, right, g)
+        low, high = sides(own, outer, inner, g)
         up = jnp.where(part == 0, roll(low, -16, 1), roll(high, -8, 1))
         down = jnp.where(part == 2, roll(high, 8, 1), roll(low, 16, 1))
         out[g] = jnp.where(part < 2, up, down)
@@ -127,25 +159,6 @@
 def grid_ends():
     place = lax.axis_index("gz")
     return place == 0, place == lax.axis_size("gz") - 1
-
-
-def planes_of(wide, before, after):
-    first, last = grid_ends()
-
-    def plane(c, z):
-        if 0 <= z < 4:
-            return wide[z, c]
-        if z < 0:
-            if (c, z + 4) not in Z_UP:
-                return None
-            got = before[Z_UP.index((c, z + 4))]
-            return jnp.where(first, 0.0, got)
-        if (c, z - 4) not in Z_DOWN:
-            return None
-        got = after[Z_DOWN.index((c, z - 4))]
-        return jnp.where(last, 0.0, got)
-
-    return plane
 
 
 def lanes():
@@ -184,12 +197,16 @@
     return [None if h[k] is None else keep * h[k] - push * curl[k] for k in range(3)]
 
 
-def electric_new(e, h, hy, hz, hx, drag, keep, push):
-    curl = (
+def curl_back(h, hy, hz, hx):
+    return (
         (h[2] - hy[2]) - (h[1] - hz[1]),
         (h[0] - hz[0]) - (h[2] - hx[2]),
         (h[1] - hx[1]) - (h[0] - hy[0]),
     )
+
+
+def electric_new(e, h, hy, hz, hx, drag, keep, push):
+    curl = curl_back(h, hy, hz, hx)
     return [keep * e[k] + push * (curl[k] - drag[k]) for k in range(3)]
 
 
@@ -199,62 +216,53 @@
 y_back = lambda a: roll(a, 1, 0)
 
 
-def first_step(wide, before, after, polar, h1, e1, p1, j1, fh, fe):
-    plane = planes_of(wide, before, after)
-    for z in range(-2, 5):
-        e = [plane(EX + k, z) for k in range(3)]
-        up = [plane(EX + k, z + 1) for k in range(2)]
-        h = [plane(HX + k, z) for k in range(3)]
-        keep_h, push_h, keep_e, push_e, metal = factors(plane(CODE, z))
-        new = magnetic_new(
-            h,
-            e,
-            {0: y_next(e[0]), 2: y_next(e[2])},
-            {0: up[0], 1: up[1]},
-            {1: x_next(e[1]), 2: x_next(e[2])},
-            keep_h,
-            push_h,
-        )
-        for k in range(3):
-            if new[k] is not None:
-                h1[z + 2, k] = new[k]
-        if -1 <= z < 4:
-            fh[z + 1, 0] = keep_h
-            fh[z + 1, 1] = push_h
-        if 0 <= z < 4:
-            for k, f in enumerate((keep_e, push_e, metal)):
-                fe[z, k] = f[0:16]
-        if z == -2:
-            continue
-        h = new
-        down = [h1[z + 1, k] for k in range(2)]
-        held = [plane(QX + k, z) for k in range(3)]
-        flow = [None if held[k] is None else held[k] + GAIN * metal * e[k] for k in range(3)]
-        if 0 <= z < 4:
-            for k in range(3):
-                j1[k, z] = flow[k][0:16]
-                p1[k, z] = polar[k, z] + time_step * flow[k][0:16]
-        new = electric_new(
-            e,
+def first_step(wide, before, after, part, r1, fh, push, h1, e1, low):
+    first, last = grid_ends()
+
+    def from_below(i):
+        return jnp.where(first, 0.0, before[i])
+
+    def from_above(i):
+        return jnp.where(last, 0.0, after[i])
+
+    def with_next(h, push_h, x, y):
+        return [h[0] + push_h * y, h[1] - push_h * x, h[2]]
+
+    def electric(z, rest, push_e, h, back):
+        curl = curl_back(
             h,
             {0: y_back(h[0]), 2: y_back(h[2])},
-            {0: down[0], 1: down[1]},
+            {0: back[0], 1: back[1]},
             {1: x_back(h[1]), 2: x_back(h[2])},
-            [0.0 if flow[k] is None else metal * flow[k] for k in range(3)],
-            keep_e,
-            push_e,
         )
+        for k, r in enumerate(rest):
+            e1[z + 1, k] = r + push_e * curl[k]
+
+    keep_h, push_h, _, push_e, _ = factors(from_below(6))
+    low[0] = keep_h
+    low[1] = push_h
+    h = with_next([from_below(k) for k in range(3)], push_h, wide[0, EX], wide[0, EY])
+    electric(-1, [from_below(3 + k) for k in range(3)], push_e, h, [from_below(7), from_below(8)])
+    for z in range(4):
         for k in range(3):
-            e1[z + 1, k] = new[k]
-
-
-def columns(own, left, right, before, after):
+            h1[z, k] = h[k]
+        back, h = h, [part[z, k] for k in range(3)]
+        if z == 3:
+            h = with_next(h, fh[z, 1], from_above(6), from_above(7))
+        electric(z, [r1[z, k] for k in range(3)], push[z], h, back)
+    for k in range(3):
+        h1[4, k] = h[k]
+    _, _, _, push_e, _ = factors(from_above(5))
+    electric(4, [from_above(3 + k) for k in range(2)], push_e, [from_above(k) for k in range(3)], h)
+
+
+def columns(own, outer, inner, before, after):
     first, last = grid_ends()
     lane = lanes()
     part = (lane % SPAN) // 8
     values = []
     for g in range(3):
-        low, high = sides(own, left, right, g)
+        low, high = sides(own, outer, inner, g)
         up = jnp.where(first, 0.0, before[g])
         down = jnp.where(last, 0.0, after[g])
         low = jnp.where(part == 0, up, jnp.where(part == 3, down, low))
@@ -276,11 +284,11 @@
     return h1, e1, h2
 
 
-def second_step(own, left, right, before, after, h1, e1, p1, j1, fh, fe, *rest):
+def second_step(own, outer, inner, before, after, h1, e1, low, p1, j1, fh, fe, *rest):
     outs, near, h2, done = rest[:4], rest[4:8], rest[8], rest[9]
     e_near, h_near, p_near, j_near = near
     lane = lanes()
-    ch1, ce1, ch2 = columns(own, left, right, before, after)
+    ch1, ce1, ch2 = columns(own, outer, inner, before, after)
 
     def at_ends(column):
         return jnp.where(lane % 4 == 1, roll(column, -SPAN, 1), column)
@@ -298,7 +306,7 @@
         return lambda k: jnp.where(lane == 0, roll(ch2[k], -(4 * (z + 2) + 1), 1), x_back(array[k]))
 
     def fixed_e(z):
-        return [put_right(e1[z + 1, k], z, ends_e[k]) for k in range(3)]
+        return [put_right(e1[z + 1, k], z, ends_e[k]) for k in range(3 if z < 4 else 2)]
 
     copies = [pltpu.make_async_copy(a, b, done.at[i]) for i, (a, b) in enumerate(zip(near, outs))]
     for z in range(4):
@@ -313,7 +321,7 @@
     e = fixed_e(-1)
     for z in range(-1, 4):
         up = fixed_e(z + 1)
-        h = [h1[z + 2, 0]] + [put_right(h1[z + 2, k], z, ends_h[k]) for k in (1, 2)]
+        h = [h1[z + 1, 0]] + [put_right(h1[z + 1, k], z, ends_h[k]) for k in (1, 2)]
         x = after_x(e, z)
         new = magnetic_new(
             h,
@@ -321,8 +329,8 @@
             {0: y_next(e[0]), 2: y_next(e[2])},
             {0: up[0], 1: up[1]},
             {1: x(1), 2: x(2)},
-            fh[z + 1, 0],
-            fh[z + 1, 1],
+            fh[z, 0] if z >= 0 else low[0],
+            fh[z, 1] if z >= 0 else low[1],
         )
         for k in range(3):
             h2[z + 1, k] = new[k]
@@ -400,32 +408,40 @@
         (*cells, before, after, later),
         name="widen_rows",
     )
-    right = lax.ppermute(own, "gx", down_of(gx))
-    left = lax.ppermute(own, "gx", up_of(gx))
+    pairs = [(i, i ^ 1) for i in range(gx) if i ^ 1 < gx]
+    between = [(i, j) for i in range(1, gx - 1, 2) if i + 1 < gx for i, j in ((i, i + 1), (i + 1, i))]
+    outer = lax.ppermute(own, "gx", pairs)
+    inner = lax.ppermute(own, "gx", between)
 
     ring_up = [(i, (i + 1) % gz) for i in range(gz)]
     ring_down = [((i + 1) % gz, i) for i in range(gz)]
-    up, down = call(z_faces, [f32(16, ROWS, 128), f32(11, ROWS, 128)], (wide, right), name="z_faces")
+    brick, plane = f32(3, 4, 16, 128), (ROWS, 128)
+    up, down, h1, r1, p1, j1, fh, fe, push = call(
+        z_faces,
+        [f32(Z_UP, *plane), f32(Z_DOWN, *plane), f32(4, 3, *plane), f32(4, 3, *plane), brick, brick]
+        + [f32(4, 2, *plane), f32(4, 3, 16, 128), f32(4, *plane)],
+        (wide, cells[2], own),
+        flops=1_000_000,
+        name="z_faces",
+    )
     before = lax.ppermute(up, "gz", ring_up)
     after = lax.ppermute(down, "gz", ring_down)
-    (beside,) = call(columns_on, [f32(3, ROWS, 128)], (own, left, right), size=1 << 30, flops=1 << 36, name="columns_on")
+    (beside,) = call(columns_on, [f32(3, ROWS, 128)], (own, outer, inner), size=1 << 30, flops=1 << 36, name="columns_on")
     columns_before = lax.ppermute(beside, "gz", ring_up)
     columns_after = lax.ppermute(beside, "gz", ring_down)
 
-    polar = cells[2]
-    brick = f32(3, 4, 16, 128)
-    first = call(
+    h1, e1, low = call(
         first_step,
-        [f32(7, 3, ROWS, 128), f32(6, 3, ROWS, 128), brick, brick, f32(5, 2, ROWS, 128), f32(4, 3, 16, 128)],
-        (wide, before, after, polar),
-        flops=2_000_000,
+        [f32(5, 3, *plane), f32(6, 3, *plane), f32(2, *plane)],
+        (wide, before, after, h1, r1, fh, push),
+        flops=1_000_000,
         name="first_step",
     )
     return tuple(
         call(
             second_step,
             [brick] * 4,
-            (own, left, right, columns_before, columns_after, *first),
+            (own, outer, inner, columns_before, columns_after, h1, e1, low, p1, j1, fh, fe),
             scratch=[pltpu.VMEM((3, 4, 16, 128), jnp.float32)] * 4
             + [pltpu.VMEM((5, 3, ROWS, 128), jnp.float32), pltpu.SemaphoreType.DMA((4,))],
             far_out=True,

time: 34.8 us -> 34.2 us (0.983)
  the two profiles are of different devices: /device:TPU:31 before, /device:TPU:63 now
where the time goes in v5:
time: 34.2 us; the launch traced here: 34 us
  starting transfers between devices  24.8 us (73%)
  waiting for transfers between devices  5.4 us (16%)
  Pallas kernels  3.07 us (9%)
  between operations  0.73 us (2%)
    ppermute x1, starting transfers between devices, on_device(): before = lax.ppermute(up, 'gy', up_of(gy))  9.45 us
    ppermute x1, starting transfers between devices, on_device(): later = lax.ppermute(down, 'gy', rest)  3.66 us
    pallas_call x8, Pallas kernels, call(): pl.pallas_call(kernel, out_shape=outs, in_specs=[HBM if far else VMEM] *...  3.07 us
    ppermute x1, starting transfers between devices, on_device(): columns_before = lax.ppermute(beside, 'gz', ring_up)  2.77 us
    ppermute x1, starting transfers between devices, on_device(): inner = lax.ppermute(own, 'gx', between)  2.66 us
    ppermute x1, starting transfers between devices, on_device(): outer = lax.ppermute(own, 'gx', pairs)  2.64 us
    ppermute x1, waiting for transfers between devices, on_device(): columns_after = lax.ppermute(beside, 'gz', ring_down)  2.3 us
    ppermute x1, waiting for transfers between devices, on_device(): after = lax.ppermute(down, 'gz', ring_down)  2.16 us
  transfers between devices with their start and end apart: 9, of which 3 were waited for; matrix products, arithmetic and copies ran while one was open for 0% of the time, Pallas kernels for 1%

profile of v5, /device:TPU:63, one launch (start us, length us, event | category | flops | bytes accessed | tf_op | source)
XLA Modules:
  0.0 34.0 jit_solution(7495666044125894865)
XLA Ops:
  0.6 1.1 %load_and_low_faces.1 = (f32[3,4,16,128]{3,2,1,0:T(8,128)S(1)}, f32[3,4,16,128]{3,2,1,0:T(8,128)S(1)}, f32[3,4,16,128]{3,2,1,0:T(8,128)S(1)}, f32[3,4,16,128]{3,...) custom-call(f32[3,4,16,128]{3,2,1,0:T(8,128)} %refs_0_.1, ...), custom_call_target="tpu_custom_call" | custom-call | bytes 954368 | tf_op jit(solution)/shard_map/load_and_low_faces/pallas_call | solution.py:368
  1.8 1.3 %collective-permute-start.1 = (f32[72,128]{1,0:T(8,128)S(1)}, f32[72,128]{1,0:T(8,128)S(1)}, u32[]{:S(2)}, u32[]{:S(2)}) collective-permute-start(f32[72,128]{1,0:T(8,128)S(1)} %get-tuple-element.31.refs_6_.down), channel_id=1, source_target_pairs={{8,0},{16,8},{40,32},{48,40},{72,64},{80,72},{104,96},{112,104},{9... | collective-permute-start | bytes 110600 | tf_op jit(solution)/shard_map/ppermute | solution.py:399
  3.1 9.4 %collective-permute-start = (f32[64,128]{1,0:T(8,128)S(1)}, f32[64,128]{1,0:T(8,128)S(1)}, u32[]{:S(2)}, u32[]{:S(2)}) collective-permute-start(f32[64,128]{1,0:T(8,128)S(1)} %high_faces.1._), channel_id=1, source_target_pairs={{0,8},{8,16},{16,24},{24,32},{32,40},{40,48},{48,56},{56,64},{64,7... | collective-permute-start | bytes 98312 | tf_op jit(solution)/shard_map/ppermute | solution.py:401
  12.6 3.7 %collective-permute-start.2 = (f32[48,128]{1,0:T(8,128)S(1)}, f32[48,128]{1,0:T(8,128)S(1)}, u32[]{:S(2)}, u32[]{:S(2)}) collective-permute-start(f32[48,128]{1,0:T(8,128)S(1)} %again.1), channel_id=1, source_target_pairs={{24,16},{32,24},{56,48},{64,56},{88,80},{96,88},{120,112},{25,17},... | collective-permute-start | bytes 73736 | tf_op jit(solution)/shard_map/ppermute | solution.py:403
  16.2 0.9 %collective-permute-done.2.later = f32[48,128]{1,0:T(8,128)S(1)} collective-permute-done((f32[48,128]{1,0:T(8,128)S(1)}, f32[48,128]{1,0:T(8,128)S(1)}, u32[]{:S(2)}, u32[]{:S(2)}) %collective-permute-start.2) | collective-permute-done | bytes 24608 | tf_op jit(solution)/shard_map/ppermute | solution.py:403
  17.2 0.0 collective-permute-done.before
  17.2 0.0 collective-permute-done.1.after
  17.2 0.2 widen_rows.1
  17.4 2.6 %collective-permute-start.3 = (f32[3,24,128]{2,1,0:T(8,128)S(1)}, f32[3,24,128]{2,1,0:T(8,128)S(1)}, u32[]{:S(2)}, u32[]{:S(2)}) collective-permute-start(f32[3,24,128]{2,1,0:T(8,128)S(1)} %get-tuple-element.32.own._), channel_id=1, source_target_pairs={{0,128},{128,0},{256,384},{384,256},{1,129},{129,1},{257,385},{385... | collective-permute-start | bytes 110600 | tf_op jit(solution)/shard_map/ppermute | solution.py:413
  20.1 2.7 %collective-permute-start.4 = (f32[3,24,128]{2,1,0:T(8,128)S(1)}, f32[3,24,128]{2,1,0:T(8,128)S(1)}, u32[]{:S(2)}, u32[]{:S(2)}) collective-permute-start(f32[3,24,128]{2,1,0:T(8,128)S(1)} %get-tuple-element.32.own._), channel_id=1, source_target_pairs={{128,256},{256,128},{129,257},{257,129},{130,258},{258,130},{131,2... | collective-permute-start | bytes 110600 | tf_op jit(solution)/shard_map/ppermute | solution.py:414
  22.7 0.1 z_faces.1
  22.9 2.1 %collective-permute-start.7 = (f32[9,24,128]{2,1,0:T(8,128)S(1)}, f32[9,24,128]{2,1,0:T(8,128)S(1)}, u32[]{:S(2)}, u32[]{:S(2)}) collective-permute-start(f32[9,24,128]{2,1,0:T(8,128)S(1)} %get-tuple-element.34), channel_id=1, source_target_pairs={{0,1},{1,2},{2,3},{3,4},{4,5},{5,6},{6,7},{7,0},{8,9},{9,10},{10,1... | collective-permute-start | bytes 331784 | tf_op jit(solution)/shard_map/ppermute | solution.py:427
  25.0 0.2 collective-permute-start.8
  25.2 0.0 collective-permute-done.3.outer
  25.2 0.0 collective-permute-done.4.inner
  25.2 0.1 columns_on.1
  25.3 2.8 %collective-permute-start.5 = (f32[3,24,128]{2,1,0:T(8,128)S(1)}, f32[3,24,128]{2,1,0:T(8,128)S(1)}, u32[]{:S(2)}, u32[]{:S(2)}) collective-permute-start(f32[3,24,128]{2,1,0:T(8,128)S(1)} %columns_on.1), channel_id=1, source_target_pairs={{0,1},{1,2},{2,3},{3,4},{4,5},{5,6},{6,7},{7,0},{8,9},{9,10},{10,1... | collective-permute-start | bytes 110600 | tf_op jit(solution)/shard_map/ppermute | solution.py:430
  28.1 0.0 collective-permute-start.6
  28.1 2.2 %collective-permute-done.8.after = f32[8,24,128]{2,1,0:T(8,128)S(1)} collective-permute-done((f32[8,24,128]{2,1,0:T(8,128)S(1)}, f32[8,24,128]{2,1,0:T(8,128)S(1)}, u32[]{:S(2)}, u32[]{:S(2)}) %collective-permute-start.8) | collective-permute-done | bytes 98336 | tf_op jit(solution)/shard_map/ppermute | solution.py:428
  30.2 0.0 collective-permute-done.7.before
  30.2 0.1 first_step.1
  30.4 0.0 collective-permute-done.5.before
  30.4 2.3 %collective-permute-done.6.after = f32[3,24,128]{2,1,0:T(8,128)S(1)} collective-permute-done((f32[3,24,128]{2,1,0:T(8,128)S(1)}, f32[3,24,128]{2,1,0:T(8,128)S(1)}, u32[]{:S(2)}, u32[]{:S(2)}) %collective-permute-start.6) | collective-permute-done | bytes 36896 | tf_op jit(solution)/shard_map/ppermute | solution.py:431
  32.7 1.3 %second_step.1 = (f32[3,4,16,128]{3,2,1,0:T(8,128)}, f32[3,4,16,128]{3,2,1,0:T(8,128)}, f32[3,4,16,128]{3,2,1,0:T(8,128)}, f32[3,4,16,128]{3,2,1,0:T(8,128)}) custom-call(f32[3,24,128]{2,1,0:T(8,128)S(1)} %get-tuple-element.32.own._, f32[3,24,128]{2,1,0:T(8,128)S(1)} %collective-permute-done.3.outer, f32[3,24,128]{2,1,0:T(8,128)S(1)} %collective-permute-done.4.inner, ...), custom_call_target="tpu_custom_call" | custom-call | flops 2000000 | bytes 1400832 | tf_op jit(solution)/shard_map/second_step/pallas_call | solution.py:368
  (2 shorter events, 0.0 us)
Async XLA Ops:
  1.8 15.4 %collective-permute-start.1 = (f32[72,128]{1,0:T(8,128)S(1)}, f32[72,128]{1,0:T(8,128)S(1)}, u32[]{:S(2)}, u32[]{:S(2)}) collective-permute-start(f32[72,128]{1,0:T(8,128)S(1)} %get-tuple-element.31.refs_6_.down), channel_id=1, source_target_pairs={{8,0},{16,8},{40,32},{48,40},{72,64},{80,72},{104,96},{112,104},{9... | collective-permute-start | bytes 110600 | tf_op jit(solution)/shard_map/ppermute | solution.py:399
  3.1 14.1 %collective-permute-start = (f32[64,128]{1,0:T(8,128)S(1)}, f32[64,128]{1,0:T(8,128)S(1)}, u32[]{:S(2)}, u32[]{:S(2)}) collective-permute-start(f32[64,128]{1,0:T(8,128)S(1)} %high_faces.1._), channel_id=1, source_target_pairs={{0,8},{8,16},{16,24},{24,32},{32,40},{40,48},{48,56},{56,64},{64,7... | collective-permute-start | bytes 98312 | tf_op jit(solution)/shard_map/ppermute | solution.py:401
  12.6 4.6 %collective-permute-start.2 = (f32[48,128]{1,0:T(8,128)S(1)}, f32[48,128]{1,0:T(8,128)S(1)}, u32[]{:S(2)}, u32[]{:S(2)}) collective-permute-start(f32[48,128]{1,0:T(8,128)S(1)} %again.1), channel_id=1, source_target_pairs={{24,16},{32,24},{56,48},{64,56},{88,80},{96,88},{120,112},{25,17},... | collective-permute-start | bytes 73736 | tf_op jit(solution)/shard_map/ppermute | solution.py:403
  17.4 7.8 %collective-permute-start.3 = (f32[3,24,128]{2,1,0:T(8,128)S(1)}, f32[3,24,128]{2,1,0:T(8,128)S(1)}, u32[]{:S(2)}, u32[]{:S(2)}) collective-permute-start(f32[3,24,128]{2,1,0:T(8,128)S(1)} %get-tuple-element.32.own._), channel_id=1, source_target_pairs={{0,128},{128,0},{256,384},{384,256},{1,129},{129,1},{257,385},{385... | collective-permute-start | bytes 110600 | tf_op jit(solution)/shard_map/ppermute | solution.py:413
  20.1 5.1 %collective-permute-start.4 = (f32[3,24,128]{2,1,0:T(8,128)S(1)}, f32[3,24,128]{2,1,0:T(8,128)S(1)}, u32[]{:S(2)}, u32[]{:S(2)}) collective-permute-start(f32[3,24,128]{2,1,0:T(8,128)S(1)} %get-tuple-element.32.own._), channel_id=1, source_target_pairs={{128,256},{256,128},{129,257},{257,129},{130,258},{258,130},{131,2... | collective-permute-start | bytes 110600 | tf_op jit(solution)/shard_map/ppermute | solution.py:414
  22.9 7.4 %collective-permute-start.7 = (f32[9,24,128]{2,1,0:T(8,128)S(1)}, f32[9,24,128]{2,1,0:T(8,128)S(1)}, u32[]{:S(2)}, u32[]{:S(2)}) collective-permute-start(f32[9,24,128]{2,1,0:T(8,128)S(1)} %get-tuple-element.34), channel_id=1, source_target_pairs={{0,1},{1,2},{2,3},{3,4},{4,5},{5,6},{6,7},{7,0},{8,9},{9,10},{10,1... | collective-permute-start | bytes 331784 | tf_op jit(solution)/shard_map/ppermute | solution.py:427
  25.0 5.3 %collective-permute-start.8 = (f32[8,24,128]{2,1,0:T(8,128)S(1)}, f32[8,24,128]{2,1,0:T(8,128)S(1)}, u32[]{:S(2)}, u32[]{:S(2)}) collective-permute-start(f32[8,24,128]{2,1,0:T(8,128)S(1)} %get-tuple-element.35), channel_id=1, source_target_pairs={{1,0},{2,1},{3,2},{4,3},{5,4},{6,5},{7,6},{0,7},{9,8},{10,9},{11,1... | collective-permute-start | bytes 294920 | tf_op jit(solution)/shard_map/ppermute | solution.py:428
  25.3 5.1 %collective-permute-start.5 = (f32[3,24,128]{2,1,0:T(8,128)S(1)}, f32[3,24,128]{2,1,0:T(8,128)S(1)}, u32[]{:S(2)}, u32[]{:S(2)}) collective-permute-start(f32[3,24,128]{2,1,0:T(8,128)S(1)} %columns_on.1), channel_id=1, source_target_pairs={{0,1},{1,2},{2,3},{3,4},{4,5},{5,6},{6,7},{7,0},{8,9},{9,10},{10,1... | collective-permute-start | bytes 110600 | tf_op jit(solution)/shard_map/ppermute | solution.py:430
  28.1 4.6 %collective-permute-start.6 = (f32[3,24,128]{2,1,0:T(8,128)S(1)}, f32[3,24,128]{2,1,0:T(8,128)S(1)}, u32[]{:S(2)}, u32[]{:S(2)}) collective-permute-start(f32[3,24,128]{2,1,0:T(8,128)S(1)} %columns_on.1), channel_id=1, source_target_pairs={{1,0},{2,1},{3,2},{4,3},{5,4},{6,5},{7,6},{0,7},{9,8},{10,9},{11,1... | collective-permute-start | bytes 110600 | tf_op jit(solution)/shard_map/ppermute | solution.py:431

commit v6 on v5

--- a/solution.py
+++ b/solution.py
@@ -147,13 +147,14 @@
     return jnp.where(near, left, own[g]), jnp.where(near, own[g], right)
 
 
-def columns_on(own, outer, inner, out):
+def columns_on(own, outer, inner, *outs):
     part = (lanes() % SPAN) // 8
     for g in range(3):
         low, high = sides(own, outer, inner, g)
         up = jnp.where(part == 0, roll(low, -16, 1), roll(high, -8, 1))
         down = jnp.where(part == 2, roll(high, 8, 1), roll(low, 16, 1))
-        out[g] = jnp.where(part < 2, up, down)
+        for out in outs:
+            out[ROWS * g : ROWS * (g + 1), :] = jnp.where(part < 2, up, down)
 
 
 def grid_ends():
@@ -263,8 +264,9 @@
     values = []
     for g in range(3):
         low, high = sides(own, outer, inner, g)
-        up = jnp.where(first, 0.0, before[g])
-        down = jnp.where(last, 0.0, after[g])
+        rows = slice(ROWS * g, ROWS * (g + 1))
+        up = jnp.where(first, 0.0, before[rows, :])
+        down = jnp.where(last, 0.0, after[rows, :])
         low = jnp.where(part == 0, up, jnp.where(part == 3, down, low))
         high = jnp.where(part == 0, roll(up, -8, 1), jnp.where(part == 3, roll(down, 8, 1), high))
         for k in range(4):
@@ -426,9 +428,9 @@
     )
     before = lax.ppermute(up, "gz", ring_up)
     after = lax.ppermute(down, "gz", ring_down)
-    (beside,) = call(columns_on, [f32(3, ROWS, 128)], (own, outer, inner), size=1 << 30, flops=1 << 36, name="columns_on")
-    columns_before = lax.ppermute(beside, "gz", ring_up)
-    columns_after = lax.ppermute(beside, "gz", ring_down)
+    up, down = call(columns_on, [f32(72, 128), f32(73, 128)], (own, outer, inner), size=1 << 30, flops=1 << 36, name="columns_on")
+    columns_before = lax.ppermute(up, "gz", ring_up)
+    columns_after = lax.ppermute(down, "gz", ring_down)
 
     h1, e1, low = call(
         first_step,

time: 34.2 us -> 33.9 us (level)
  the two profiles are of different devices: /device:TPU:63 before, /device:TPU:38 now
where the time goes in v6:
time: 33.9 us; the launch traced here: 33.7 us
  starting transfers between devices  24.2 us (71%)
  waiting for transfers between devices  5.68 us (17%)
  Pallas kernels  3.07 us (9%)
  between operations  0.73 us (2%)
    ppermute x1, starting transfers between devices, on_device(): before = lax.ppermute(up, 'gy', up_of(gy))  9.73 us
    ppermute x1, starting transfers between devices, on_device(): later = lax.ppermute(down, 'gy', rest)  3.66 us
    ppermute x1, starting transfers between devices, on_device(): inner = lax.ppermute(own, 'gx', between)  3.13 us
    pallas_call x8, Pallas kernels, call(): pl.pallas_call(kernel, out_shape=outs, in_specs=[HBM if far else VMEM] *...  3.07 us
    ppermute x1, starting transfers between devices, on_device(): after = lax.ppermute(down, 'gz', ring_down)  2.94 us
    ppermute x1, starting transfers between devices, on_device(): outer = lax.ppermute(own, 'gx', pairs)  2.92 us
    ppermute x1, waiting for transfers between devices, on_device(): columns_before = lax.ppermute(up, 'gz', ring_up)  2.38 us
    ppermute x1, waiting for transfers between devices, on_device(): after = lax.ppermute(down, 'gz', ring_down)  1.57 us
  transfers between devices with their start and end apart: 9, of which 4 were waited for; matrix products, arithmetic and copies ran while one was open for 0% of the time, Pallas kernels for 1%

profile of v6, /device:TPU:38, one launch (start us, length us, event | category | flops | bytes accessed | tf_op | source)
XLA Modules:
  0.0 33.7 jit_solution(4012070676495675486)
XLA Ops:
  0.6 1.1 %load_and_low_faces.1 = (f32[3,4,16,128]{3,2,1,0:T(8,128)S(1)}, f32[3,4,16,128]{3,2,1,0:T(8,128)S(1)}, f32[3,4,16,128]{3,2,1,0:T(8,128)S(1)}, f32[3,4,16,128]{3,...) custom-call(f32[3,4,16,128]{3,2,1,0:T(8,128)} %refs_0_.1, ...), custom_call_target="tpu_custom_call" | custom-call | bytes 954368 | tf_op jit(solution)/shard_map/load_and_low_faces/pallas_call | solution.py:370
  1.8 1.3 %collective-permute-start.1 = (f32[72,128]{1,0:T(8,128)S(1)}, f32[72,128]{1,0:T(8,128)S(1)}, u32[]{:S(2)}, u32[]{:S(2)}) collective-permute-start(f32[72,128]{1,0:T(8,128)S(1)} %get-tuple-element.33.refs_6_.down), channel_id=1, source_target_pairs={{8,0},{16,8},{40,32},{48,40},{72,64},{80,72},{104,96},{112,104},{9... | collective-permute-start | bytes 110600 | tf_op jit(solution)/shard_map/ppermute | solution.py:401
  3.1 9.7 %collective-permute-start = (f32[64,128]{1,0:T(8,128)S(1)}, f32[64,128]{1,0:T(8,128)S(1)}, u32[]{:S(2)}, u32[]{:S(2)}) collective-permute-start(f32[64,128]{1,0:T(8,128)S(1)} %high_faces.1._), channel_id=1, source_target_pairs={{0,8},{8,16},{16,24},{24,32},{32,40},{40,48},{48,56},{56,64},{64,7... | collective-permute-start | bytes 98312 | tf_op jit(solution)/shard_map/ppermute | solution.py:403
  12.8 3.7 %collective-permute-start.2 = (f32[48,128]{1,0:T(8,128)S(1)}, f32[48,128]{1,0:T(8,128)S(1)}, u32[]{:S(2)}, u32[]{:S(2)}) collective-permute-start(f32[48,128]{1,0:T(8,128)S(1)} %again.1), channel_id=1, source_target_pairs={{24,16},{32,24},{56,48},{64,56},{88,80},{96,88},{120,112},{25,17},... | collective-permute-start | bytes 73736 | tf_op jit(solution)/shard_map/ppermute | solution.py:405
  16.5 1.5 %collective-permute-done.2.later = f32[48,128]{1,0:T(8,128)S(1)} collective-permute-done((f32[48,128]{1,0:T(8,128)S(1)}, f32[48,128]{1,0:T(8,128)S(1)}, u32[]{:S(2)}, u32[]{:S(2)}) %collective-permute-start.2) | collective-permute-done | bytes 24608 | tf_op jit(solution)/shard_map/ppermute | solution.py:405
  18.0 0.0 collective-permute-done.before
  18.0 0.0 collective-permute-done.1.after
  18.0 0.2 widen_rows.1
  18.3 2.9 %collective-permute-start.3 = (f32[3,24,128]{2,1,0:T(8,128)S(1)}, f32[3,24,128]{2,1,0:T(8,128)S(1)}, u32[]{:S(2)}, u32[]{:S(2)}) collective-permute-start(f32[3,24,128]{2,1,0:T(8,128)S(1)} %get-tuple-element.34.own._), channel_id=1, source_target_pairs={{0,128},{128,0},{256,384},{384,256},{1,129},{129,1},{257,385},{385... | collective-permute-start | bytes 110600 | tf_op jit(solution)/shard_map/ppermute | solution.py:415
  21.2 3.1 %collective-permute-start.4 = (f32[3,24,128]{2,1,0:T(8,128)S(1)}, f32[3,24,128]{2,1,0:T(8,128)S(1)}, u32[]{:S(2)}, u32[]{:S(2)}) collective-permute-start(f32[3,24,128]{2,1,0:T(8,128)S(1)} %get-tuple-element.34.own._), channel_id=1, source_target_pairs={{128,256},{256,128},{129,257},{257,129},{130,258},{258,130},{131,2... | collective-permute-start | bytes 110600 | tf_op jit(solution)/shard_map/ppermute | solution.py:416
  24.3 0.1 z_faces.1
  24.5 0.0 collective-permute-start.7
  24.5 2.9 %collective-permute-start.8 = (f32[8,24,128]{2,1,0:T(8,128)S(1)}, f32[8,24,128]{2,1,0:T(8,128)S(1)}, u32[]{:S(2)}, u32[]{:S(2)}) collective-permute-start(f32[8,24,128]{2,1,0:T(8,128)S(1)} %get-tuple-element.39), channel_id=1, source_target_pairs={{1,0},{2,1},{3,2},{4,3},{5,4},{6,5},{7,6},{0,7},{9,8},{10,9},{11,1... | collective-permute-start | bytes 294920 | tf_op jit(solution)/shard_map/ppermute | solution.py:430
  27.4 0.0 collective-permute-done.3.outer
  27.4 0.0 collective-permute-done.4.inner
  27.4 0.1 columns_on.1
  27.6 0.2 collective-permute-start.6
  27.8 0.3 collective-permute-start.5
  28.1 1.6 %collective-permute-done.8.after = f32[8,24,128]{2,1,0:T(8,128)S(1)} collective-permute-done((f32[8,24,128]{2,1,0:T(8,128)S(1)}, f32[8,24,128]{2,1,0:T(8,128)S(1)}, u32[]{:S(2)}, u32[]{:S(2)}) %collective-permute-start.8) | collective-permute-done | bytes 98336 | tf_op jit(solution)/shard_map/ppermute | solution.py:430
  29.6 0.2 collective-permute-done.7.before
  29.9 0.1 first_step.1
  30.0 2.4 %collective-permute-done.5.before = f32[72,128]{1,0:T(8,128)S(1)} collective-permute-done((f32[72,128]{1,0:T(8,128)S(1)}, f32[72,128]{1,0:T(8,128)S(1)}, u32[]{:S(2)}, u32[]{:S(2)}) %collective-permute-start.5) | collective-permute-done | bytes 36896 | tf_op jit(solution)/shard_map/ppermute | solution.py:432
  32.4 0.0 collective-permute-done.6.after
  32.4 1.3 %second_step.1 = (f32[3,4,16,128]{3,2,1,0:T(8,128)}, f32[3,4,16,128]{3,2,1,0:T(8,128)}, f32[3,4,16,128]{3,2,1,0:T(8,128)}, f32[3,4,16,128]{3,2,1,0:T(8,128)}) custom-call(f32[3,24,128]{2,1,0:T(8,128)S(1)} %get-tuple-element.34.own._, f32[3,24,128]{2,1,0:T(8,128)S(1)} %collective-permute-done.3.outer, f32[3,24,128]{2,1,0:T(8,128)S(1)} %collective-permute-done.4.inner, ...), custom_call_target="tpu_custom_call" | custom-call | flops 2000000 | bytes 1401344 | tf_op jit(solution)/shard_map/second_step/pallas_call | solution.py:370
  (2 shorter events, 0.0 us)
Async XLA Ops:
  1.8 16.3 %collective-permute-start.1 = (f32[72,128]{1,0:T(8,128)S(1)}, f32[72,128]{1,0:T(8,128)S(1)}, u32[]{:S(2)}, u32[]{:S(2)}) collective-permute-start(f32[72,128]{1,0:T(8,128)S(1)} %get-tuple-element.33.refs_6_.down), channel_id=1, source_target_pairs={{8,0},{16,8},{40,32},{48,40},{72,64},{80,72},{104,96},{112,104},{9... | collective-permute-start | bytes 110600 | tf_op jit(solution)/shard_map/ppermute | solution.py:401
  3.1 14.9 %collective-permute-start = (f32[64,128]{1,0:T(8,128)S(1)}, f32[64,128]{1,0:T(8,128)S(1)}, u32[]{:S(2)}, u32[]{:S(2)}) collective-permute-start(f32[64,128]{1,0:T(8,128)S(1)} %high_faces.1._), channel_id=1, source_target_pairs={{0,8},{8,16},{16,24},{24,32},{32,40},{40,48},{48,56},{56,64},{64,7... | collective-permute-start | bytes 98312 | tf_op jit(solution)/shard_map/ppermute | solution.py:403
  12.8 5.2 %collective-permute-start.2 = (f32[48,128]{1,0:T(8,128)S(1)}, f32[48,128]{1,0:T(8,128)S(1)}, u32[]{:S(2)}, u32[]{:S(2)}) collective-permute-start(f32[48,128]{1,0:T(8,128)S(1)} %again.1), channel_id=1, source_target_pairs={{24,16},{32,24},{56,48},{64,56},{88,80},{96,88},{120,112},{25,17},... | collective-permute-start | bytes 73736 | tf_op jit(solution)/shard_map/ppermute | solution.py:405
  18.3 9.2 %collective-permute-start.3 = (f32[3,24,128]{2,1,0:T(8,128)S(1)}, f32[3,24,128]{2,1,0:T(8,128)S(1)}, u32[]{:S(2)}, u32[]{:S(2)}) collective-permute-start(f32[3,24,128]{2,1,0:T(8,128)S(1)} %get-tuple-element.34.own._), channel_id=1, source_target_pairs={{0,128},{128,0},{256,384},{384,256},{1,129},{129,1},{257,385},{385... | collective-permute-start | bytes 110600 | tf_op jit(solution)/shard_map/ppermute | solution.py:415
  21.2 6.2 %collective-permute-start.4 = (f32[3,24,128]{2,1,0:T(8,128)S(1)}, f32[3,24,128]{2,1,0:T(8,128)S(1)}, u32[]{:S(2)}, u32[]{:S(2)}) collective-permute-start(f32[3,24,128]{2,1,0:T(8,128)S(1)} %get-tuple-element.34.own._), channel_id=1, source_target_pairs={{128,256},{256,128},{129,257},{257,129},{130,258},{258,130},{131,2... | collective-permute-start | bytes 110600 | tf_op jit(solution)/shard_map/ppermute | solution.py:416
  24.5 5.4 %collective-permute-start.7 = (f32[9,24,128]{2,1,0:T(8,128)S(1)}, f32[9,24,128]{2,1,0:T(8,128)S(1)}, u32[]{:S(2)}, u32[]{:S(2)}) collective-permute-start(f32[9,24,128]{2,1,0:T(8,128)S(1)} %get-tuple-element.38), channel_id=1, source_target_pairs={{0,1},{1,2},{2,3},{3,4},{4,5},{5,6},{6,7},{7,0},{8,9},{9,10},{10,1... | collective-permute-start | bytes 331784 | tf_op jit(solution)/shard_map/ppermute | solution.py:429
  24.5 5.2 %collective-permute-start.8 = (f32[8,24,128]{2,1,0:T(8,128)S(1)}, f32[8,24,128]{2,1,0:T(8,128)S(1)}, u32[]{:S(2)}, u32[]{:S(2)}) collective-permute-start(f32[8,24,128]{2,1,0:T(8,128)S(1)} %get-tuple-element.39), channel_id=1, source_target_pairs={{1,0},{2,1},{3,2},{4,3},{5,4},{6,5},{7,6},{0,7},{9,8},{10,9},{11,1... | collective-permute-start | bytes 294920 | tf_op jit(solution)/shard_map/ppermute | solution.py:430
  27.6 4.8 %collective-permute-start.6 = (f32[73,128]{1,0:T(8,128)S(1)}, f32[73,128]{1,0:T(8,128)S(1)}, u32[]{:S(2)}, u32[]{:S(2)}) collective-permute-start(f32[73,128]{1,0:T(8,128)S(1)} %get-tuple-element.36), channel_id=1, source_target_pairs={{1,0},{2,1},{3,2},{4,3},{5,4},{6,5},{7,6},{0,7},{9,8},{10,9},{11,1... | collective-permute-start | bytes 112136 | tf_op jit(solution)/shard_map/ppermute | solution.py:433
  27.8 4.6 %collective-permute-start.5 = (f32[72,128]{1,0:T(8,128)S(1)}, f32[72,128]{1,0:T(8,128)S(1)}, u32[]{:S(2)}, u32[]{:S(2)}) collective-permute-start(f32[72,128]{1,0:T(8,128)S(1)} %get-tuple-element.35), channel_id=1, source_target_pairs={{0,1},{1,2},{2,3},{3,4},{4,5},{5,6},{6,7},{7,0},{8,9},{9,10},{10,1... | collective-permute-start | bytes 110600 | tf_op jit(solution)/shard_map/ppermute | solution.py:432

commit v7 on v6

--- a/solution.py
+++ b/solution.py
@@ -68,12 +68,24 @@
         up[4 * i : 4 * i + 4, :] = y_face(near, c, row)
 
 
-def again(down, _, copy):
+def block_class():
+    return lax.axis_index("gy") % 4
+
+
+def last_faces(down, up, copy, mixed):
     copy[...] = down[0:48, :]
-
-
-def widen_rows(e, h, p, j, material, pml, before, after, later, wide, edges):
+    mixed[0:48, :] = jnp.where(block_class() == 2, up[0:48, :], down[0:48, :])
+    mixed[48:64, :] = up[48:64, :]
+
+
+def joined(after, later, before, rows_after, rows_before):
+    rows_after[...] = after[0:48, :] + later[...]
+    rows_before[...] = before[...]
+
+
+def widen_rows(e, h, p, j, material, pml, before, after, last, wide, edges):
     lane = lanes()
+    low, high = block_class() == 3, block_class() == 2
     for z in range(4):
         for c in EVERY:
             if c < HX:
@@ -87,10 +99,11 @@
             wide[z, c, 0:16, :] = own
             wide[z, c, 16:24, :] = jnp.zeros((8, 128), jnp.float32)
         for i, (c, row) in enumerate(Y_UP):
-            wide[z, c, row + 8 : row + 9, :] = before[4 * i + z : 4 * i + z + 1, :]
+            at = slice(4 * i + z, 4 * i + z + 1)
+            wide[z, c, row + 8 : row + 9, :] = jnp.where(low, last[at, :], before[at, :])
         for i, (c, row) in enumerate(Y_DOWN):
             at = slice(4 * i + z, 4 * i + z + 1)
-            wide[z, c, row + 16 : row + 17, :] = after[at, :] + later[at, :]
+            wide[z, c, row + 16 : row + 17, :] = jnp.where(high, last[at, :], after[at, :])
     for g in range(3):
         total = jnp.zeros((ROWS, 128), jnp.float32)
         for c in range(4 * g, min(4 * g + 4, 10)):
@@ -396,18 +409,25 @@
         far=True,
         name="load_and_low_faces",
     )
-    near = [(i, j) for i, j in down_of(gy) if i % 4 in (1, 2)]
-    rest = [(i, j) for i, j in down_of(gy) if i % 4 in (0, 3)]
-    after = lax.ppermute(down, "gy", near)
+    ups, downs = up_of(gy), down_of(gy)
+    after = lax.ppermute(down, "gy", [(i, j) for i, j in downs if i % 4 in (1, 2)])
     (up,) = call(high_faces, [f32(64, 128)], (*cells, down), size=HINT, name="high_faces")
-    before = lax.ppermute(up, "gy", up_of(gy))
-    (down,) = call(again, [f32(48, 128)], (down, up), size=HINT, name="again")
-    later = lax.ppermute(down, "gy", rest)
-
+    before = lax.ppermute(up, "gy", [(i, j) for i, j in ups if i % 4 != 2])
+    down, mixed = call(last_faces, [f32(48, 128), f32(64, 128)], (down, up), size=HINT, name="last_faces")
+    later = lax.ppermute(down, "gy", [(i, j) for i, j in downs if i % 4 == 0])
+    last = lax.ppermute(mixed, "gy", [(i, j) for i, j in ups if i % 4 == 2] + [(i, j) for i, j in downs if i % 4 == 3])
+    after, before = call(
+        joined,
+        [f32(48, 128), f32(64, 128)],
+        (after, later, before),
+        size=1 << 30,
+        flops=1 << 36,
+        name="joined",
+    )
     wide, own = call(
         widen_rows,
         [f32(4, 10, ROWS, 128), f32(3, ROWS, 128)],
-        (*cells, before, after, later),
+        (*cells, before, after, last),
         name="widen_rows",
     )
     pairs = [(i, i ^ 1) for i in range(gx) if i ^ 1 < gx]

time: 33.9 us -> 33.3 us (0.982)
  waiting for transfers between devices: 5.68 us -> 5.01 us
    ppermute x3 -> x4, waiting for transfers between devices: 1.51 us -> 0.84 us  [the longest x1 0.83 us: on_device(): later = lax.ppermute(down, 'gy', [(i, j) for i, j in downs if i % 4 == 0])]
    pallas_call x8 -> x9, Pallas kernels: 3.07 us -> 3.11 us  [call(): pl.pallas_call(kernel, out_shape=outs, in_specs=[HBM if far else VMEM] *...]
    ppermute x3 -> x4, starting transfers between devices: 14.7 us -> 14.7 us  [the longest x1 9.73 us: on_device(): before = lax.ppermute(up, 'gy', [(i, j) for i, j in ups if i % 4 != 2])]
  transfers between devices with their start and end apart: 9 -> 10, of which waited for: 4 -> 4; matrix products, arithmetic and copies ran while one was open for 0% -> 0% of each run, Pallas kernels for 1% -> 1%
where the time goes in v7:
time: 33.3 us; the launch traced here: 33.1 us
  starting transfers between devices  24.2 us (73%)
  waiting for transfers between devices  5.01 us (15%)
  Pallas kernels  3.11 us (9%)
  between operations  0.75 us (2%)
    ppermute x1, starting transfers between devices, on_device(): before = lax.ppermute(up, 'gy', [(i, j) for i, j in ups if i % 4 != 2])  9.73 us
    ppermute x1, starting transfers between devices, on_device(): inner = lax.ppermute(own, 'gx', between)  3.12 us
    pallas_call x9, Pallas kernels, call(): pl.pallas_call(kernel, out_shape=outs, in_specs=[HBM if far else VMEM] *...  3.11 us
    ppermute x1, starting transfers between devices, on_device(): later = lax.ppermute(down, 'gy', [(i, j) for i, j in downs if i % 4 == 0])  3.04 us
    ppermute x1, starting transfers between devices, on_device(): after = lax.ppermute(down, 'gz', ring_down)  2.94 us
    ppermute x1, starting transfers between devices, on_device(): outer = lax.ppermute(own, 'gx', pairs)  2.92 us
    ppermute x1, waiting for transfers between devices, on_device(): columns_before = lax.ppermute(up, 'gz', ring_up)  2.38 us
    ppermute x1, waiting for transfers between devices, on_device(): after = lax.ppermute(down, 'gz', ring_down)  1.57 us
  transfers between devices with their start and end apart: 10, of which 4 were waited for; matrix products, arithmetic and copies ran while one was open for 0% of the time, Pallas kernels for 1%

profile of v7, /device:TPU:38, one launch (start us, length us, event | category | flops | bytes accessed | tf_op | source)
XLA Modules:
  0.0 33.1 jit_solution(7223925613641156456)
XLA Ops:
  0.6 1.1 %load_and_low_faces.1 = (f32[3,4,16,128]{3,2,1,0:T(8,128)S(1)}, f32[3,4,16,128]{3,2,1,0:T(8,128)S(1)}, f32[3,4,16,128]{3,2,1,0:T(8,128)S(1)}, f32[3,4,16,128]{3,...) custom-call(f32[3,4,16,128]{3,2,1,0:T(8,128)} %refs_0_.1, ...), custom_call_target="tpu_custom_call" | custom-call | bytes 954368 | tf_op jit(solution)/shard_map/load_and_low_faces/pallas_call | solution.py:383
  1.8 1.3 %collective-permute-start = (f32[72,128]{1,0:T(8,128)S(1)}, f32[72,128]{1,0:T(8,128)S(1)}, u32[]{:S(2)}, u32[]{:S(2)}) collective-permute-start(f32[72,128]{1,0:T(8,128)S(1)} %get-tuple-element.37.refs_6_.down), channel_id=1, source_target_pairs={{8,0},{16,8},{40,32},{48,40},{72,64},{80,72},{104,96},{112,104},{9... | collective-permute-start | bytes 110600 | tf_op jit(solution)/shard_map/ppermute | solution.py:413
  3.1 9.7 %collective-permute-start.2 = (f32[64,128]{1,0:T(8,128)S(1)}, f32[64,128]{1,0:T(8,128)S(1)}, u32[]{:S(2)}, u32[]{:S(2)}) collective-permute-start(f32[64,128]{1,0:T(8,128)S(1)} %high_faces.1.up), channel_id=1, source_target_pairs={{0,8},{8,16},{24,32},{32,40},{40,48},{56,64},{64,72},{72,80},{88,9... | collective-permute-start | bytes 98312 | tf_op jit(solution)/shard_map/ppermute | solution.py:415
  12.9 3.0 %collective-permute-start.1 = (f32[48,128]{1,0:T(8,128)S(1)}, f32[48,128]{1,0:T(8,128)S(1)}, u32[]{:S(2)}, u32[]{:S(2)}) collective-permute-start(f32[48,128]{1,0:T(8,128)S(1)} %get-tuple-element.38), channel_id=1, source_target_pairs={{32,24},{64,56},{96,88},{33,25},{65,57},{97,89},{34,26},{66,58},{9... | collective-permute-start | bytes 73736 | tf_op jit(solution)/shard_map/ppermute | solution.py:417
  15.9 0.7 %collective-permute-start.3 = (f32[64,128]{1,0:T(8,128)S(1)}, f32[64,128]{1,0:T(8,128)S(1)}, u32[]{:S(2)}, u32[]{:S(2)}) collective-permute-start(f32[64,128]{1,0:T(8,128)S(1)} %get-tuple-element.41), channel_id=1, source_target_pairs={{16,24},{48,56},{80,88},{112,120},{24,16},{56,48},{88,80},{120,112... | collective-permute-start | bytes 98312 | tf_op jit(solution)/shard_map/ppermute | solution.py:418
  16.6 0.8 %collective-permute-done.1.later = f32[48,128]{1,0:T(8,128)S(1)} collective-permute-done((f32[48,128]{1,0:T(8,128)S(1)}, f32[48,128]{1,0:T(8,128)S(1)}, u32[]{:S(2)}, u32[]{:S(2)}) %collective-permute-start.1) | collective-permute-done | bytes 24608 | tf_op jit(solution)/shard_map/ppermute | solution.py:417
  17.4 0.0 collective-permute-done.2.before
  17.4 0.0 collective-permute-done.after
  17.4 0.0 collective-permute-done.3.last
  17.4 0.2 widen_rows.1
  17.7 2.9 %collective-permute-start.4 = (f32[3,24,128]{2,1,0:T(8,128)S(1)}, f32[3,24,128]{2,1,0:T(8,128)S(1)}, u32[]{:S(2)}, u32[]{:S(2)}) collective-permute-start(f32[3,24,128]{2,1,0:T(8,128)S(1)} %get-tuple-element.42.own._), channel_id=1, source_target_pairs={{0,128},{128,0},{256,384},{384,256},{1,129},{129,1},{257,385},{385... | collective-permute-start | bytes 110600 | tf_op jit(solution)/shard_map/ppermute | solution.py:435
  20.6 3.1 %collective-permute-start.5 = (f32[3,24,128]{2,1,0:T(8,128)S(1)}, f32[3,24,128]{2,1,0:T(8,128)S(1)}, u32[]{:S(2)}, u32[]{:S(2)}) collective-permute-start(f32[3,24,128]{2,1,0:T(8,128)S(1)} %get-tuple-element.42.own._), channel_id=1, source_target_pairs={{128,256},{256,128},{129,257},{257,129},{130,258},{258,130},{131,2... | collective-permute-start | bytes 110600 | tf_op jit(solution)/shard_map/ppermute | solution.py:436
  23.7 0.1 z_faces.1
  23.9 0.0 collective-permute-start.8
  23.9 2.9 %collective-permute-start.9 = (f32[8,24,128]{2,1,0:T(8,128)S(1)}, f32[8,24,128]{2,1,0:T(8,128)S(1)}, u32[]{:S(2)}, u32[]{:S(2)}) collective-permute-start(f32[8,24,128]{2,1,0:T(8,128)S(1)} %get-tuple-element.47), channel_id=1, source_target_pairs={{1,0},{2,1},{3,2},{4,3},{5,4},{6,5},{7,6},{0,7},{9,8},{10,9},{11,1... | collective-permute-start | bytes 294920 | tf_op jit(solution)/shard_map/ppermute | solution.py:450
  26.8 0.0 collective-permute-done.4.outer
  26.8 0.0 collective-permute-done.5.inner
  26.8 0.1 columns_on.1
  27.0 0.2 collective-permute-start.7
  27.2 0.3 collective-permute-start.6
  27.5 1.6 %collective-permute-done.9.after = f32[8,24,128]{2,1,0:T(8,128)S(1)} collective-permute-done((f32[8,24,128]{2,1,0:T(8,128)S(1)}, f32[8,24,128]{2,1,0:T(8,128)S(1)}, u32[]{:S(2)}, u32[]{:S(2)}) %collective-permute-start.9) | collective-permute-done | bytes 98336 | tf_op jit(solution)/shard_map/ppermute | solution.py:450
  29.1 0.2 collective-permute-done.8.before
  29.3 0.1 first_step.1
  29.4 2.4 %collective-permute-done.6.before = f32[72,128]{1,0:T(8,128)S(1)} collective-permute-done((f32[72,128]{1,0:T(8,128)S(1)}, f32[72,128]{1,0:T(8,128)S(1)}, u32[]{:S(2)}, u32[]{:S(2)}) %collective-permute-start.6) | collective-permute-done | bytes 36896 | tf_op jit(solution)/shard_map/ppermute | solution.py:452
  31.8 0.0 collective-permute-done.7.after
  31.8 1.3 %second_step.1 = (f32[3,4,16,128]{3,2,1,0:T(8,128)}, f32[3,4,16,128]{3,2,1,0:T(8,128)}, f32[3,4,16,128]{3,2,1,0:T(8,128)}, f32[3,4,16,128]{3,2,1,0:T(8,128)}) custom-call(f32[3,24,128]{2,1,0:T(8,128)S(1)} %get-tuple-element.42.own._, f32[3,24,128]{2,1,0:T(8,128)S(1)} %collective-permute-done.4.outer, f32[3,24,128]{2,1,0:T(8,128)S(1)} %collective-permute-done.5.inner, ...), custom_call_target="tpu_custom_call" | custom-call | flops 2000000 | bytes 1401344 | tf_op jit(solution)/shard_map/second_step/pallas_call | solution.py:383
  (3 shorter events, 0.1 us)
Async XLA Ops:
  1.8 15.7 %collective-permute-start = (f32[72,128]{1,0:T(8,128)S(1)}, f32[72,128]{1,0:T(8,128)S(1)}, u32[]{:S(2)}, u32[]{:S(2)}) collective-permute-start(f32[72,128]{1,0:T(8,128)S(1)} %get-tuple-element.37.refs_6_.down), channel_id=1, source_target_pairs={{8,0},{16,8},{40,32},{48,40},{72,64},{80,72},{104,96},{112,104},{9... | collective-permute-start | bytes 110600 | tf_op jit(solution)/shard_map/ppermute | solution.py:413
  3.1 14.3 %collective-permute-start.2 = (f32[64,128]{1,0:T(8,128)S(1)}, f32[64,128]{1,0:T(8,128)S(1)}, u32[]{:S(2)}, u32[]{:S(2)}) collective-permute-start(f32[64,128]{1,0:T(8,128)S(1)} %high_faces.1.up), channel_id=1, source_target_pairs={{0,8},{8,16},{24,32},{32,40},{40,48},{56,64},{64,72},{72,80},{88,9... | collective-permute-start | bytes 98312 | tf_op jit(solution)/shard_map/ppermute | solution.py:415
  12.9 4.5 %collective-permute-start.1 = (f32[48,128]{1,0:T(8,128)S(1)}, f32[48,128]{1,0:T(8,128)S(1)}, u32[]{:S(2)}, u32[]{:S(2)}) collective-permute-start(f32[48,128]{1,0:T(8,128)S(1)} %get-tuple-element.38), channel_id=1, source_target_pairs={{32,24},{64,56},{96,88},{33,25},{65,57},{97,89},{34,26},{66,58},{9... | collective-permute-start | bytes 73736 | tf_op jit(solution)/shard_map/ppermute | solution.py:417
  15.9 1.5 %collective-permute-start.3 = (f32[64,128]{1,0:T(8,128)S(1)}, f32[64,128]{1,0:T(8,128)S(1)}, u32[]{:S(2)}, u32[]{:S(2)}) collective-permute-start(f32[64,128]{1,0:T(8,128)S(1)} %get-tuple-element.41), channel_id=1, source_target_pairs={{16,24},{48,56},{80,88},{112,120},{24,16},{56,48},{88,80},{120,112... | collective-permute-start | bytes 98312 | tf_op jit(solution)/shard_map/ppermute | solution.py:418
  17.7 9.2 %collective-permute-start.4 = (f32[3,24,128]{2,1,0:T(8,128)S(1)}, f32[3,24,128]{2,1,0:T(8,128)S(1)}, u32[]{:S(2)}, u32[]{:S(2)}) collective-permute-start(f32[3,24,128]{2,1,0:T(8,128)S(1)} %get-tuple-element.42.own._), channel_id=1, source_target_pairs={{0,128},{128,0},{256,384},{384,256},{1,129},{129,1},{257,385},{385... | collective-permute-start | bytes 110600 | tf_op jit(solution)/shard_map/ppermute | solution.py:435
  20.6 6.2 %collective-permute-start.5 = (f32[3,24,128]{2,1,0:T(8,128)S(1)}, f32[3,24,128]{2,1,0:T(8,128)S(1)}, u32[]{:S(2)}, u32[]{:S(2)}) collective-permute-start(f32[3,24,128]{2,1,0:T(8,128)S(1)} %get-tuple-element.42.own._), channel_id=1, source_target_pairs={{128,256},{256,128},{129,257},{257,129},{130,258},{258,130},{131,2... | collective-permute-start | bytes 110600 | tf_op jit(solution)/shard_map/ppermute | solution.py:436
  23.9 5.4 %collective-permute-start.8 = (f32[9,24,128]{2,1,0:T(8,128)S(1)}, f32[9,24,128]{2,1,0:T(8,128)S(1)}, u32[]{:S(2)}, u32[]{:S(2)}) collective-permute-start(f32[9,24,128]{2,1,0:T(8,128)S(1)} %get-tuple-element.46), channel_id=1, source_target_pairs={{0,1},{1,2},{2,3},{3,4},{4,5},{5,6},{6,7},{7,0},{8,9},{9,10},{10,1... | collective-permute-start | bytes 331784 | tf_op jit(solution)/shard_map/ppermute | solution.py:449
  23.9 5.2 %collective-permute-start.9 = (f32[8,24,128]{2,1,0:T(8,128)S(1)}, f32[8,24,128]{2,1,0:T(8,128)S(1)}, u32[]{:S(2)}, u32[]{:S(2)}) collective-permute-start(f32[8,24,128]{2,1,0:T(8,128)S(1)} %get-tuple-element.47), channel_id=1, source_target_pairs={{1,0},{2,1},{3,2},{4,3},{5,4},{6,5},{7,6},{0,7},{9,8},{10,9},{11,1... | collective-permute-start | bytes 294920 | tf_op jit(solution)/shard_map/ppermute | solution.py:450
  27.0 4.8 %collective-permute-start.7 = (f32[73,128]{1,0:T(8,128)S(1)}, f32[73,128]{1,0:T(8,128)S(1)}, u32[]{:S(2)}, u32[]{:S(2)}) collective-permute-start(f32[73,128]{1,0:T(8,128)S(1)} %get-tuple-element.44), channel_id=1, source_target_pairs={{1,0},{2,1},{3,2},{4,3},{5,4},{6,5},{7,6},{0,7},{9,8},{10,9},{11,1... | collective-permute-start | bytes 112136 | tf_op jit(solution)/shard_map/ppermute | solution.py:453
  27.2 4.6 %collective-permute-start.6 = (f32[72,128]{1,0:T(8,128)S(1)}, f32[72,128]{1,0:T(8,128)S(1)}, u32[]{:S(2)}, u32[]{:S(2)}) collective-permute-start(f32[72,128]{1,0:T(8,128)S(1)} %get-tuple-element.43), channel_id=1, source_target_pairs={{0,1},{1,2},{2,3},{3,4},{4,5},{5,6},{6,7},{7,0},{8,9},{9,10},{10,1... | collective-permute-start | bytes 110600 | tf_op jit(solution)/shard_map/ppermute | solution.py:452

commit v8 on v7

--- a/solution.py
+++ b/solution.py
@@ -24,7 +24,6 @@
 
 ROWS = 24
 SPAN = 32
-HINT = 1 << 26
 
 
 def up_of(n):
@@ -50,32 +49,30 @@
     return code_of(material[:, row, :], pml[:, row, :])
 
 
-def load_and_low_faces(*refs):
-    far, near, down, done = refs[:6], refs[6:12], refs[12], refs[13]
+def block_class():
+    return lax.axis_index("gy") % 4
+
+
+def load_and_faces(*refs):
+    far, near, (down, up, late, mixed), done = refs[:6], refs[6:12], refs[12:16], refs[16]
     copies = [pltpu.make_async_copy(a, b, done.at[i]) for i, (a, b) in enumerate(zip(far, near))]
     for copy in copies:
         copy.start()
     for copy in copies:
         copy.wait()
+    is_up = block_class() == 2
     down[...] = jnp.zeros_like(down)
-    for i, (c, row) in enumerate(Y_DOWN):
-        down[4 * i : 4 * i + 4, :] = y_face(near, c, row)
-
-
-def high_faces(*refs):
-    near, _, up = refs[:6], refs[6], refs[7]
+    late[...] = jnp.zeros_like(late)
     for i, (c, row) in enumerate(Y_UP):
-        up[4 * i : 4 * i + 4, :] = y_face(near, c, row)
-
-
-def block_class():
-    return lax.axis_index("gy") % 4
-
-
-def last_faces(down, up, copy, mixed):
-    copy[...] = down[0:48, :]
-    mixed[0:48, :] = jnp.where(block_class() == 2, up[0:48, :], down[0:48, :])
-    mixed[48:64, :] = up[48:64, :]
+        value = y_face(near, c, row)
+        at = slice(4 * i, 4 * i + 4)
+        up[at, :] = value
+        if i < len(Y_DOWN):
+            low = y_face(near, *Y_DOWN[i])
+            down[at, :] = low
+            late[at, :] = low
+            value = jnp.where(is_up, value, low)
+        mixed[at, :] = value
 
 
 def joined(after, later, before, rows_after, rows_before):
@@ -83,43 +80,69 @@
     rows_before[...] = before[...]
 
 
-def widen_rows(e, h, p, j, material, pml, before, after, last, wide, edges):
-    lane = lanes()
+def own_value(cells, c, z):
+    e, h, p, j, material, pml = cells
+    if c < HX:
+        return e[c, z]
+    if c < QX:
+        return h[c - HX, z]
+    if c < CODE:
+        return HOLD * j[c - QX, z] - PULL * p[c - QX, z]
+    return code_of(material[z], pml[z])
+
+
+def edge_columns(value, g, rows):
+    lane = lax.broadcasted_iota(jnp.int32, (rows, 128), 1)
+    total = jnp.zeros((rows, 128), jnp.float32)
+    for c in range(4 * g, min(4 * g + 4, 10)):
+        for z in range(4):
+            at = SPAN * (c - 4 * g) + 4 * (z + 2)
+            total = jnp.where((lane >= at) & (lane < at + 4), roll(value(c, z), at - 126, 1), total)
+    return total
+
+
+def own_planes(*refs):
+    cells, (planes, edges, p1, j1, fe) = refs[:6], refs[6:]
+    for z in range(4):
+        _, _, keep_e, push_e, metal = factors(own_value(cells, CODE, z))
+        for k, f in enumerate((keep_e, push_e, metal)):
+            fe[z, k] = f
+        for k in range(3):
+            flow = own_value(cells, QX + k, z) + GAIN * metal * cells[0][k, z]
+            j1[k, z] = flow
+            p1[k, z] = cells[2][k, z] + time_step * flow
+        for c in EVERY:
+            planes[z, c] = own_value(cells, c, z)
+    for g in range(3):
+        edges[g] = edge_columns(lambda c, z: own_value(cells, c, z), g, 16)
+
+
+def widen_rows(before, after, last, own, beside, edges):
     low, high = block_class() == 3, block_class() == 2
+    beside[...] = jnp.zeros_like(beside)
     for z in range(4):
-        for c in EVERY:
-            if c < HX:
-                own = e[c, z]
-            elif c < QX:
-                own = h[c - HX, z]
-            elif c < CODE:
-                own = HOLD * j[c - QX, z] - PULL * p[c - QX, z]
-            else:
-                own = code_of(material[z], pml[z])
-            wide[z, c, 0:16, :] = own
-            wide[z, c, 16:24, :] = jnp.zeros((8, 128), jnp.float32)
         for i, (c, row) in enumerate(Y_UP):
             at = slice(4 * i + z, 4 * i + z + 1)
-            wide[z, c, row + 8 : row + 9, :] = jnp.where(low, last[at, :], before[at, :])
+            beside[z, c, row - 8 : row - 7, :] = jnp.where(low, last[at, :], before[at, :])
         for i, (c, row) in enumerate(Y_DOWN):
             at = slice(4 * i + z, 4 * i + z + 1)
-            wide[z, c, row + 16 : row + 17, :] = jnp.where(high, last[at, :], after[at, :])
+            beside[z, c, row : row + 1, :] = jnp.where(high, last[at, :], after[at, :])
     for g in range(3):
-        total = jnp.zeros((ROWS, 128), jnp.float32)
-        for c in range(4 * g, min(4 * g + 4, 10)):
-            for z in range(4):
-                at = SPAN * (c - 4 * g) + 4 * (z + 2)
-                moved = roll(wide[z, c], at - 126, 1)
-                total = jnp.where((lane >= at) & (lane < at + 4), moved, total)
-        edges[g] = total
-
-
-def z_faces(wide, polar, _, up, down, h1, r1, p1, j1, fh, fe, push):
+        edges[g, 0:16, :] = own[g]
+        edges[g, 16:24, :] = edge_columns(lambda c, z: beside[z, c], g, 8)
+
+
+def widened(planes, beside, z, c):
+    return jnp.concatenate([planes[z, c], beside[z, c]])
+
+
+def z_faces(planes, beside, _, up, down, h1, r1, fh, push):
+    wide = [[widened(planes, beside, z, c) for c in EVERY] for z in range(4)]
     for z in range(4):
-        e = [wide[z, EX + k] for k in range(3)]
-        h = [wide[z, HX + k] for k in range(3)]
-        keep_h, push_h, keep_e, push_e, metal = factors(wide[z, CODE])
-        later = [wide[z + 1, EX + k] for k in range(2)] if z < 3 else [0.0, 0.0]
+        e = wide[z][EX : EZ + 1]
+        h = wide[z][HX : HZ + 1]
+        keep_h, push_h, keep_e, push_e, metal = factors(wide[z][CODE])
+        later = [wide[z + 1][EX + k] for k in range(2)] if z < 3 else [0.0, 0.0]
         new = magnetic_new(
             h,
             e,
@@ -129,26 +152,22 @@
             keep_h,
             push_h,
         )
-        flow = [wide[z, QX + k] + GAIN * metal * e[k] for k in range(3)]
+        flow = [wide[z][QX + k] + GAIN * metal * e[k] for k in range(3)]
         rest = [keep_e * e[k] - push_e * (metal * flow[k]) for k in range(3)]
         for k in range(3):
             h1[z, k] = new[k]
             r1[z, k] = rest[k]
-            j1[k, z] = flow[k][0:16]
-            p1[k, z] = polar[k, z] + time_step * flow[k][0:16]
         fh[z, 0] = keep_h
         fh[z, 1] = push_h
         push[z] = push_e
-        for k, f in enumerate((keep_e, push_e, metal)):
-            fe[z, k] = f[0:16]
         if z == 0:
-            for i, value in enumerate(new + rest[:2] + [wide[z, CODE]] + e[:2]):
+            for i, value in enumerate(new + rest[:2] + [wide[z][CODE]] + e[:2]):
                 down[i] = value
         if z == 2:
             up[7] = new[0]
             up[8] = new[1]
         if z == 3:
-            for i, value in enumerate(new + rest + [wide[z, CODE]]):
+            for i, value in enumerate(new + rest + [wide[z][CODE]]):
                 up[i] = value
 
 
@@ -230,7 +249,7 @@
 y_back = lambda a: roll(a, 1, 0)
 
 
-def first_step(wide, before, after, part, r1, fh, push, h1, e1, low):
+def first_step(planes, beside, before, after, part, r1, fh, push, h1, e1, low):
     first, last = grid_ends()
 
     def from_below(i):
@@ -255,7 +274,7 @@
     keep_h, push_h, _, push_e, _ = factors(from_below(6))
     low[0] = keep_h
     low[1] = push_h
-    h = with_next([from_below(k) for k in range(3)], push_h, wide[0, EX], wide[0, EY])
+    h = with_next([from_below(k) for k in range(3)], push_h, widened(planes, beside, 0, EX), widened(planes, beside, 0, EY))
     electric(-1, [from_below(3 + k) for k in range(3)], push_e, h, [from_below(7), from_below(8)])
     for z in range(4):
         for k in range(3):
@@ -300,7 +319,7 @@
 
 
 def second_step(own, outer, inner, before, after, h1, e1, low, p1, j1, fh, fe, *rest):
-    outs, near, h2, done = rest[:4], rest[4:8], rest[8], rest[9]
+    outs, near, h2, fixed, done = rest[:4], rest[4:8], rest[8], rest[9], rest[10]
     e_near, h_near, p_near, j_near = near
     lane = lanes()
     ch1, ce1, ch2 = columns(own, outer, inner, before, after)
@@ -323,19 +342,22 @@
     def fixed_e(z):
         return [put_right(e1[z + 1, k], z, ends_e[k]) for k in range(3 if z < 4 else 2)]
 
+    for z in range(-1, 5):
+        for k, a in enumerate(fixed_e(z)):
+            fixed[z + 1, k] = a
     copies = [pltpu.make_async_copy(a, b, done.at[i]) for i, (a, b) in enumerate(zip(near, outs))]
     for z in range(4):
         metal = fe[z, 2]
         for k in range(3):
-            e = put_right(e1[z + 1, k], z, ends_e[k])[0:16]
+            e = fixed[z + 1, k, 0:16, :]
             flow = HOLD * j1[k, z] - PULL * p1[k, z] + GAIN * metal * e
             j_near[k, z] = flow
             p_near[k, z] = p1[k, z] + time_step * flow
     copies[2].start()
     copies[3].start()
-    e = fixed_e(-1)
+    e = [fixed[0, k] for k in range(3)]
     for z in range(-1, 4):
-        up = fixed_e(z + 1)
+        up = [fixed[z + 2, k] for k in range(3 if z < 3 else 2)]
         h = [h1[z + 1, 0]] + [put_right(h1[z + 1, k], z, ends_h[k]) for k in (1, 2)]
         x = after_x(e, z)
         new = magnetic_new(
@@ -358,7 +380,7 @@
         down = [h2[z, k] for k in range(2)]
         x = before_x(h, z)
         new = electric_new(
-            [a[0:16] for a in fixed_e(z)],
+            [fixed[z + 1, k, 0:16, :] for k in range(3)],
             [a[0:16] for a in h],
             {0: y_back(h[0])[0:16], 2: y_back(h[2])[0:16]},
             {0: down[0][0:16], 1: down[1][0:16]},
@@ -401,20 +423,18 @@
     gx, gy, gz = (lax.axis_size(a) for a in ("gx", "gy", "gz"))
     shapes = [jax.ShapeDtypeStruct(a.shape, a.dtype) for a in cells]
     cells = [pltpu.with_memory_space_constraint(a, pltpu.HBM) for a in cells]
-    *cells, down = call(
-        load_and_low_faces,
-        [*shapes, f32(72, 128)],
+    *cells, down, up, late, mixed = call(
+        load_and_faces,
+        [*shapes, f32(72, 128), f32(64, 128), f32(48, 128), f32(64, 128)],
         cells,
         scratch=[pltpu.SemaphoreType.DMA((6,))],
         far=True,
-        name="load_and_low_faces",
+        name="load_and_faces",
     )
     ups, downs = up_of(gy), down_of(gy)
     after = lax.ppermute(down, "gy", [(i, j) for i, j in downs if i % 4 in (1, 2)])
-    (up,) = call(high_faces, [f32(64, 128)], (*cells, down), size=HINT, name="high_faces")
     before = lax.ppermute(up, "gy", [(i, j) for i, j in ups if i % 4 != 2])
-    down, mixed = call(last_faces, [f32(48, 128), f32(64, 128)], (down, up), size=HINT, name="last_faces")
-    later = lax.ppermute(down, "gy", [(i, j) for i, j in downs if i % 4 == 0])
+    later = lax.ppermute(late, "gy", [(i, j) for i, j in downs if i % 4 == 0])
     last = lax.ppermute(mixed, "gy", [(i, j) for i, j in ups if i % 4 == 2] + [(i, j) for i, j in downs if i % 4 == 3])
     after, before = call(
         joined,
@@ -424,10 +444,17 @@
         flops=1 << 36,
         name="joined",
     )
-    wide, own = call(
+    brick, plane = f32(3, 4, 16, 128), (ROWS, 128)
+    planes, own, p1, j1, fe = call(
+        own_planes,
+        [f32(4, 10, 16, 128), f32(3, 16, 128), brick, brick, f32(4, 3, 16, 128)],
+        cells,
+        name="own_planes",
+    )
+    beside, own = call(
         widen_rows,
-        [f32(4, 10, ROWS, 128), f32(3, ROWS, 128)],
-        (*cells, before, after, last),
+        [f32(4, 10, 8, 128), f32(3, *plane)],
+        (before, after, last, own),
         name="widen_rows",
     )
     pairs = [(i, i ^ 1) for i in range(gx) if i ^ 1 < gx]
@@ -437,12 +464,11 @@
 
     ring_up = [(i, (i + 1) % gz) for i in range(gz)]
     ring_down = [((i + 1) % gz, i) for i in range(gz)]
-    brick, plane = f32(3, 4, 16, 128), (ROWS, 128)
-    up, down, h1, r1, p1, j1, fh, fe, push = call(
+    up, down, h1, r1, fh, push = call(
         z_faces,
-        [f32(Z_UP, *plane), f32(Z_DOWN, *plane), f32(4, 3, *plane), f32(4, 3, *plane), brick, brick]
-        + [f32(4, 2, *plane), f32(4, 3, 16, 128), f32(4, *plane)],
-        (wide, cells[2], own),
+        [f32(Z_UP, *plane), f32(Z_DOWN, *plane), f32(4, 3, *plane), f32(4, 3, *plane)]
+        + [f32(4, 2, *plane), f32(4, *plane)],
+        (planes, beside, own),
         flops=1_000_000,
         name="z_faces",
     )
@@ -455,7 +481,7 @@
     h1, e1, low = call(
         first_step,
         [f32(5, 3, *plane), f32(6, 3, *plane), f32(2, *plane)],
-        (wide, before, after, h1, r1, fh, push),
+        (planes, beside, before, after, h1, r1, fh, push),
         flops=1_000_000,
         name="first_step",
     )
@@ -465,7 +491,7 @@
             [brick] * 4,
             (own, outer, inner, columns_before, columns_after, h1, e1, low, p1, j1, fh, fe),
             scratch=[pltpu.VMEM((3, 4, 16, 128), jnp.float32)] * 4
-            + [pltpu.VMEM((5, 3, ROWS, 128), jnp.float32), pltpu.SemaphoreType.DMA((4,))],
+            + [pltpu.VMEM((5, 3, ROWS, 128), jnp.float32), pltpu.VMEM((6, 3, ROWS, 128), jnp.float32), pltpu.SemaphoreType.DMA((4,))],
             far_out=True,
             flops=2_000_000,
             name="second_step",

time: 33.3 us -> 33.2 us (level)
    pallas_call x9 -> x8, Pallas kernels: 3.11 us -> 3.14 us  [call(): pl.pallas_call(kernel, out_shape=outs, in_specs=[HBM if far else VMEM] *...]
  transfers between devices with their start and end apart: 10 -> 10, of which waited for: 4 -> 4; matrix products, arithmetic and copies ran while one was open for 0% -> 0% of each run, Pallas kernels for 1% -> 2%
where the time goes in v8:
time: 33.2 us; the launch traced here: 33 us
  starting transfers between devices  24.3 us (73%)
  waiting for transfers between devices  4.84 us (15%)
  Pallas kernels  3.14 us (9%)
  between operations  0.74 us (2%)
    ppermute x1, starting transfers between devices, on_device(): before = lax.ppermute(up, 'gy', [(i, j) for i, j in ups if i % 4 != 2])  9.73 us
    pallas_call x8, Pallas kernels, call(): pl.pallas_call(kernel, out_shape=outs, in_specs=[HBM if far else VMEM] *...  3.14 us
    ppermute x1, starting transfers between devices, on_device(): inner = lax.ppermute(own, 'gx', between)  3.14 us
    ppermute x1, starting transfers between devices, on_device(): later = lax.ppermute(late, 'gy', [(i, j) for i, j in downs if i % 4 == 0])  3.04 us
    ppermute x1, starting transfers between devices, on_device(): after = lax.ppermute(down, 'gz', ring_down)  2.94 us
    ppermute x1, starting transfers between devices, on_device(): outer = lax.ppermute(own, 'gx', pairs)  2.92 us
    ppermute x1, waiting for transfers between devices, on_device(): columns_before = lax.ppermute(up, 'gz', ring_up)  2.38 us
    ppermute x1, waiting for transfers between devices, on_device(): after = lax.ppermute(down, 'gz', ring_down)  1.57 us
  transfers between devices with their start and end apart: 10, of which 4 were waited for; matrix products, arithmetic and copies ran while one was open for 0% of the time, Pallas kernels for 2%

profile of v8, /device:TPU:38, one launch (start us, length us, event | category | flops | bytes accessed | tf_op | source)
XLA Modules:
  0.0 33.0 jit_solution(17723004742003911480)
XLA Ops:
  0.6 1.2 %load_and_faces.1 = (f32[3,4,16,128]{3,2,1,0:T(8,128)S(1)}, f32[3,4,16,128]{3,2,1,0:T(8,128)S(1)}, f32[3,4,16,128]{3,2,1,0:T(8,128)S(1)}, f32[3,4,16,128]{3,2,1,...) custom-call(f32[3,4,16,128]{3,2,1,0:T(8,128)} %refs_0_.1, ...), custom_call_target="tpu_custom_call" | custom-call | bytes 1044480 | tf_op jit(solution)/shard_map/load_and_faces/pallas_call | solution.py:405
  1.8 1.3 %collective-permute-start = (f32[72,128]{1,0:T(8,128)S(1)}, f32[72,128]{1,0:T(8,128)S(1)}, u32[]{:S(2)}, u32[]{:S(2)}) collective-permute-start(f32[72,128]{1,0:T(8,128)S(1)} %get-tuple-element.34), channel_id=1, source_target_pairs={{8,0},{16,8},{40,32},{48,40},{72,64},{80,72},{104,96},{112,104},{9... | collective-permute-start | bytes 110600 | tf_op jit(solution)/shard_map/ppermute | solution.py:435
  3.1 9.7 %collective-permute-start.2 = (f32[64,128]{1,0:T(8,128)S(1)}, f32[64,128]{1,0:T(8,128)S(1)}, u32[]{:S(2)}, u32[]{:S(2)}) collective-permute-start(f32[64,128]{1,0:T(8,128)S(1)} %get-tuple-element.36), channel_id=1, source_target_pairs={{0,8},{8,16},{24,32},{32,40},{40,48},{56,64},{64,72},{72,80},{88,9... | collective-permute-start | bytes 98312 | tf_op jit(solution)/shard_map/ppermute | solution.py:436
  12.8 3.0 %collective-permute-start.1 = (f32[48,128]{1,0:T(8,128)S(1)}, f32[48,128]{1,0:T(8,128)S(1)}, u32[]{:S(2)}, u32[]{:S(2)}) collective-permute-start(f32[48,128]{1,0:T(8,128)S(1)} %get-tuple-element.35), channel_id=1, source_target_pairs={{32,24},{64,56},{96,88},{33,25},{65,57},{97,89},{34,26},{66,58},{9... | collective-permute-start | bytes 73736 | tf_op jit(solution)/shard_map/ppermute | solution.py:437
  15.9 0.7 %collective-permute-start.3 = (f32[64,128]{1,0:T(8,128)S(1)}, f32[64,128]{1,0:T(8,128)S(1)}, u32[]{:S(2)}, u32[]{:S(2)}) collective-permute-start(f32[64,128]{1,0:T(8,128)S(1)} %get-tuple-element.39), channel_id=1, source_target_pairs={{16,24},{48,56},{80,88},{112,120},{24,16},{56,48},{88,80},{120,112... | collective-permute-start | bytes 98312 | tf_op jit(solution)/shard_map/ppermute | solution.py:438
  16.5 0.2 own_planes.1
  16.7 0.7 %collective-permute-done.1.later = f32[48,128]{1,0:T(8,128)S(1)} collective-permute-done((f32[48,128]{1,0:T(8,128)S(1)}, f32[48,128]{1,0:T(8,128)S(1)}, u32[]{:S(2)}, u32[]{:S(2)}) %collective-permute-start.1) | collective-permute-done | bytes 24608 | tf_op jit(solution)/shard_map/ppermute | solution.py:437
  17.4 0.0 collective-permute-done.2.before
  17.4 0.0 collective-permute-done.after
  17.4 0.0 collective-permute-done.3.last
  17.4 0.2 widen_rows.1
  17.6 2.9 %collective-permute-start.4 = (f32[3,24,128]{2,1,0:T(8,128)S(1)}, f32[3,24,128]{2,1,0:T(8,128)S(1)}, u32[]{:S(2)}, u32[]{:S(2)}) collective-permute-start(f32[3,24,128]{2,1,0:T(8,128)S(1)} %get-tuple-element.47.own._), channel_id=1, source_target_pairs={{0,128},{128,0},{256,384},{384,256},{1,129},{129,1},{257,385},{385... | collective-permute-start | bytes 110600 | tf_op jit(solution)/shard_map/ppermute | solution.py:462
  20.5 3.1 %collective-permute-start.5 = (f32[3,24,128]{2,1,0:T(8,128)S(1)}, f32[3,24,128]{2,1,0:T(8,128)S(1)}, u32[]{:S(2)}, u32[]{:S(2)}) collective-permute-start(f32[3,24,128]{2,1,0:T(8,128)S(1)} %get-tuple-element.47.own._), channel_id=1, source_target_pairs={{128,256},{256,128},{129,257},{257,129},{130,258},{258,130},{131,2... | collective-permute-start | bytes 110600 | tf_op jit(solution)/shard_map/ppermute | solution.py:463
  23.6 0.1 z_faces.1
  23.8 0.0 collective-permute-start.8
  23.8 2.9 %collective-permute-start.9 = (f32[8,24,128]{2,1,0:T(8,128)S(1)}, f32[8,24,128]{2,1,0:T(8,128)S(1)}, u32[]{:S(2)}, u32[]{:S(2)}) collective-permute-start(f32[8,24,128]{2,1,0:T(8,128)S(1)} %get-tuple-element.53), channel_id=1, source_target_pairs={{1,0},{2,1},{3,2},{4,3},{5,4},{6,5},{7,6},{0,7},{9,8},{10,9},{11,1... | collective-permute-start | bytes 294920 | tf_op jit(solution)/shard_map/ppermute | solution.py:476
  26.7 0.0 collective-permute-done.4.outer
  26.7 0.0 collective-permute-done.5.inner
  26.8 0.1 columns_on.1
  26.9 0.2 collective-permute-start.7
  27.1 0.3 collective-permute-start.6
  27.4 1.6 %collective-permute-done.9.after = f32[8,24,128]{2,1,0:T(8,128)S(1)} collective-permute-done((f32[8,24,128]{2,1,0:T(8,128)S(1)}, f32[8,24,128]{2,1,0:T(8,128)S(1)}, u32[]{:S(2)}, u32[]{:S(2)}) %collective-permute-start.9) | collective-permute-done | bytes 98336 | tf_op jit(solution)/shard_map/ppermute | solution.py:476
  29.0 0.2 collective-permute-done.8.before
  29.2 0.1 first_step.1
  29.3 2.4 %collective-permute-done.6.before = f32[72,128]{1,0:T(8,128)S(1)} collective-permute-done((f32[72,128]{1,0:T(8,128)S(1)}, f32[72,128]{1,0:T(8,128)S(1)}, u32[]{:S(2)}, u32[]{:S(2)}) %collective-permute-start.6) | collective-permute-done | bytes 36896 | tf_op jit(solution)/shard_map/ppermute | solution.py:478
  31.7 0.0 collective-permute-done.7.after
  31.7 1.3 %second_step.1 = (f32[3,4,16,128]{3,2,1,0:T(8,128)}, f32[3,4,16,128]{3,2,1,0:T(8,128)}, f32[3,4,16,128]{3,2,1,0:T(8,128)}, f32[3,4,16,128]{3,2,1,0:T(8,128)}) custom-call(f32[3,24,128]{2,1,0:T(8,128)S(1)} %get-tuple-element.47.own._, f32[3,24,128]{2,1,0:T(8,128)S(1)} %collective-permute-done.4.outer, f32[3,24,128]{2,1,0:T(8,128)S(1)} %collective-permute-done.5.inner, ...), custom_call_target="tpu_custom_call" | custom-call | flops 2000000 | bytes 1401344 | tf_op jit(solution)/shard_map/second_step/pallas_call | solution.py:405
  (1 shorter events, 0.0 us)
Async XLA Ops:
  1.8 15.6 %collective-permute-start = (f32[72,128]{1,0:T(8,128)S(1)}, f32[72,128]{1,0:T(8,128)S(1)}, u32[]{:S(2)}, u32[]{:S(2)}) collective-permute-start(f32[72,128]{1,0:T(8,128)S(1)} %get-tuple-element.34), channel_id=1, source_target_pairs={{8,0},{16,8},{40,32},{48,40},{72,64},{80,72},{104,96},{112,104},{9... | collective-permute-start | bytes 110600 | tf_op jit(solution)/shard_map/ppermute | solution.py:435
  3.1 14.3 %collective-permute-start.2 = (f32[64,128]{1,0:T(8,128)S(1)}, f32[64,128]{1,0:T(8,128)S(1)}, u32[]{:S(2)}, u32[]{:S(2)}) collective-permute-start(f32[64,128]{1,0:T(8,128)S(1)} %get-tuple-element.36), channel_id=1, source_target_pairs={{0,8},{8,16},{24,32},{32,40},{40,48},{56,64},{64,72},{72,80},{88,9... | collective-permute-start | bytes 98312 | tf_op jit(solution)/shard_map/ppermute | solution.py:436
  12.8 4.5 %collective-permute-start.1 = (f32[48,128]{1,0:T(8,128)S(1)}, f32[48,128]{1,0:T(8,128)S(1)}, u32[]{:S(2)}, u32[]{:S(2)}) collective-permute-start(f32[48,128]{1,0:T(8,128)S(1)} %get-tuple-element.35), channel_id=1, source_target_pairs={{32,24},{64,56},{96,88},{33,25},{65,57},{97,89},{34,26},{66,58},{9... | collective-permute-start | bytes 73736 | tf_op jit(solution)/shard_map/ppermute | solution.py:437
  15.9 1.5 %collective-permute-start.3 = (f32[64,128]{1,0:T(8,128)S(1)}, f32[64,128]{1,0:T(8,128)S(1)}, u32[]{:S(2)}, u32[]{:S(2)}) collective-permute-start(f32[64,128]{1,0:T(8,128)S(1)} %get-tuple-element.39), channel_id=1, source_target_pairs={{16,24},{48,56},{80,88},{112,120},{24,16},{56,48},{88,80},{120,112... | collective-permute-start | bytes 98312 | tf_op jit(solution)/shard_map/ppermute | solution.py:438
  17.6 9.2 %collective-permute-start.4 = (f32[3,24,128]{2,1,0:T(8,128)S(1)}, f32[3,24,128]{2,1,0:T(8,128)S(1)}, u32[]{:S(2)}, u32[]{:S(2)}) collective-permute-start(f32[3,24,128]{2,1,0:T(8,128)S(1)} %get-tuple-element.47.own._), channel_id=1, source_target_pairs={{0,128},{128,0},{256,384},{384,256},{1,129},{129,1},{257,385},{385... | collective-permute-start | bytes 110600 | tf_op jit(solution)/shard_map/ppermute | solution.py:462
  20.5 6.3 %collective-permute-start.5 = (f32[3,24,128]{2,1,0:T(8,128)S(1)}, f32[3,24,128]{2,1,0:T(8,128)S(1)}, u32[]{:S(2)}, u32[]{:S(2)}) collective-permute-start(f32[3,24,128]{2,1,0:T(8,128)S(1)} %get-tuple-element.47.own._), channel_id=1, source_target_pairs={{128,256},{256,128},{129,257},{257,129},{130,258},{258,130},{131,2... | collective-permute-start | bytes 110600 | tf_op jit(solution)/shard_map/ppermute | solution.py:463
  23.8 5.4 %collective-permute-start.8 = (f32[9,24,128]{2,1,0:T(8,128)S(1)}, f32[9,24,128]{2,1,0:T(8,128)S(1)}, u32[]{:S(2)}, u32[]{:S(2)}) collective-permute-start(f32[9,24,128]{2,1,0:T(8,128)S(1)} %get-tuple-element.52), channel_id=1, source_target_pairs={{0,1},{1,2},{2,3},{3,4},{4,5},{5,6},{6,7},{7,0},{8,9},{9,10},{10,1... | collective-permute-start | bytes 331784 | tf_op jit(solution)/shard_map/ppermute | solution.py:475
  23.8 5.2 %collective-permute-start.9 = (f32[8,24,128]{2,1,0:T(8,128)S(1)}, f32[8,24,128]{2,1,0:T(8,128)S(1)}, u32[]{:S(2)}, u32[]{:S(2)}) collective-permute-start(f32[8,24,128]{2,1,0:T(8,128)S(1)} %get-tuple-element.53), channel_id=1, source_target_pairs={{1,0},{2,1},{3,2},{4,3},{5,4},{6,5},{7,6},{0,7},{9,8},{10,9},{11,1... | collective-permute-start | bytes 294920 | tf_op jit(solution)/shard_map/ppermute | solution.py:476
  26.9 4.8 %collective-permute-start.7 = (f32[73,128]{1,0:T(8,128)S(1)}, f32[73,128]{1,0:T(8,128)S(1)}, u32[]{:S(2)}, u32[]{:S(2)}) collective-permute-start(f32[73,128]{1,0:T(8,128)S(1)} %get-tuple-element.49), channel_id=1, source_target_pairs={{1,0},{2,1},{3,2},{4,3},{5,4},{6,5},{7,6},{0,7},{9,8},{10,9},{11,1... | collective-permute-start | bytes 112136 | tf_op jit(solution)/shard_map/ppermute | solution.py:479
  27.1 4.6 %collective-permute-start.6 = (f32[72,128]{1,0:T(8,128)S(1)}, f32[72,128]{1,0:T(8,128)S(1)}, u32[]{:S(2)}, u32[]{:S(2)}) collective-permute-start(f32[72,128]{1,0:T(8,128)S(1)} %get-tuple-element.48), channel_id=1, source_target_pairs={{0,1},{1,2},{2,3},{3,4},{4,5},{5,6},{6,7},{7,0},{8,9},{9,10},{10,1... | collective-permute-start | bytes 110600 | tf_op jit(solution)/shard_map/ppermute | solution.py:478

commit v9 on v8

--- a/solution.py
+++ b/solution.py
@@ -94,9 +94,12 @@
 def edge_columns(value, g, rows):
     lane = lax.broadcasted_iota(jnp.int32, (rows, 128), 1)
     total = jnp.zeros((rows, 128), jnp.float32)
-    for c in range(4 * g, min(4 * g + 4, 10)):
+    starts = [(4 * g + k, SPAN * k) for k in range(4)]
+    if g == 0:
+        starts += [(8, SPAN // 2), (9, SPAN + SPAN // 2)]
+    for c, start in starts:
         for z in range(4):
-            at = SPAN * (c - 4 * g) + 4 * (z + 2)
+            at = start + 4 * (z + 2)
             total = jnp.where((lane >= at) & (lane < at + 4), roll(value(c, z), at - 126, 1), total)
     return total
 
@@ -113,7 +116,7 @@
             p1[k, z] = cells[2][k, z] + time_step * flow
         for c in EVERY:
             planes[z, c] = own_value(cells, c, z)
-    for g in range(3):
+    for g in range(2):
         edges[g] = edge_columns(lambda c, z: own_value(cells, c, z), g, 16)
 
 
@@ -127,7 +130,7 @@
         for i, (c, row) in enumerate(Y_DOWN):
             at = slice(4 * i + z, 4 * i + z + 1)
             beside[z, c, row : row + 1, :] = jnp.where(high, last[at, :], after[at, :])
-    for g in range(3):
+    for g in range(2):
         edges[g, 0:16, :] = own[g]
         edges[g, 16:24, :] = edge_columns(lambda c, z: beside[z, c], g, 8)
 
@@ -172,6 +175,8 @@
 
 
 def sides(own, outer, inner, g):
+    if g == 2:
+        return [roll(a, -SPAN // 2, 1) for a in sides(own, outer, inner, 0)]
     near = (lanes() % 4) < 2
     odd = lax.axis_index("gx") % 2 == 1
     left = jnp.where(odd, outer[g], inner[g])
@@ -179,10 +184,11 @@
     return jnp.where(near, left, own[g]), jnp.where(near, own[g], right)
 
 
-def columns_on(own, outer, inner, *outs):
+def columns_on(own, outer, inner, lows, highs, *outs):
     part = (lanes() % SPAN) // 8
     for g in range(3):
         low, high = sides(own, outer, inner, g)
+        lows[g], highs[g] = low, high
         up = jnp.where(part == 0, roll(low, -16, 1), roll(high, -8, 1))
         down = jnp.where(part == 2, roll(high, 8, 1), roll(low, 16, 1))
         for out in outs:
@@ -289,13 +295,13 @@
     electric(4, [from_above(3 + k) for k in range(2)], push_e, [from_above(k) for k in range(3)], h)
 
 
-def columns(own, outer, inner, before, after):
+def columns(lows, highs, before, after):
     first, last = grid_ends()
     lane = lanes()
     part = (lane % SPAN) // 8
     values = []
     for g in range(3):
-        low, high = sides(own, outer, inner, g)
+        low, high = lows[g], highs[g]
         rows = slice(ROWS * g, ROWS * (g + 1))
         up = jnp.where(first, 0.0, before[rows, :])
         down = jnp.where(last, 0.0, after[rows, :])
@@ -318,11 +324,11 @@
     return h1, e1, h2
 
 
-def second_step(own, outer, inner, before, after, h1, e1, low, p1, j1, fh, fe, *rest):
+def second_step(lows, highs, before, after, h1, e1, low, p1, j1, fh, fe, *rest):
     outs, near, h2, fixed, done = rest[:4], rest[4:8], rest[8], rest[9], rest[10]
     e_near, h_near, p_near, j_near = near
     lane = lanes()
-    ch1, ce1, ch2 = columns(own, outer, inner, before, after)
+    ch1, ce1, ch2 = columns(lows, highs, before, after)
 
     def at_ends(column):
         return jnp.where(lane % 4 == 1, roll(column, -SPAN, 1), column)
@@ -447,13 +453,13 @@
     brick, plane = f32(3, 4, 16, 128), (ROWS, 128)
     planes, own, p1, j1, fe = call(
         own_planes,
-        [f32(4, 10, 16, 128), f32(3, 16, 128), brick, brick, f32(4, 3, 16, 128)],
+        [f32(4, 10, 16, 128), f32(2, 16, 128), brick, brick, f32(4, 3, 16, 128)],
         cells,
         name="own_planes",
     )
     beside, own = call(
         widen_rows,
-        [f32(4, 10, 8, 128), f32(3, *plane)],
+        [f32(4, 10, 8, 128), f32(2, *plane)],
         (before, after, last, own),
         name="widen_rows",
     )
@@ -474,7 +480,7 @@
     )
     before = lax.ppermute(up, "gz", ring_up)
     after = lax.ppermute(down, "gz", ring_down)
-    up, down = call(columns_on, [f32(72, 128), f32(73, 128)], (own, outer, inner), size=1 << 30, flops=1 << 36, name="columns_on")
+    lows, highs, up, down = call(columns_on, [f32(3, *plane)] * 2 + [f32(72, 128), f32(73, 128)], (own, outer, inner), size=1 << 30, flops=1 << 36, name="columns_on")
     columns_before = lax.ppermute(up, "gz", ring_up)
     columns_after = lax.ppermute(down, "gz", ring_down)
 
@@ -489,7 +495,7 @@
         call(
             second_step,
             [brick] * 4,
-            (own, outer, inner, columns_before, columns_after, h1, e1, low, p1, j1, fh, fe),
+            (lows, highs, columns_before, columns_after, h1, e1, low, p1, j1, fh, fe),
             scratch=[pltpu.VMEM((3, 4, 16, 128), jnp.float32)] * 4
             + [pltpu.VMEM((5, 3, ROWS, 128), jnp.float32), pltpu.VMEM((6, 3, ROWS, 128), jnp.float32), pltpu.SemaphoreType.DMA((4,))],
             far_out=True,

time: 33.2 us -> 33.2 us (level)
  no operation moved by 1% of the time
where the time goes in v9:
time: 33.2 us; the launch traced here: 33 us
  starting transfers between devices  24.3 us (73%)
  waiting for transfers between devices  4.85 us (15%)
  Pallas kernels  3.18 us (10%)
  between operations  0.73 us (2%)
    ppermute x1, starting transfers between devices, on_device(): before = lax.ppermute(up, 'gy', [(i, j) for i, j in ups if i % 4 != 2])  9.73 us
    pallas_call x8, Pallas kernels, call(): pl.pallas_call(kernel, out_shape=outs, in_specs=[HBM if far else VMEM] *...  3.18 us
    ppermute x1, starting transfers between devices, on_device(): inner = lax.ppermute(own, 'gx', between)  3.14 us
    ppermute x1, starting transfers between devices, on_device(): later = lax.ppermute(late, 'gy', [(i, j) for i, j in downs if i % 4 == 0])  3.04 us
    ppermute x1, starting transfers between devices, on_device(): after = lax.ppermute(down, 'gz', ring_down)  2.94 us
    ppermute x1, starting transfers between devices, on_device(): outer = lax.ppermute(own, 'gx', pairs)  2.92 us
    ppermute x1, waiting for transfers between devices, on_device(): columns_before = lax.ppermute(up, 'gz', ring_up)  2.42 us
    ppermute x1, waiting for transfers between devices, on_device(): after = lax.ppermute(down, 'gz', ring_down)  1.53 us
  transfers between devices with their start and end apart: 10, of which 4 were waited for; matrix products, arithmetic and copies ran while one was open for 0% of the time, Pallas kernels for 2%

profile of v9, /device:TPU:38, one launch (start us, length us, event | category | flops | bytes accessed | tf_op | source)
XLA Modules:
  0.0 33.0 jit_solution(6030915595307704209)
XLA Ops:
  0.6 1.2 %load_and_faces.1 = (f32[3,4,16,128]{3,2,1,0:T(8,128)S(1)}, f32[3,4,16,128]{3,2,1,0:T(8,128)S(1)}, f32[3,4,16,128]{3,2,1,0:T(8,128)S(1)}, f32[3,4,16,128]{3,2,1,...) custom-call(f32[3,4,16,128]{3,2,1,0:T(8,128)} %refs_0_.1, ...), custom_call_target="tpu_custom_call" | custom-call | bytes 1044480 | tf_op jit(solution)/shard_map/load_and_faces/pallas_call | solution.py:411
  1.8 1.3 %collective-permute-start = (f32[72,128]{1,0:T(8,128)S(1)}, f32[72,128]{1,0:T(8,128)S(1)}, u32[]{:S(2)}, u32[]{:S(2)}) collective-permute-start(f32[72,128]{1,0:T(8,128)S(1)} %get-tuple-element.36), channel_id=1, source_target_pairs={{8,0},{16,8},{40,32},{48,40},{72,64},{80,72},{104,96},{112,104},{9... | collective-permute-start | bytes 110600 | tf_op jit(solution)/shard_map/ppermute | solution.py:441
  3.1 9.7 %collective-permute-start.2 = (f32[64,128]{1,0:T(8,128)S(1)}, f32[64,128]{1,0:T(8,128)S(1)}, u32[]{:S(2)}, u32[]{:S(2)}) collective-permute-start(f32[64,128]{1,0:T(8,128)S(1)} %get-tuple-element.38), channel_id=1, source_target_pairs={{0,8},{8,16},{24,32},{32,40},{40,48},{56,64},{64,72},{72,80},{88,9... | collective-permute-start | bytes 98312 | tf_op jit(solution)/shard_map/ppermute | solution.py:442
  12.8 3.0 %collective-permute-start.1 = (f32[48,128]{1,0:T(8,128)S(1)}, f32[48,128]{1,0:T(8,128)S(1)}, u32[]{:S(2)}, u32[]{:S(2)}) collective-permute-start(f32[48,128]{1,0:T(8,128)S(1)} %get-tuple-element.37), channel_id=1, source_target_pairs={{32,24},{64,56},{96,88},{33,25},{65,57},{97,89},{34,26},{66,58},{9... | collective-permute-start | bytes 73736 | tf_op jit(solution)/shard_map/ppermute | solution.py:443
  15.9 0.7 %collective-permute-start.3 = (f32[64,128]{1,0:T(8,128)S(1)}, f32[64,128]{1,0:T(8,128)S(1)}, u32[]{:S(2)}, u32[]{:S(2)}) collective-permute-start(f32[64,128]{1,0:T(8,128)S(1)} %get-tuple-element.41), channel_id=1, source_target_pairs={{16,24},{48,56},{80,88},{112,120},{24,16},{56,48},{88,80},{120,112... | collective-permute-start | bytes 98312 | tf_op jit(solution)/shard_map/ppermute | solution.py:444
  16.5 0.2 own_planes.1
  16.7 0.7 %collective-permute-done.1.later = f32[48,128]{1,0:T(8,128)S(1)} collective-permute-done((f32[48,128]{1,0:T(8,128)S(1)}, f32[48,128]{1,0:T(8,128)S(1)}, u32[]{:S(2)}, u32[]{:S(2)}) %collective-permute-start.1) | collective-permute-done | bytes 24608 | tf_op jit(solution)/shard_map/ppermute | solution.py:443
  17.4 0.0 collective-permute-done.2.before
  17.4 0.0 collective-permute-done.after
  17.4 0.0 collective-permute-done.3.last
  17.4 0.2 widen_rows.1
  17.6 2.9 %collective-permute-start.4 = (f32[2,24,128]{2,1,0:T(8,128)S(1)}, f32[2,24,128]{2,1,0:T(8,128)S(1)}, u32[]{:S(2)}, u32[]{:S(2)}) collective-permute-start(f32[2,24,128]{2,1,0:T(8,128)S(1)} %get-tuple-element.49.own._), channel_id=1, source_target_pairs={{0,128},{128,0},{256,384},{384,256},{1,129},{129,1},{257,385},{385... | collective-permute-start | bytes 73736 | tf_op jit(solution)/shard_map/ppermute | solution.py:468
  20.5 3.1 %collective-permute-start.5 = (f32[2,24,128]{2,1,0:T(8,128)S(1)}, f32[2,24,128]{2,1,0:T(8,128)S(1)}, u32[]{:S(2)}, u32[]{:S(2)}) collective-permute-start(f32[2,24,128]{2,1,0:T(8,128)S(1)} %get-tuple-element.49.own._), channel_id=1, source_target_pairs={{128,256},{256,128},{129,257},{257,129},{130,258},{258,130},{131,2... | collective-permute-start | bytes 73736 | tf_op jit(solution)/shard_map/ppermute | solution.py:469
  23.6 0.1 z_faces.1
  23.8 0.0 collective-permute-start.8
  23.8 2.9 %collective-permute-start.9 = (f32[8,24,128]{2,1,0:T(8,128)S(1)}, f32[8,24,128]{2,1,0:T(8,128)S(1)}, u32[]{:S(2)}, u32[]{:S(2)}) collective-permute-start(f32[8,24,128]{2,1,0:T(8,128)S(1)} %get-tuple-element.57), channel_id=1, source_target_pairs={{1,0},{2,1},{3,2},{4,3},{5,4},{6,5},{7,6},{0,7},{9,8},{10,9},{11,1... | collective-permute-start | bytes 294920 | tf_op jit(solution)/shard_map/ppermute | solution.py:482
  26.7 0.0 collective-permute-done.4.outer
  26.7 0.0 collective-permute-done.5.inner
  26.7 0.2 columns_on.1
  26.9 0.2 collective-permute-start.7
  27.1 0.3 collective-permute-start.6
  27.4 1.5 %collective-permute-done.9.after = f32[8,24,128]{2,1,0:T(8,128)S(1)} collective-permute-done((f32[8,24,128]{2,1,0:T(8,128)S(1)}, f32[8,24,128]{2,1,0:T(8,128)S(1)}, u32[]{:S(2)}, u32[]{:S(2)}) %collective-permute-start.9) | collective-permute-done | bytes 98336 | tf_op jit(solution)/shard_map/ppermute | solution.py:482
  29.0 0.2 collective-permute-done.8.before
  29.2 0.1 first_step.1
  29.3 2.4 %collective-permute-done.6.before = f32[72,128]{1,0:T(8,128)S(1)} collective-permute-done((f32[72,128]{1,0:T(8,128)S(1)}, f32[72,128]{1,0:T(8,128)S(1)}, u32[]{:S(2)}, u32[]{:S(2)}) %collective-permute-start.6) | collective-permute-done | bytes 36896 | tf_op jit(solution)/shard_map/ppermute | solution.py:484
  31.7 0.0 collective-permute-done.7.after
  31.7 1.3 %second_step.1 = (f32[3,4,16,128]{3,2,1,0:T(8,128)}, f32[3,4,16,128]{3,2,1,0:T(8,128)}, f32[3,4,16,128]{3,2,1,0:T(8,128)}, f32[3,4,16,128]{3,2,1,0:T(8,128)}) custom-call(f32[3,24,128]{2,1,0:T(8,128)S(1)} %get-tuple-element.50.lows, f32[3,24,128]{2,1,0:T(8,128)S(1)} %get-tuple-element.51.highs, f32[72,128]{1,0:T(8,128)S(1)} %collective-permute-done.6.before, ...), custom_call_target="tpu_custom_call" | custom-call | flops 2000000 | bytes 1364480 | tf_op jit(solution)/shard_map/second_step/pallas_call | solution.py:411
  (1 shorter events, 0.0 us)
Async XLA Ops:
  1.8 15.6 %collective-permute-start = (f32[72,128]{1,0:T(8,128)S(1)}, f32[72,128]{1,0:T(8,128)S(1)}, u32[]{:S(2)}, u32[]{:S(2)}) collective-permute-start(f32[72,128]{1,0:T(8,128)S(1)} %get-tuple-element.36), channel_id=1, source_target_pairs={{8,0},{16,8},{40,32},{48,40},{72,64},{80,72},{104,96},{112,104},{9... | collective-permute-start | bytes 110600 | tf_op jit(solution)/shard_map/ppermute | solution.py:441
  3.1 14.3 %collective-permute-start.2 = (f32[64,128]{1,0:T(8,128)S(1)}, f32[64,128]{1,0:T(8,128)S(1)}, u32[]{:S(2)}, u32[]{:S(2)}) collective-permute-start(f32[64,128]{1,0:T(8,128)S(1)} %get-tuple-element.38), channel_id=1, source_target_pairs={{0,8},{8,16},{24,32},{32,40},{40,48},{56,64},{64,72},{72,80},{88,9... | collective-permute-start | bytes 98312 | tf_op jit(solution)/shard_map/ppermute | solution.py:442
  12.8 4.5 %collective-permute-start.1 = (f32[48,128]{1,0:T(8,128)S(1)}, f32[48,128]{1,0:T(8,128)S(1)}, u32[]{:S(2)}, u32[]{:S(2)}) collective-permute-start(f32[48,128]{1,0:T(8,128)S(1)} %get-tuple-element.37), channel_id=1, source_target_pairs={{32,24},{64,56},{96,88},{33,25},{65,57},{97,89},{34,26},{66,58},{9... | collective-permute-start | bytes 73736 | tf_op jit(solution)/shard_map/ppermute | solution.py:443
  15.9 1.5 %collective-permute-start.3 = (f32[64,128]{1,0:T(8,128)S(1)}, f32[64,128]{1,0:T(8,128)S(1)}, u32[]{:S(2)}, u32[]{:S(2)}) collective-permute-start(f32[64,128]{1,0:T(8,128)S(1)} %get-tuple-element.41), channel_id=1, source_target_pairs={{16,24},{48,56},{80,88},{112,120},{24,16},{56,48},{88,80},{120,112... | collective-permute-start | bytes 98312 | tf_op jit(solution)/shard_map/ppermute | solution.py:444
  17.6 9.2 %collective-permute-start.4 = (f32[2,24,128]{2,1,0:T(8,128)S(1)}, f32[2,24,128]{2,1,0:T(8,128)S(1)}, u32[]{:S(2)}, u32[]{:S(2)}) collective-permute-start(f32[2,24,128]{2,1,0:T(8,128)S(1)} %get-tuple-element.49.own._), channel_id=1, source_target_pairs={{0,128},{128,0},{256,384},{384,256},{1,129},{129,1},{257,385},{385... | collective-permute-start | bytes 73736 | tf_op jit(solution)/shard_map/ppermute | solution.py:468
  20.5 6.3 %collective-permute-start.5 = (f32[2,24,128]{2,1,0:T(8,128)S(1)}, f32[2,24,128]{2,1,0:T(8,128)S(1)}, u32[]{:S(2)}, u32[]{:S(2)}) collective-permute-start(f32[2,24,128]{2,1,0:T(8,128)S(1)} %get-tuple-element.49.own._), channel_id=1, source_target_pairs={{128,256},{256,128},{129,257},{257,129},{130,258},{258,130},{131,2... | collective-permute-start | bytes 73736 | tf_op jit(solution)/shard_map/ppermute | solution.py:469
  23.8 5.4 %collective-permute-start.8 = (f32[9,24,128]{2,1,0:T(8,128)S(1)}, f32[9,24,128]{2,1,0:T(8,128)S(1)}, u32[]{:S(2)}, u32[]{:S(2)}) collective-permute-start(f32[9,24,128]{2,1,0:T(8,128)S(1)} %get-tuple-element.56), channel_id=1, source_target_pairs={{0,1},{1,2},{2,3},{3,4},{4,5},{5,6},{6,7},{7,0},{8,9},{9,10},{10,1... | collective-permute-start | bytes 331784 | tf_op jit(solution)/shard_map/ppermute | solution.py:481
  23.8 5.2 %collective-permute-start.9 = (f32[8,24,128]{2,1,0:T(8,128)S(1)}, f32[8,24,128]{2,1,0:T(8,128)S(1)}, u32[]{:S(2)}, u32[]{:S(2)}) collective-permute-start(f32[8,24,128]{2,1,0:T(8,128)S(1)} %get-tuple-element.57), channel_id=1, source_target_pairs={{1,0},{2,1},{3,2},{4,3},{5,4},{6,5},{7,6},{0,7},{9,8},{10,9},{11,1... | collective-permute-start | bytes 294920 | tf_op jit(solution)/shard_map/ppermute | solution.py:482
  26.9 4.8 %collective-permute-start.7 = (f32[73,128]{1,0:T(8,128)S(1)}, f32[73,128]{1,0:T(8,128)S(1)}, u32[]{:S(2)}, u32[]{:S(2)}) collective-permute-start(f32[73,128]{1,0:T(8,128)S(1)} %get-tuple-element.53), channel_id=1, source_target_pairs={{1,0},{2,1},{3,2},{4,3},{5,4},{6,5},{7,6},{0,7},{9,8},{10,9},{11,1... | collective-permute-start | bytes 112136 | tf_op jit(solution)/shard_map/ppermute | solution.py:485
  27.1 4.6 %collective-permute-start.6 = (f32[72,128]{1,0:T(8,128)S(1)}, f32[72,128]{1,0:T(8,128)S(1)}, u32[]{:S(2)}, u32[]{:S(2)}) collective-permute-start(f32[72,128]{1,0:T(8,128)S(1)} %get-tuple-element.52), channel_id=1, source_target_pairs={{0,1},{1,2},{2,3},{3,4},{4,5},{5,6},{6,7},{7,0},{8,9},{9,10},{10,1... | collective-permute-start | bytes 110600 | tf_op jit(solution)/shard_map/ppermute | solution.py:484

commit v10 on v8

--- a/solution.py
+++ b/solution.py
@@ -18,8 +18,8 @@
 EX, EY, EZ, HX, HY, HZ, QX, QY, QZ, CODE = range(10)
 EVERY = tuple(range(10))
 
-Y_UP = [(c, 14) for c in (EX, EY, EZ, HX, HZ, CODE)] + [(c, 15) for c in EVERY]
-Y_DOWN = [(c, 0) for c in (EX, EY, EZ, HX, HY, HZ, QX, QZ, CODE)] + [(EX, 1), (EZ, 1)]
+Y_UP = [(c, 14) for c in (EY, HX, HZ, CODE)] + [(c, 15) for c in EVERY]
+Y_DOWN = [(c, 0) for c in (EX, EY, EZ, HX, HY, HZ, QX, QZ, CODE)]
 Z_UP, Z_DOWN = 9, 8
 
 ROWS = 24
@@ -43,7 +43,15 @@
     if c < HX:
         return e[c, :, row, :]
     if c < QX:
-        return h[c - HX, :, row, :]
+        value = h[c - HX, :, row, :]
+        if c == HY or row == 15:
+            return value
+        other, sign = (EZ, 1.0) if c == HX else (EX, -1.0)
+        level = pml[:, row, :]
+        loss = jnp.where(level > 2, 0.25, jnp.where(level > 1, 0.1, jnp.where(level > 0, 0.025, 0.0)))
+        if row == 0:
+            return value - sign * time_step / (1.0 - loss) * e[other, :, 1, :]
+        return value + sign * time_step / (1.0 - loss) * e[other, :, 14, :]
     if c < CODE:
         return HOLD * j[c - QX, :, row, :] - PULL * p[c - QX, :, row, :]
     return code_of(material[:, row, :], pml[:, row, :])
@@ -76,7 +84,7 @@
 
 
 def joined(after, later, before, rows_after, rows_before):
-    rows_after[...] = after[0:48, :] + later[...]
+    rows_after[...] = after[0:40, :] + later[...]
     rows_before[...] = before[...]
 
 
@@ -425,7 +433,7 @@
     cells = [pltpu.with_memory_space_constraint(a, pltpu.HBM) for a in cells]
     *cells, down, up, late, mixed = call(
         load_and_faces,
-        [*shapes, f32(72, 128), f32(64, 128), f32(48, 128), f32(64, 128)],
+        [*shapes, f32(64, 128), f32(56, 128), f32(40, 128), f32(56, 128)],
         cells,
         scratch=[pltpu.SemaphoreType.DMA((6,))],
         far=True,
@@ -438,7 +446,7 @@
     last = lax.ppermute(mixed, "gy", [(i, j) for i, j in ups if i % 4 == 2] + [(i, j) for i, j in downs if i % 4 == 3])
     after, before = call(
         joined,
-        [f32(48, 128), f32(64, 128)],
+        [f32(40, 128), f32(56, 128)],
         (after, later, before),
         size=1 << 30,
         flops=1 << 36,

time: 33.2 us -> 33 us (level)
  no operation moved by 1% of the time
where the time goes in v10:
time: 33 us; the launch traced here: 32.8 us
  starting transfers between devices  24.1 us (73%)
  waiting for transfers between devices  4.8 us (15%)
  Pallas kernels  3.14 us (10%)
  between operations  0.74 us (2%)
    ppermute x1, starting transfers between devices, on_device(): before = lax.ppermute(up, 'gy', [(i, j) for i, j in ups if i % 4 != 2])  9.73 us
    pallas_call x8, Pallas kernels, call(): pl.pallas_call(kernel, out_shape=outs, in_specs=[HBM if far else VMEM] *...  3.14 us
    ppermute x1, starting transfers between devices, on_device(): later = lax.ppermute(late, 'gy', [(i, j) for i, j in downs if i % 4 == 0])  3.04 us
    ppermute x1, starting transfers between devices, on_device(): inner = lax.ppermute(own, 'gx', between)  2.99 us
    ppermute x1, starting transfers between devices, on_device(): after = lax.ppermute(down, 'gz', ring_down)  2.94 us
    ppermute x1, starting transfers between devices, on_device(): outer = lax.ppermute(own, 'gx', pairs)  2.92 us
    ppermute x1, waiting for transfers between devices, on_device(): columns_before = lax.ppermute(up, 'gz', ring_up)  2.38 us
    ppermute x1, waiting for transfers between devices, on_device(): after = lax.ppermute(down, 'gz', ring_down)  1.57 us
  transfers between devices with their start and end apart: 10, of which 4 were waited for; matrix products, arithmetic and copies ran while one was open for 0% of the time, Pallas kernels for 2%

profile of v10, /device:TPU:38, one launch (start us, length us, event | category | flops | bytes accessed | tf_op | source)
XLA Modules:
  0.0 32.8 jit_solution(15699956571188450910)
XLA Ops:
  0.6 1.2 %load_and_faces.1 = (f32[3,4,16,128]{3,2,1,0:T(8,128)S(1)}, f32[3,4,16,128]{3,2,1,0:T(8,128)S(1)}, f32[3,4,16,128]{3,2,1,0:T(8,128)S(1)}, f32[3,4,16,128]{3,2,1,...) custom-call(f32[3,4,16,128]{3,2,1,0:T(8,128)} %refs_0_.1, ...), custom_call_target="tpu_custom_call" | custom-call | bytes 1028096 | tf_op jit(solution)/shard_map/load_and_faces/pallas_call | solution.py:413
  1.8 1.3 %collective-permute-start = (f32[64,128]{1,0:T(8,128)S(1)}, f32[64,128]{1,0:T(8,128)S(1)}, u32[]{:S(2)}, u32[]{:S(2)}) collective-permute-start(f32[64,128]{1,0:T(8,128)S(1)} %get-tuple-element.34), channel_id=1, source_target_pairs={{8,0},{16,8},{40,32},{48,40},{72,64},{80,72},{104,96},{112,104},{9... | collective-permute-start | bytes 98312 | tf_op jit(solution)/shard_map/ppermute | solution.py:443
  3.1 9.7 %collective-permute-start.2 = (f32[56,128]{1,0:T(8,128)S(1)}, f32[56,128]{1,0:T(8,128)S(1)}, u32[]{:S(2)}, u32[]{:S(2)}) collective-permute-start(f32[56,128]{1,0:T(8,128)S(1)} %get-tuple-element.36), channel_id=1, source_target_pairs={{0,8},{8,16},{24,32},{32,40},{40,48},{56,64},{64,72},{72,80},{88,9... | collective-permute-start | bytes 86024 | tf_op jit(solution)/shard_map/ppermute | solution.py:444
  12.8 3.0 %collective-permute-start.1 = (f32[40,128]{1,0:T(8,128)S(1)}, f32[40,128]{1,0:T(8,128)S(1)}, u32[]{:S(2)}, u32[]{:S(2)}) collective-permute-start(f32[40,128]{1,0:T(8,128)S(1)} %get-tuple-element.35), channel_id=1, source_target_pairs={{32,24},{64,56},{96,88},{33,25},{65,57},{97,89},{34,26},{66,58},{9... | collective-permute-start | bytes 61448 | tf_op jit(solution)/shard_map/ppermute | solution.py:445
  15.9 0.7 %collective-permute-start.3 = (f32[56,128]{1,0:T(8,128)S(1)}, f32[56,128]{1,0:T(8,128)S(1)}, u32[]{:S(2)}, u32[]{:S(2)}) collective-permute-start(f32[56,128]{1,0:T(8,128)S(1)} %get-tuple-element.39), channel_id=1, source_target_pairs={{16,24},{48,56},{80,88},{112,120},{24,16},{56,48},{88,80},{120,112... | collective-permute-start | bytes 86024 | tf_op jit(solution)/shard_map/ppermute | solution.py:446
  16.6 0.2 own_planes.1
  16.7 0.6 %collective-permute-done.1.later = f32[40,128]{1,0:T(8,128)S(1)} collective-permute-done((f32[40,128]{1,0:T(8,128)S(1)}, f32[40,128]{1,0:T(8,128)S(1)}, u32[]{:S(2)}, u32[]{:S(2)}) %collective-permute-start.1) | collective-permute-done | bytes 20512 | tf_op jit(solution)/shard_map/ppermute | solution.py:445
  17.3 0.0 collective-permute-done.2.before
  17.4 0.0 collective-permute-done.after
  17.4 0.0 collective-permute-done.3.last
  17.4 0.1 widen_rows.1
  17.5 2.9 %collective-permute-start.4 = (f32[3,24,128]{2,1,0:T(8,128)S(1)}, f32[3,24,128]{2,1,0:T(8,128)S(1)}, u32[]{:S(2)}, u32[]{:S(2)}) collective-permute-start(f32[3,24,128]{2,1,0:T(8,128)S(1)} %get-tuple-element.47.own._), channel_id=1, source_target_pairs={{0,128},{128,0},{256,384},{384,256},{1,129},{129,1},{257,385},{385... | collective-permute-start | bytes 110600 | tf_op jit(solution)/shard_map/ppermute | solution.py:470
  20.4 3.0 %collective-permute-start.5 = (f32[3,24,128]{2,1,0:T(8,128)S(1)}, f32[3,24,128]{2,1,0:T(8,128)S(1)}, u32[]{:S(2)}, u32[]{:S(2)}) collective-permute-start(f32[3,24,128]{2,1,0:T(8,128)S(1)} %get-tuple-element.47.own._), channel_id=1, source_target_pairs={{128,256},{256,128},{129,257},{257,129},{130,258},{258,130},{131,2... | collective-permute-start | bytes 110600 | tf_op jit(solution)/shard_map/ppermute | solution.py:471
  23.4 0.1 z_faces.1
  23.6 0.0 collective-permute-start.8
  23.6 2.9 %collective-permute-start.9 = (f32[8,24,128]{2,1,0:T(8,128)S(1)}, f32[8,24,128]{2,1,0:T(8,128)S(1)}, u32[]{:S(2)}, u32[]{:S(2)}) collective-permute-start(f32[8,24,128]{2,1,0:T(8,128)S(1)} %get-tuple-element.53), channel_id=1, source_target_pairs={{1,0},{2,1},{3,2},{4,3},{5,4},{6,5},{7,6},{0,7},{9,8},{10,9},{11,1... | collective-permute-start | bytes 294920 | tf_op jit(solution)/shard_map/ppermute | solution.py:484
  26.6 0.0 collective-permute-done.4.outer
  26.6 0.0 collective-permute-done.5.inner
  26.6 0.1 columns_on.1
  26.7 0.2 collective-permute-start.7
  26.9 0.3 collective-permute-start.6
  27.2 1.6 %collective-permute-done.9.after = f32[8,24,128]{2,1,0:T(8,128)S(1)} collective-permute-done((f32[8,24,128]{2,1,0:T(8,128)S(1)}, f32[8,24,128]{2,1,0:T(8,128)S(1)}, u32[]{:S(2)}, u32[]{:S(2)}) %collective-permute-start.9) | collective-permute-done | bytes 98336 | tf_op jit(solution)/shard_map/ppermute | solution.py:484
  28.8 0.2 collective-permute-done.8.before
  29.0 0.1 first_step.1
  29.1 2.4 %collective-permute-done.6.before = f32[72,128]{1,0:T(8,128)S(1)} collective-permute-done((f32[72,128]{1,0:T(8,128)S(1)}, f32[72,128]{1,0:T(8,128)S(1)}, u32[]{:S(2)}, u32[]{:S(2)}) %collective-permute-start.6) | collective-permute-done | bytes 36896 | tf_op jit(solution)/shard_map/ppermute | solution.py:486
  31.5 0.0 collective-permute-done.7.after
  31.5 1.3 %second_step.1 = (f32[3,4,16,128]{3,2,1,0:T(8,128)}, f32[3,4,16,128]{3,2,1,0:T(8,128)}, f32[3,4,16,128]{3,2,1,0:T(8,128)}, f32[3,4,16,128]{3,2,1,0:T(8,128)}) custom-call(f32[3,24,128]{2,1,0:T(8,128)S(1)} %get-tuple-element.47.own._, f32[3,24,128]{2,1,0:T(8,128)S(1)} %collective-permute-done.4.outer, f32[3,24,128]{2,1,0:T(8,128)S(1)} %collective-permute-done.5.inner, ...), custom_call_target="tpu_custom_call" | custom-call | flops 2000000 | bytes 1401344 | tf_op jit(solution)/shard_map/second_step/pallas_call | solution.py:413
  (1 shorter events, 0.0 us)
Async XLA Ops:
  1.8 15.5 %collective-permute-start = (f32[64,128]{1,0:T(8,128)S(1)}, f32[64,128]{1,0:T(8,128)S(1)}, u32[]{:S(2)}, u32[]{:S(2)}) collective-permute-start(f32[64,128]{1,0:T(8,128)S(1)} %get-tuple-element.34), channel_id=1, source_target_pairs={{8,0},{16,8},{40,32},{48,40},{72,64},{80,72},{104,96},{112,104},{9... | collective-permute-start | bytes 98312 | tf_op jit(solution)/shard_map/ppermute | solution.py:443
  3.1 14.2 %collective-permute-start.2 = (f32[56,128]{1,0:T(8,128)S(1)}, f32[56,128]{1,0:T(8,128)S(1)}, u32[]{:S(2)}, u32[]{:S(2)}) collective-permute-start(f32[56,128]{1,0:T(8,128)S(1)} %get-tuple-element.36), channel_id=1, source_target_pairs={{0,8},{8,16},{24,32},{32,40},{40,48},{56,64},{64,72},{72,80},{88,9... | collective-permute-start | bytes 86024 | tf_op jit(solution)/shard_map/ppermute | solution.py:444
  12.8 4.5 %collective-permute-start.1 = (f32[40,128]{1,0:T(8,128)S(1)}, f32[40,128]{1,0:T(8,128)S(1)}, u32[]{:S(2)}, u32[]{:S(2)}) collective-permute-start(f32[40,128]{1,0:T(8,128)S(1)} %get-tuple-element.35), channel_id=1, source_target_pairs={{32,24},{64,56},{96,88},{33,25},{65,57},{97,89},{34,26},{66,58},{9... | collective-permute-start | bytes 61448 | tf_op jit(solution)/shard_map/ppermute | solution.py:445
  15.9 1.5 %collective-permute-start.3 = (f32[56,128]{1,0:T(8,128)S(1)}, f32[56,128]{1,0:T(8,128)S(1)}, u32[]{:S(2)}, u32[]{:S(2)}) collective-permute-start(f32[56,128]{1,0:T(8,128)S(1)} %get-tuple-element.39), channel_id=1, source_target_pairs={{16,24},{48,56},{80,88},{112,120},{24,16},{56,48},{88,80},{120,112... | collective-permute-start | bytes 86024 | tf_op jit(solution)/shard_map/ppermute | solution.py:446
  17.5 9.0 %collective-permute-start.4 = (f32[3,24,128]{2,1,0:T(8,128)S(1)}, f32[3,24,128]{2,1,0:T(8,128)S(1)}, u32[]{:S(2)}, u32[]{:S(2)}) collective-permute-start(f32[3,24,128]{2,1,0:T(8,128)S(1)} %get-tuple-element.47.own._), channel_id=1, source_target_pairs={{0,128},{128,0},{256,384},{384,256},{1,129},{129,1},{257,385},{385... | collective-permute-start | bytes 110600 | tf_op jit(solution)/shard_map/ppermute | solution.py:470
  20.4 6.1 %collective-permute-start.5 = (f32[3,24,128]{2,1,0:T(8,128)S(1)}, f32[3,24,128]{2,1,0:T(8,128)S(1)}, u32[]{:S(2)}, u32[]{:S(2)}) collective-permute-start(f32[3,24,128]{2,1,0:T(8,128)S(1)} %get-tuple-element.47.own._), channel_id=1, source_target_pairs={{128,256},{256,128},{129,257},{257,129},{130,258},{258,130},{131,2... | collective-permute-start | bytes 110600 | tf_op jit(solution)/shard_map/ppermute | solution.py:471
  23.6 5.4 %collective-permute-start.8 = (f32[9,24,128]{2,1,0:T(8,128)S(1)}, f32[9,24,128]{2,1,0:T(8,128)S(1)}, u32[]{:S(2)}, u32[]{:S(2)}) collective-permute-start(f32[9,24,128]{2,1,0:T(8,128)S(1)} %get-tuple-element.52), channel_id=1, source_target_pairs={{0,1},{1,2},{2,3},{3,4},{4,5},{5,6},{6,7},{7,0},{8,9},{9,10},{10,1... | collective-permute-start | bytes 331784 | tf_op jit(solution)/shard_map/ppermute | solution.py:483
  23.6 5.2 %collective-permute-start.9 = (f32[8,24,128]{2,1,0:T(8,128)S(1)}, f32[8,24,128]{2,1,0:T(8,128)S(1)}, u32[]{:S(2)}, u32[]{:S(2)}) collective-permute-start(f32[8,24,128]{2,1,0:T(8,128)S(1)} %get-tuple-element.53), channel_id=1, source_target_pairs={{1,0},{2,1},{3,2},{4,3},{5,4},{6,5},{7,6},{0,7},{9,8},{10,9},{11,1... | collective-permute-start | bytes 294920 | tf_op jit(solution)/shard_map/ppermute | solution.py:484
  26.7 4.8 %collective-permute-start.7 = (f32[73,128]{1,0:T(8,128)S(1)}, f32[73,128]{1,0:T(8,128)S(1)}, u32[]{:S(2)}, u32[]{:S(2)}) collective-permute-start(f32[73,128]{1,0:T(8,128)S(1)} %get-tuple-element.49), channel_id=1, source_target_pairs={{1,0},{2,1},{3,2},{4,3},{5,4},{6,5},{7,6},{0,7},{9,8},{10,9},{11,1... | collective-permute-start | bytes 112136 | tf_op jit(solution)/shard_map/ppermute | solution.py:487
  26.9 4.6 %collective-permute-start.6 = (f32[72,128]{1,0:T(8,128)S(1)}, f32[72,128]{1,0:T(8,128)S(1)}, u32[]{:S(2)}, u32[]{:S(2)}) collective-permute-start(f32[72,128]{1,0:T(8,128)S(1)} %get-tuple-element.48), channel_id=1, source_target_pairs={{0,1},{1,2},{2,3},{3,4},{4,5},{5,6},{6,7},{7,0},{8,9},{9,10},{10,1... | collective-permute-start | bytes 110600 | tf_op jit(solution)/shard_map/ppermute | solution.py:486
